TPU v7x, 32 devices: a whole 2x2x4 slice. The times are simulated.
32 devices in a mesh: dp: 32 (over z, y, x, core).
Axes of the slice: x: 2, y: 2, z: 4, core: 2. Of those that a mesh axis runs over, the one named last changes fastest.
Arguments:
- block_input: bfloat16 [64, 512, 768], P('dp'), may hold values from -6 to 6
- memory: bfloat16 [64, 512, 768], P('dp'), may hold values from -6 to 6
- cotangent: bfloat16 [64, 512, 768], P('dp'), may hold values from -6 to 6
- segments: int32 [64, 512], P('dp'), may hold values from 0 to 3, as said below
- memory_segments: int32 [64, 512], P('dp'), may hold values from 0 to 3, as said below
- task_of_segment: int32 [64, 4], P('dp'), may hold values from 0 to 7
- self_query: bfloat16 [768, 768], P('dp'), may hold values from -0.21875 to 0.21875
- self_key: bfloat16 [768, 768], P('dp'), may hold values from -0.21875 to 0.21875
- self_value: bfloat16 [768, 768], P('dp'), may hold values from -0.21875 to 0.21875
- self_output: bfloat16 [768, 768], P('dp'), may hold values from -0.875 to 0.875
- cross_query: bfloat16 [768, 768], P('dp'), may hold values from -0.21875 to 0.21875
- cross_key: bfloat16 [768, 768], P('dp'), may hold values from -0.21875 to 0.21875
- cross_value: bfloat16 [768, 768], P('dp'), may hold values from -0.21875 to 0.21875
- cross_output: bfloat16 [768, 768], P('dp'), may hold values from -0.875 to 0.875
- hidden_in: bfloat16 [768, 3072], P('dp'), may hold values from -0.21875 to 0.21875
- hidden_out: bfloat16 [3072, 768], P('dp'), may hold values from -0.109375 to 0.109375
- task_table: float32 [8, 64], replicated, may hold values from -6 to 6
- task_weight: float32 [64, 128], replicated, may hold values from -0.75 to 0.75
- task_bias: float32 [128], replicated, may hold values from -3 to 3
- down_maker: bfloat16 [18432, 128], P('dp'), may hold values from -0.0390625 to 0.0390625
- up_maker: bfloat16 [18432, 128], P('dp'), may hold values from -0.21875 to 0.21875
- gain_maker: bfloat16 [2304, 128], P('dp'), may hold values from -0.25 to 0.25
Outputs:
- output: bfloat16 [64, 512, 768], P('dp')
- input_gradient: float32 [64, 512, 768], P('dp')
- memory_gradient: float32 [64, 512, 768], P('dp')
- self_query_gradient: float32 [768, 768], P('dp')
- self_key_gradient: float32 [768, 768], P('dp')
- self_value_gradient: float32 [768, 768], P('dp')
- self_output_gradient: float32 [768, 768], P('dp')
- cross_query_gradient: float32 [768, 768], P('dp')
- cross_key_gradient: float32 [768, 768], P('dp')
- cross_value_gradient: float32 [768, 768], P('dp')
- cross_output_gradient: float32 [768, 768], P('dp')
- hidden_in_gradient: float32 [768, 3072], P('dp')
- hidden_out_gradient: float32 [3072, 768], P('dp')
- task_table_gradient: float32 [8, 64], replicated
- task_weight_gradient: float32 [64, 128], replicated
- task_bias_gradient: float32 [128], replicated
- down_maker_gradient: float32 [18432, 128], P('dp')
- up_maker_gradient: float32 [18432, 128], P('dp')
- gain_maker_gradient: float32 [2304, 128], P('dp')
Inputs may be any that keep to these rules, and one draw needn't show every extreme that they name: In each row segment numbers start at 0 and rise by one at each boundary; every segment holds one position or more; a row's memory holds as many segments as its targets, and some row holds 4. `memory_segments`: segment numbers of the memory, with the same rule and count as the row's targets. `task_of_segment`: entries past a row's last segment are not read.
All inputs are finite; a program needn't handle non-finite values.
Results may differ from a plain program's by a relative error of at most 0.025.
Values may be sent and summed in bfloat16 or wider, within the bound.
A program may use at most 256 MiB of HBM per device.

v0:
```python
import jax
import jax.numpy as jnp
from jax import lax
from jax.sharding import PartitionSpec as P

HEADS = 12
HEAD = 64
ADA = 24


exact_mode = lax.Precision.HIGHEST
norm_eps = 1e-06
masked_score = -1e30


def plain_dot(left_side, right_side):
    return jnp.dot(left_side, right_side, preferred_element_type=jnp.float32)


def exact_dot(left_side, right_side):
    return jnp.dot(left_side, right_side, precision=exact_mode, preferred_element_type=jnp.float32)


def inner_rows(left_side, right_side):
    return lax.dot_general(
        left_side, right_side, (((1,), (1,)), ((), ())), preferred_element_type=jnp.float32
    )


def inner_cols(left_side, right_side, precision_mode=None):
    return lax.dot_general(
        left_side,
        right_side,
        (((0,), (0,)), ((), ())),
        precision=precision_mode,
        preferred_element_type=jnp.float32,
    )


def gelu_exact(operand):
    return jax.nn.gelu(operand, approximate=False)


def gelu_back(operand, cotan):
    return jax.vjp(gelu_exact, operand)[1](cotan)[0]


def rms_norm(stream, gain_row):
    return (
        stream * lax.rsqrt(jnp.mean(stream * stream, axis=-1, keepdims=True) + norm_eps) * gain_row
    )


def norm_back(stream, gain_row, cotan):
    return jax.vjp(rms_norm, stream, gain_row)[1](cotan)


def task_network(table_rows, weight_in, bias_row):
    return gelu_exact(exact_dot(table_rows, weight_in) + bias_row)


def row_scores(queries, key_rows, allowed):
    scores = jnp.einsum("qhe,khe->hqk", queries, key_rows, preferred_element_type=jnp.float32)
    scores = scores * queries.shape[-1] ** (-0.5)
    return jnp.where(allowed[None], scores, masked_score)


def attend_forward(inputs):
    queries, key_rows, value_rows, allowed = inputs
    scores = row_scores(queries, key_rows, allowed)
    row_peak = jnp.max(scores, axis=-1, keepdims=True)
    shifted = jnp.exp(scores - row_peak)
    totals = jnp.sum(shifted, axis=-1, keepdims=True)
    mix_weights = (shifted / totals).astype(jnp.bfloat16)
    mixed_rows = jnp.einsum(
        "hqk,khe->qhe", mix_weights, value_rows, preferred_element_type=jnp.float32
    )
    return (mixed_rows.astype(jnp.bfloat16), (row_peak + jnp.log(totals))[..., 0])


def attend_backward(inputs):
    queries, key_rows, value_rows, allowed, log_totals, grad_mixed = inputs
    score_scale = queries.shape[-1] ** (-0.5)
    scores = row_scores(queries, key_rows, allowed)
    weights_full = jnp.exp(scores - log_totals[..., None])
    grad_values = jnp.einsum(
        "hqk,qhe->khe",
        weights_full.astype(jnp.bfloat16),
        grad_mixed,
        preferred_element_type=jnp.float32,
    )
    grad_weights = jnp.einsum(
        "qhe,khe->hqk", grad_mixed, value_rows, preferred_element_type=jnp.float32
    )
    inner_sum = jnp.sum(weights_full * grad_weights, axis=-1, keepdims=True)
    grad_scores = (weights_full * (grad_weights - inner_sum)).astype(jnp.bfloat16)
    grad_queries = (
        jnp.einsum("hqk,khe->qhe", grad_scores, key_rows, preferred_element_type=jnp.float32)
        * score_scale
    )
    grad_keys = (
        jnp.einsum("hqk,qhe->khe", grad_scores, queries, preferred_element_type=jnp.float32)
        * score_scale
    )
    return (
        grad_queries.astype(jnp.bfloat16),
        grad_keys.astype(jnp.bfloat16),
        grad_values.astype(jnp.bfloat16),
    )


def on_device(
    block_input,
    memory,
    cotangent,
    segments,
    memory_segments,
    task_of_segment,
    self_query,
    self_key,
    self_value,
    self_output,
    cross_query,
    cross_key,
    cross_value,
    cross_output,
    hidden_in,
    hidden_out,
    task_table,
    task_weight,
    task_bias,
    down_maker,
    up_maker,
    gain_maker,
):
    row_count, seq_len, model_width = block_input.shape
    mem_len = memory.shape[1]
    task_count = task_table.shape[0]
    token_count = row_count * seq_len
    backbone = (
        lax.all_gather(self_query, "dp", axis=0, tiled=True),
        lax.all_gather(self_key, "dp", axis=0, tiled=True),
        lax.all_gather(self_value, "dp", axis=0, tiled=True),
        lax.all_gather(self_output, "dp", axis=0, tiled=True),
        lax.all_gather(cross_query, "dp", axis=0, tiled=True),
        lax.all_gather(cross_key, "dp", axis=0, tiled=True),
        lax.all_gather(cross_value, "dp", axis=0, tiled=True),
        lax.all_gather(cross_output, "dp", axis=0, tiled=True),
        lax.all_gather(hidden_in, "dp", axis=0, tiled=True),
        lax.all_gather(hidden_out, "dp", axis=0, tiled=True),
    )
    task_state, task_back = jax.vjp(task_network, task_table, task_weight, task_bias)
    task_low = task_state.astype(jnp.bfloat16)
    whole_down, whole_up, whole_gain = (
        lax.all_gather(down_maker, "dp", axis=0, tiled=True),
        lax.all_gather(up_maker, "dp", axis=0, tiled=True),
        lax.all_gather(gain_maker, "dp", axis=0, tiled=True),
    )
    made_down = inner_rows(task_low, whole_down).astype(jnp.bfloat16)
    made_up = inner_rows(task_low, whole_up).astype(jnp.bfloat16)
    gain_table = 1.0 + inner_rows(task_low, whole_gain)
    down_all = (
        made_down.reshape(task_count, model_width, ADA)
        .transpose(1, 0, 2)
        .reshape(model_width, task_count * ADA)
    )
    up_all = made_up.reshape(task_count * ADA, model_width)
    seg_match = (
        segments[:, :, None] == jnp.arange(task_of_segment.shape[1], dtype=jnp.int32)[None, None, :]
    )
    token_task = jnp.sum(jnp.where(seg_match, task_of_segment[:, None, :], 0), axis=-1).reshape(
        token_count
    )
    task_hot = (token_task[:, None] == jnp.arange(task_count, dtype=jnp.int32)[None, :]).astype(
        jnp.float32
    )
    token_gain = exact_dot(task_hot, gain_table)
    gain_one = token_gain[:, :model_width]
    gain_two = token_gain[:, model_width : 2 * model_width]
    gain_three = token_gain[:, 2 * model_width :]
    position = jnp.arange(seq_len, dtype=jnp.int32)
    self_allow = (segments[:, :, None] == segments[:, None, :]) & (
        position[:, None] >= position[None, :]
    )[None]
    cross_allow = segments[:, :, None] == memory_segments[:, None, :]

    def split_heads(flat_rows, length):
        return flat_rows.reshape(row_count, length, HEADS, HEAD)

    def project(source, weight_full, length):
        return split_heads(plain_dot(source, weight_full).astype(jnp.bfloat16), length)

    (
        self_query_full,
        self_key_full,
        self_value_full,
        self_output_full,
        cross_query_full,
        cross_key_full,
        cross_value_full,
        cross_output_full,
        hidden_in_full,
        hidden_out_full,
    ) = backbone
    stream_in = block_input.reshape(token_count, model_width).astype(jnp.float32)
    normed_one = rms_norm(stream_in, gain_one).astype(jnp.bfloat16)
    queries_one = project(normed_one, self_query_full, seq_len)
    keys_one = project(normed_one, self_key_full, seq_len)
    values_one = project(normed_one, self_value_full, seq_len)
    mixed_one, totals_one = lax.map(attend_forward, (queries_one, keys_one, values_one, self_allow))
    mixed_one = mixed_one.reshape(token_count, model_width)
    stream_one = stream_in + plain_dot(mixed_one, self_output_full)
    normed_two = rms_norm(stream_one, gain_two).astype(jnp.bfloat16)
    memory_flat = memory.reshape(row_count * mem_len, model_width)
    queries_two = project(normed_two, cross_query_full, seq_len)
    keys_two = project(memory_flat, cross_key_full, mem_len)
    values_two = project(memory_flat, cross_value_full, mem_len)
    mixed_two, totals_two = lax.map(
        attend_forward, (queries_two, keys_two, values_two, cross_allow)
    )
    mixed_two = mixed_two.reshape(token_count, model_width)
    stream_two = stream_one + plain_dot(mixed_two, cross_output_full)
    normed_three = rms_norm(stream_two, gain_three).astype(jnp.bfloat16)
    hidden_units = plain_dot(normed_three, hidden_in_full)
    activated = gelu_exact(hidden_units).astype(jnp.bfloat16)
    feed_result = plain_dot(activated, hidden_out_full)
    feed_low = feed_result.astype(jnp.bfloat16)
    task_mask = jnp.repeat(task_hot, ADA, axis=1)
    bottleneck = plain_dot(feed_low, down_all) * task_mask
    narrow_low = gelu_exact(bottleneck).astype(jnp.bfloat16)
    adapter_out = plain_dot(narrow_low, up_all)
    output = (
        (stream_two + feed_result + adapter_out)
        .astype(jnp.bfloat16)
        .reshape(row_count, seq_len, model_width)
    )
    backbone = (
        lax.all_gather(self_query, "dp", axis=0, tiled=True),
        lax.all_gather(self_key, "dp", axis=0, tiled=True),
        lax.all_gather(self_value, "dp", axis=0, tiled=True),
        lax.all_gather(self_output, "dp", axis=0, tiled=True),
        lax.all_gather(cross_query, "dp", axis=0, tiled=True),
        lax.all_gather(cross_key, "dp", axis=0, tiled=True),
        lax.all_gather(cross_value, "dp", axis=0, tiled=True),
        lax.all_gather(cross_output, "dp", axis=0, tiled=True),
        lax.all_gather(hidden_in, "dp", axis=0, tiled=True),
        lax.all_gather(hidden_out, "dp", axis=0, tiled=True),
    )
    (
        self_query_full,
        self_key_full,
        self_value_full,
        self_output_full,
        cross_query_full,
        cross_key_full,
        cross_value_full,
        cross_output_full,
        hidden_in_full,
        hidden_out_full,
    ) = backbone
    grad_out = cotangent.reshape(token_count, model_width).astype(jnp.float32)
    grad_adapter = cotangent.reshape(token_count, model_width)
    up_all_grad = inner_cols(narrow_low, grad_adapter)
    grad_narrow = inner_rows(grad_adapter, up_all)
    grad_bottleneck = (gelu_back(bottleneck, grad_narrow) * task_mask).astype(jnp.bfloat16)
    down_all_grad = inner_cols(feed_low, grad_bottleneck)
    grad_feed = (grad_out + inner_rows(grad_bottleneck, down_all)).astype(jnp.bfloat16)
    hidden_out_grad = inner_cols(activated, grad_feed)
    grad_units = gelu_back(hidden_units, inner_rows(grad_feed, hidden_out_full)).astype(
        jnp.bfloat16
    )
    hidden_in_grad = inner_cols(normed_three, grad_units)
    down_rows = (
        down_all_grad.reshape(model_width, task_count, ADA)
        .transpose(0, 2, 1)
        .reshape(model_width * ADA, task_count)
    )
    up_rows = (
        up_all_grad.reshape(task_count, ADA, model_width)
        .transpose(1, 2, 0)
        .reshape(ADA * model_width, task_count)
    )
    grad_normed_three = inner_rows(grad_units, hidden_in_full)
    stream_grad_three, gain_grad_three = norm_back(stream_two, gain_three, grad_normed_three)
    grad_two = grad_out + stream_grad_three
    grad_two_low = grad_two.astype(jnp.bfloat16)
    cross_output_grad = inner_cols(mixed_two, grad_two_low)
    grad_mixed_two = split_heads(
        inner_rows(grad_two_low, cross_output_full).astype(jnp.bfloat16), seq_len
    )
    grad_queries_two, grad_keys_two, grad_values_two = lax.map(
        attend_backward,
        (queries_two, keys_two, values_two, cross_allow, totals_two, grad_mixed_two),
    )
    grad_queries_two = grad_queries_two.reshape(token_count, model_width)
    grad_keys_two = grad_keys_two.reshape(row_count * mem_len, model_width)
    grad_values_two = grad_values_two.reshape(row_count * mem_len, model_width)
    cross_query_grad = inner_cols(normed_two, grad_queries_two)
    cross_key_grad = inner_cols(memory_flat, grad_keys_two)
    cross_value_grad = inner_cols(memory_flat, grad_values_two)
    memory_grad = inner_rows(grad_keys_two, cross_key_full) + inner_rows(
        grad_values_two, cross_value_full
    )
    grad_normed_two = inner_rows(grad_queries_two, cross_query_full)
    stream_grad_two, gain_grad_two = norm_back(stream_one, gain_two, grad_normed_two)
    grad_one = grad_two + stream_grad_two
    grad_one_low = grad_one.astype(jnp.bfloat16)
    self_output_grad = inner_cols(mixed_one, grad_one_low)
    grad_mixed_one = split_heads(
        inner_rows(grad_one_low, self_output_full).astype(jnp.bfloat16), seq_len
    )
    grad_queries_one, grad_keys_one, grad_values_one = lax.map(
        attend_backward, (queries_one, keys_one, values_one, self_allow, totals_one, grad_mixed_one)
    )
    grad_queries_one = grad_queries_one.reshape(token_count, model_width)
    grad_keys_one = grad_keys_one.reshape(token_count, model_width)
    grad_values_one = grad_values_one.reshape(token_count, model_width)
    self_query_grad = inner_cols(normed_one, grad_queries_one)
    self_key_grad = inner_cols(normed_one, grad_keys_one)
    self_value_grad = inner_cols(normed_one, grad_values_one)
    grad_normed_one = (
        inner_rows(grad_queries_one, self_query_full)
        + inner_rows(grad_keys_one, self_key_full)
        + inner_rows(grad_values_one, self_value_full)
    )
    stream_grad_one, gain_grad_one = norm_back(stream_in, gain_one, grad_normed_one)
    input_grad = grad_one + stream_grad_one
    gain_grads = jnp.concatenate((gain_grad_one, gain_grad_two, gain_grad_three), axis=1)
    gain_rows = inner_cols(gain_grads, task_hot, exact_mode)
    shares = (
        lax.psum_scatter(self_query_grad, "dp", scatter_dimension=0, tiled=True),
        lax.psum_scatter(self_key_grad, "dp", scatter_dimension=0, tiled=True),
        lax.psum_scatter(self_value_grad, "dp", scatter_dimension=0, tiled=True),
        lax.psum_scatter(self_output_grad, "dp", scatter_dimension=0, tiled=True),
        lax.psum_scatter(cross_query_grad, "dp", scatter_dimension=0, tiled=True),
        lax.psum_scatter(cross_key_grad, "dp", scatter_dimension=0, tiled=True),
        lax.psum_scatter(cross_value_grad, "dp", scatter_dimension=0, tiled=True),
        lax.psum_scatter(cross_output_grad, "dp", scatter_dimension=0, tiled=True),
        lax.psum_scatter(hidden_in_grad, "dp", scatter_dimension=0, tiled=True),
        lax.psum_scatter(hidden_out_grad, "dp", scatter_dimension=0, tiled=True),
        lax.psum_scatter(down_rows, "dp", scatter_dimension=0, tiled=True),
        lax.psum_scatter(up_rows, "dp", scatter_dimension=0, tiled=True),
        lax.psum_scatter(gain_rows, "dp", scatter_dimension=0, tiled=True),
    )
    own_down = shares[10].astype(jnp.bfloat16)
    own_up = shares[11].astype(jnp.bfloat16)
    own_gain = shares[12]
    down_maker_grad = plain_dot(own_down, task_low)
    up_maker_grad = plain_dot(own_up, task_low)
    gain_maker_grad = exact_dot(own_gain, task_low.astype(jnp.float32))
    state_partial = (
        inner_cols(own_down, down_maker)
        + inner_cols(own_up, up_maker)
        + inner_cols(own_gain, gain_maker.astype(jnp.float32), exact_mode)
    )
    state_grad = lax.psum(state_partial, "dp")
    table_grad, weight_grad, bias_grad = task_back(state_grad)
    return (
        output,
        input_grad.reshape(row_count, seq_len, model_width),
        memory_grad.reshape(row_count, mem_len, model_width),
        shares[0],
        shares[1],
        shares[2],
        shares[3],
        shares[4],
        shares[5],
        shares[6],
        shares[7],
        shares[8],
        shares[9],
        table_grad,
        weight_grad,
        bias_grad,
        down_maker_grad,
        up_maker_grad,
        gain_maker_grad,
    )


def solution(mesh):
    in_specs = (
        P("dp", None, None),
        P("dp", None, None),
        P("dp", None, None),
        P("dp", None),
        P("dp", None),
        P("dp", None),
        P("dp", None),
        P("dp", None),
        P("dp", None),
        P("dp", None),
        P("dp", None),
        P("dp", None),
        P("dp", None),
        P("dp", None),
        P("dp", None),
        P("dp", None),
        P(),
        P(),
        P(),
        P("dp", None),
        P("dp", None),
        P("dp", None),
    )
    out_specs = (
        P("dp", None, None),
        P("dp", None, None),
        P("dp", None, None),
        P("dp", None),
        P("dp", None),
        P("dp", None),
        P("dp", None),
        P("dp", None),
        P("dp", None),
        P("dp", None),
        P("dp", None),
        P("dp", None),
        P("dp", None),
        P(),
        P(),
        P(),
        P("dp", None),
        P("dp", None),
        P("dp", None),
    )
    return jax.shard_map(
        on_device, mesh=mesh, in_specs=in_specs, out_specs=out_specs, check_vma=False
    )
```

profile of v0, /device:TPU:0, one launch (start us, length us, event | category | flops | bytes accessed | tf_op | source)
XLA Modules:
  0.0 2461.4 jit_solution(1350436443676473045)
XLA Ops:
  18.8 45.6 %all_gather.49 = bf16[2304,128]{1,0:T(8,128)(2,1)S(1)} all-gather(bf16[72,128]{1,0:T(8,128)(2,1)} %param.51), channel_id=1, replica_groups=mesh['dp'=32] {'dp'}, dimensions={0}, use_global_device_ids=true | all-gather | bytes 608256 | tf_op jit(solution)/shard_map/all_gather | solution.py:157
  86.2 38.1 %all-gather.25.cloned.1.call-done = bf16[768,768]{1,0:T(8,128)(2,1)} async-done(((bf16[24,768]{1,0:T(8,128)(2,1)}), bf16[768,768]{1,0:T(8,128)(2,1)}) %all-gather.25.cloned.1.call-update) | async-done | bytes 1179664 | tf_op jit(solution)/shard_map/all_gather | solution.py:146
  135.2 45.0 %all-gather.17.cloned.1.call-done = bf16[768,768]{1,0:T(8,128)(2,1)} async-done(((bf16[24,768]{1,0:T(8,128)(2,1)}), bf16[768,768]{1,0:T(8,128)(2,1)}) %all-gather.17.cloned.1.call-update) | async-done | bytes 1179664 | tf_op jit(solution)/shard_map/all_gather | solution.py:142
  191.2 44.8 %all-gather.15.cloned.1.call-done = bf16[768,768]{1,0:T(8,128)(2,1)} async-done(((bf16[24,768]{1,0:T(8,128)(2,1)}), bf16[768,768]{1,0:T(8,128)(2,1)}) %all-gather.15.cloned.1.call-update) | async-done | bytes 1179664 | tf_op jit(solution)/shard_map/all_gather | solution.py:141
  245.6 46.1 %all-gather.13.cloned.1.call-done = bf16[768,768]{1,0:T(8,128)(2,1)} async-done(((bf16[24,768]{1,0:T(8,128)(2,1)}), bf16[768,768]{1,0:T(8,128)(2,1)}) %all-gather.13.cloned.1.call-update) | async-done | bytes 1179664 | tf_op jit(solution)/shard_map/all_gather | solution.py:143
  306.6 24.7 %while.52 = (s32[]{:T(128)}, bf16[2,512,12,64]{1,3,2,0:T(8,128)(2,1)}, f32[2,12,512]{2,1,0:T(8,128)S(1)}, bf16[2,512,12,64]{1,3,2,0:T(8,128)(2,1)}, pred[2,512,5...) while((s32[]{:T(128)}, ...), condition=%wide.region_5.6_spmd, body=%wide.region_2.5_spmd.sunk | while | flops 843442176 | bytes 42428516 | solution.py:210
  336.6 10.9 all-gather.19.cloned.1.call-done
  355.4 48.0 %all-gather.23.cloned.1.call-done = bf16[768,768]{1,0:T(8,128)(2,1)} async-done(((bf16[24,768]{1,0:T(8,128)(2,1)}), bf16[768,768]{1,0:T(8,128)(2,1)}) %all-gather.23.cloned.1.call-update) | async-done | bytes 1179664 | tf_op jit(solution)/shard_map/all_gather | solution.py:145
  414.8 24.7 %while.53 = (s32[]{:T(128)}, bf16[2,512,12,64]{1,3,2,0:T(8,128)(2,1)}, f32[2,12,512]{2,1,0:T(8,128)S(1)}, bf16[2,512,12,64]{1,3,2,0:T(8,128)(2,1)}, pred[2,512,5...) while((s32[]{:T(128)}, ...), condition=%wide.region_10.11_spmd, body=%wide.region_7.10_spmd.sunk | while | flops 843442176 | bytes 42428516 | solution.py:218
  444.7 14.5 all-gather.27.cloned.1.call-done
  469.0 55.8 %all-gather.35.cloned.1.call-done = bf16[18432,128]{1,0:T(8,128)(2,1)} async-done(((bf16[576,128]{1,0:T(8,128)(2,1)}), bf16[18432,128]{1,0:T(8,128)(2,1)}) %all-gather.35.cloned.1.call-update) | async-done | bytes 4718608 | tf_op jit(solution)/shard_map/all_gather | solution.py:156
  529.3 60.7 %all-gather.33.cloned.1.call-done = bf16[18432,128]{1,0:T(8,128)(2,1)} async-done(((bf16[576,128]{1,0:T(8,128)(2,1)}), bf16[18432,128]{1,0:T(8,128)(2,1)}) %all-gather.33.cloned.1.call-update) | async-done | bytes 4718608 | tf_op jit(solution)/shard_map/all_gather | solution.py:155
  597.5 57.9 %all-gather.29.cloned.1.call-done = bf16[768,3072]{1,0:T(8,128)(2,1)} async-done(((bf16[24,3072]{1,0:T(8,128)(2,1)}), bf16[768,3072]{1,0:T(8,128)(2,1)}) %all-gather.29.cloned.1.call-update) | async-done | bytes 4718608 | tf_op jit(solution)/shard_map/all_gather | solution.py:149
  655.4 36.3 %multiply_convert_fusion.6 = (bf16[1024,3072]{1,0:T(8,128)(2,1)}, f32[1024,3072]{1,0:T(8,128)}, f32[1024,3072]{1,0:T(8,128)}) fusion(bf16[1024,768]{1,0:T(8,128)(2,1)} %multiply_convert_fusion.7, bf16[768,3072]{1,0:T(8,128)(2,1)} %all-gather.29.cloned.1.call-done), kind=kOutput, calls=%fused_computation.129 | convolution fusion | flops 5036310528 | bytes 37748736 | tf_op jit(solution)/shard_map/dot_general | solution.py:17
  691.8 28.9 %all-gather.31.cloned.1.call-done = bf16[3072,768]{1,0:T(8,128)(2,1)} async-done(((bf16[96,768]{1,0:T(8,128)(2,1)}), bf16[3072,768]{1,0:T(8,128)(2,1)}) %all-gather.31.cloned.1.call-update) | async-done | bytes 4718608 | tf_op jit(solution)/shard_map/all_gather | solution.py:150
  734.1 16.3 add_convert_fusion
  779.5 52.8 %while.54 = (s32[]{:T(128)}, bf16[2,512,12,64]{1,3,2,0:T(8,128)(2,1)}, bf16[2,512,12,64]{1,3,2,0:T(8,128)(2,1)}, bf16[2,512,12,64]{1,3,2,0:T(8,128)(2,1)}, bf16[...) while((s32[]{:T(128)}, ...), condition=%wide.region_15.16_spmd, body=%wide.region_13.15_spmd.sunk | while | flops 2062411776 | bytes 147780944 | solution.py:291
  859.6 53.4 %while.55 = (s32[]{:T(128)}, bf16[2,512,12,64]{1,3,2,0:T(8,128)(2,1)}, bf16[2,512,12,64]{1,3,2,0:T(8,128)(2,1)}, bf16[2,512,12,64]{1,3,2,0:T(8,128)(2,1)}, bf16[...) while((s32[]{:T(128)}, ...), condition=%wide.region_19.20_spmd, body=%wide.region_17.19_spmd.sunk | while | flops 2062411776 | bytes 147780944 | solution.py:312
  1033.5 19.6 all-reduce.3.cloned.1.call-done
  1054.8 141.5 %reduce-scatter.44.cloned.1.call-done = f32[576,8]{1,0:T(8,128)} async-done(((f32[18432,8]{1,0:T(8,128)}), f32[576,8]{1,0:T(8,128)}) %reduce-scatter.44.cloned.1.call-update) | async-done | bytes 18448
  1197.3 140.5 %reduce-scatter.42.cloned.1.call-done = f32[576,8]{1,0:T(8,128)} async-done(((f32[18432,8]{1,0:T(8,128)}), f32[576,8]{1,0:T(8,128)}) %reduce-scatter.42.cloned.1.call-update) | async-done | bytes 18448
  1340.0 39.8 %psum.7 = f32[8,128]{1,0:T(8,128)S(1)} all-reduce(f32[8,128]{1,0:T(8,128)S(1)} %convolution_add_fusion.3), channel_id=1, replica_groups=mesh['dp'=32] {'dp'}, use_global_device_ids=true, to_apply=%region_34.35 | all-reduce | flops 1024 | bytes 8192 | tf_op jit(solution)/shard_map/psum | solution.py:356
  1383.9 57.6 %reduce-scatter.32.cloned.1.call-done = f32[24,768]{1,0:T(8,128)} async-done(((f32[768,768]{1,0:T(8,128)}), f32[24,768]{1,0:T(8,128)}) %reduce-scatter.32.cloned.1.call-update) | async-done | bytes 73744 | tf_op jit(solution)/shard_map/reduce_scatter | solution.py:338
  1441.5 104.5 %reduce-scatter.30.cloned.1.call-done = f32[24,768]{1,0:T(8,128)} async-done(((f32[768,768]{1,0:T(8,128)}), f32[24,768]{1,0:T(8,128)}) %reduce-scatter.30.cloned.1.call-update) | async-done | bytes 73744 | tf_op jit(solution)/shard_map/reduce_scatter | solution.py:335
  1546.0 103.8 %reduce-scatter.28.cloned.1.call-done = f32[24,768]{1,0:T(8,128)} async-done(((f32[768,768]{1,0:T(8,128)}), f32[24,768]{1,0:T(8,128)}) %reduce-scatter.28.cloned.1.call-update) | async-done | bytes 73744 | tf_op jit(solution)/shard_map/reduce_scatter | solution.py:334
  1649.8 104.8 %reduce-scatter.40.cloned.1.call-done = f32[24,768]{1,0:T(8,128)} async-done(((f32[768,768]{1,0:T(8,128)}), f32[24,768]{1,0:T(8,128)}) %reduce-scatter.40.cloned.1.call-update) | async-done | bytes 73744
  1754.5 103.9 %reduce-scatter.38.cloned.1.call-done = f32[24,768]{1,0:T(8,128)} async-done(((f32[768,768]{1,0:T(8,128)}), f32[24,768]{1,0:T(8,128)}) %reduce-scatter.38.cloned.1.call-update) | async-done | bytes 73744
  1858.4 104.7 %reduce-scatter.24.cloned.1.call-done = f32[24,768]{1,0:T(8,128)} async-done(((f32[768,768]{1,0:T(8,128)}), f32[24,768]{1,0:T(8,128)}) %reduce-scatter.24.cloned.1.call-update) | async-done | bytes 73744 | tf_op jit(solution)/shard_map/reduce_scatter | solution.py:332
  1963.1 103.9 %reduce-scatter.22.cloned.1.call-done = f32[24,768]{1,0:T(8,128)} async-done(((f32[768,768]{1,0:T(8,128)}), f32[24,768]{1,0:T(8,128)}) %reduce-scatter.22.cloned.1.call-update) | async-done | bytes 73744 | tf_op jit(solution)/shard_map/reduce_scatter | solution.py:331
  2067.0 104.8 %reduce-scatter.26.cloned.1.call-done = f32[24,768]{1,0:T(8,128)} async-done(((f32[768,768]{1,0:T(8,128)}), f32[24,768]{1,0:T(8,128)}) %reduce-scatter.26.cloned.1.call-update) | async-done | bytes 73744 | tf_op jit(solution)/shard_map/reduce_scatter | solution.py:333
  2171.8 140.9 %reduce-scatter.34.cloned.1.call-done = f32[24,3072]{1,0:T(8,128)} async-done(((f32[768,3072]{1,0:T(8,128)}), f32[24,3072]{1,0:T(8,128)}) %reduce-scatter.34.cloned.1.call-update) | async-done | bytes 294928 | tf_op jit(solution)/shard_map/reduce_scatter | solution.py:339
  2312.7 141.9 %reduce-scatter.36.cloned.1.call-done = f32[96,768]{1,0:T(8,128)} async-done(((f32[3072,768]{1,0:T(8,128)}), f32[96,768]{1,0:T(8,128)}) %reduce-scatter.36.cloned.1.call-update) | async-done | bytes 294928 | tf_op jit(solution)/shard_map/reduce_scatter | solution.py:340
  (473 shorter events, 483.1 us)
Async XLA Ops:
  7.2 68.2 %all-gather.21.cloned.1.call-start = ((), (), s32[]{:S(2)}) async-start(), calls=%async_computation.16 | async-start | bytes 1216512 | tf_op jit(solution)/shard_map/all_gather | solution.py:147
  8.0 116.3 %all-gather.25.cloned.1.call-start = ((), (), s32[]{:S(2)}) async-start(), calls=%async_computation.18 | async-start | bytes 1216512 | tf_op jit(solution)/shard_map/all_gather | solution.py:146
  8.7 171.5 %all-gather.17.cloned.1.call-start = ((), (), s32[]{:S(2)}) async-start(), calls=%async_computation.14 | async-start | bytes 1216512 | tf_op jit(solution)/shard_map/all_gather | solution.py:142
  9.5 226.5 %all-gather.15.cloned.1.call-start = ((), (), s32[]{:S(2)}) async-start(), calls=%async_computation.13 | async-start | bytes 1216512 | tf_op jit(solution)/shard_map/all_gather | solution.py:141
  10.0 281.7 %all-gather.13.cloned.1.call-start = ((), (), s32[]{:S(2)}) async-start(), calls=%async_computation.12 | async-start | bytes 1216512 | tf_op jit(solution)/shard_map/all_gather | solution.py:143
  10.6 336.9 %all-gather.19.cloned.1.call-start = ((), (), s32[]{:S(2)}) async-start(), calls=%async_computation.15 | async-start | bytes 1216512 | tf_op jit(solution)/shard_map/all_gather | solution.py:144
  11.2 392.2 %all-gather.23.cloned.1.call-start = ((), (), s32[]{:S(2)}) async-start(), calls=%async_computation.17 | async-start | bytes 1216512 | tf_op jit(solution)/shard_map/all_gather | solution.py:145
  11.9 447.3 %all-gather.27.cloned.1.call-start = ((), (), s32[]{:S(2)}) async-start(), calls=%async_computation.19 | async-start | bytes 1216512 | tf_op jit(solution)/shard_map/all_gather | solution.py:148
  12.7 512.1 %all-gather.35.cloned.1.call-start = ((), (), s32[]{:S(2)}) async-start(), calls=%async_computation.23 | async-start | bytes 4866048 | tf_op jit(solution)/shard_map/all_gather | solution.py:156
  13.4 576.6 %all-gather.33.cloned.1.call-start = ((), (), s32[]{:S(2)}) async-start(), calls=%async_computation.22 | async-start | bytes 4866048 | tf_op jit(solution)/shard_map/all_gather | solution.py:155
  14.0 641.4 %all-gather.29.cloned.1.call-start = ((), (), s32[]{:S(2)}) async-start(), calls=%async_computation.20 | async-start | bytes 4866048 | tf_op jit(solution)/shard_map/all_gather | solution.py:149
  14.8 705.9 %all-gather.31.cloned.1.call-start = ((), (), s32[]{:S(2)}) async-start(), calls=%async_computation.21 | async-start | bytes 4866048 | tf_op jit(solution)/shard_map/all_gather | solution.py:150
  15.3 1037.8 %all-reduce.3.cloned.1.call-start = ((), (), s32[]{:S(2)}) async-start(), calls=%async_computation.36 | async-start | bytes 147456
  935.8 260.4 %reduce-scatter.44.cloned.1.call-start = ((), (), s32[]{:S(2)}) async-start(), calls=%async_computation.35 | async-start | bytes 9732096
  944.0 393.8 %reduce-scatter.42.cloned.1.call-start = ((), (), s32[]{:S(2)}) async-start(), calls=%async_computation.34 | async-start | bytes 9732096
  952.9 488.6 %reduce-scatter.32.cloned.1.call-start = ((), (), s32[]{:S(2)}) async-start(), calls=%async_computation.29 | async-start | bytes 2433024 | tf_op jit(solution)/shard_map/reduce_scatter | solution.py:338
  958.3 587.7 %reduce-scatter.30.cloned.1.call-start = ((), (), s32[]{:S(2)}) async-start(), calls=%async_computation.28 | async-start | bytes 2433024 | tf_op jit(solution)/shard_map/reduce_scatter | solution.py:335
  962.6 687.1 %reduce-scatter.28.cloned.1.call-start = ((), (), s32[]{:S(2)}) async-start(), calls=%async_computation.27 | async-start | bytes 2433024 | tf_op jit(solution)/shard_map/reduce_scatter | solution.py:334
  967.9 786.6 %reduce-scatter.40.cloned.1.call-start = ((), (), s32[]{:S(2)}) async-start(), calls=%async_computation.33 | async-start | bytes 2433024
  978.8 879.6 %reduce-scatter.38.cloned.1.call-start = ((), (), s32[]{:S(2)}) async-start(), calls=%async_computation.32 | async-start | bytes 2433024
  988.0 975.1 %reduce-scatter.24.cloned.1.call-start = ((), (), s32[]{:S(2)}) async-start(), calls=%async_computation.25 | async-start | bytes 2433024 | tf_op jit(solution)/shard_map/reduce_scatter | solution.py:332
  992.4 1074.7 %reduce-scatter.22.cloned.1.call-start = ((), (), s32[]{:S(2)}) async-start(), calls=%async_computation.24 | async-start | bytes 2433024 | tf_op jit(solution)/shard_map/reduce_scatter | solution.py:331
  997.3 1174.5 %reduce-scatter.26.cloned.1.call-start = ((), (), s32[]{:S(2)}) async-start(), calls=%async_computation.26 | async-start | bytes 2433024 | tf_op jit(solution)/shard_map/reduce_scatter | solution.py:333
  1001.7 1311.0 %reduce-scatter.34.cloned.1.call-start = ((), (), s32[]{:S(2)}) async-start(), calls=%async_computation.30 | async-start | bytes 9732096 | tf_op jit(solution)/shard_map/reduce_scatter | solution.py:339
  1011.7 1442.8 %reduce-scatter.36.cloned.1.call-start = ((), (), s32[]{:S(2)}) async-start(), calls=%async_computation.31 | async-start | bytes 9732096 | tf_op jit(solution)/shard_map/reduce_scatter | solution.py:340
  1030.3 308.5 %copy-start.68 = (bf16[576,128]{1,0:T(8,128)(2,1)S(1)}, bf16[576,128]{1,0:T(8,128)(2,1)}, u32[]{:S(2)}) copy-start(bf16[576,128]{1,0:T(8,128)(2,1)} %param.49) | copy-start | bytes 442372
  1030.3 308.7 %copy-start.69 = (bf16[576,128]{1,0:T(8,128)(2,1)S(1)}, bf16[576,128]{1,0:T(8,128)(2,1)}, u32[]{:S(2)}) copy-start(bf16[576,128]{1,0:T(8,128)(2,1)} %param.50) | copy-start | bytes 442372
  1030.3 308.8 %copy-start.76 = (bf16[72,128]{1,0:T(8,128)(2,1)S(1)}, bf16[72,128]{1,0:T(8,128)(2,1)}, u32[]{:S(2)}) copy-start(bf16[72,128]{1,0:T(8,128)(2,1)} %param.51) | copy-start | bytes 55300
  1030.3 349.5 %copy-start.93 = (f32[8,128]{1,0:T(8,128)S(1)}, f32[8,128]{1,0:T(8,128)}, u32[]{:S(2)}) copy-start(f32[8,128]{1,0:T(8,128)} %get-tuple-element.500) | copy-start | bytes 12292
  1030.3 349.5 %copy-start.94 = (f32[8,128]{1,0:T(8,128)S(1)}, f32[8,128]{1,0:T(8,128)}, u32[]{:S(2)}) copy-start(f32[8,128]{1,0:T(8,128)} %get-tuple-element.517) | copy-start | bytes 12292
  1030.3 350.0 %copy-start.87 = (f32[64,128]{1,0:T(8,128)S(1)}, f32[64,128]{1,0:T(8,128)}, u32[]{:S(2)}) copy-start(f32[64,128]{1,0:T(8,128)} %param.47) | copy-start | bytes 98308
  1030.4 350.8 %copy-start.101 = (f32[8,64]{1,0:T(8,128)S(1)}, f32[8,64]{1,0:T(8,128)}, u32[]{:S(2)}) copy-start(f32[8,64]{1,0:T(8,128)} %param.46) | copy-start | bytes 6148
  (113 other events, 985.2 us)
Sparse Core Ops, SparseCore 0:
  11.0 57.4 all-gather.20
  71.4 52.8 all-gather.24
  127.2 52.9 all-gather.16
  183.0 52.9 all-gather.14
  238.7 52.9 all-gather.12
  294.5 52.9 all-gather.18
  350.4 52.9 all-gather.22
  406.3 52.9 all-gather.26
  462.2 62.5 all-gather.34
  527.5 62.4 all-gather.32
  592.9 62.4 all-gather.28
  658.2 62.4 all-gather.30
  936.0 117.1 all-reduce.2
  1058.9 137.3 reduce-scatter.43
  1203.0 134.7 reduce-scatter.41
  1343.5 97.9 reduce-scatter.31
  1448.1 97.8 reduce-scatter.29
  1551.7 98.0 reduce-scatter.27
  1656.5 98.0 reduce-scatter.39
  1760.2 98.1 reduce-scatter.37
  1865.1 97.9 reduce-scatter.23
  1969.0 98.0 reduce-scatter.21
  2073.8 98.0 reduce-scatter.25
  2178.1 134.5 reduce-scatter.33
  2320.2 134.3 reduce-scatter.35
where the time goes:
time: 2470 us; the launch traced here: 2460 us
  waiting for transfers between devices  1830 us (74%)
  matrix products  312 us (13%)
  local copies, waits for them, and re-layouts  152 us (6%)
  blocking collectives  85.3 us (3%)
  other arithmetic  63.3 us (3%)
    unnamed x30, waiting for transfers between devices  518 us
    reduce_scatter x1, waiting for transfers between devices, on_device(): lax.psum_scatter(hidden_out_grad, 'dp', scatter_dimension=0, tiled=True)  142 us
    reduce_scatter x1, waiting for transfers between devices, on_device(): lax.psum_scatter(hidden_in_grad, 'dp', scatter_dimension=0, tiled=True)  141 us
    reduce_scatter x1, waiting for transfers between devices, on_device(): lax.psum_scatter(self_value_grad, 'dp', scatter_dimension=0, tiled=True)  105 us
    reduce_scatter x1, waiting for transfers between devices, on_device(): lax.psum_scatter(self_key_grad, 'dp', scatter_dimension=0, tiled=True)  105 us
    reduce_scatter x1, waiting for transfers between devices, on_device(): lax.psum_scatter(cross_query_grad, 'dp', scatter_dimension=0, tiled=True)  104 us
    reduce_scatter x1, waiting for transfers between devices, on_device(): lax.psum_scatter(self_query_grad, 'dp', scatter_dimension=0, tiled=True)  104 us
    reduce_scatter x1, waiting for transfers between devices, on_device(): lax.psum_scatter(self_output_grad, 'dp', scatter_dimension=0, tiled=True)  104 us
  transfers between devices with their start and end apart: 25, of which 24 were waited for; matrix products, arithmetic and copies ran while one was open for 12% of the time, Pallas kernels for 0%

commit v1 on v0

--- a/solution.py
+++ b/solution.py
@@ -137,28 +137,35 @@
     mem_len = memory.shape[1]
     task_count = task_table.shape[0]
     token_count = row_count * seq_len
-    backbone = (
-        lax.all_gather(self_query, "dp", axis=0, tiled=True),
-        lax.all_gather(self_key, "dp", axis=0, tiled=True),
-        lax.all_gather(self_value, "dp", axis=0, tiled=True),
-        lax.all_gather(self_output, "dp", axis=0, tiled=True),
-        lax.all_gather(cross_query, "dp", axis=0, tiled=True),
-        lax.all_gather(cross_key, "dp", axis=0, tiled=True),
-        lax.all_gather(cross_value, "dp", axis=0, tiled=True),
-        lax.all_gather(cross_output, "dp", axis=0, tiled=True),
-        lax.all_gather(hidden_in, "dp", axis=0, tiled=True),
-        lax.all_gather(hidden_out, "dp", axis=0, tiled=True),
+    parts = lax.axis_size("dp")
+    own_rows = self_query.shape[0]
+    squares = (
+        self_query, self_key, self_value, self_output,
+        cross_query, cross_key, cross_value, cross_output,
+    )
+    packed = jnp.concatenate(
+        squares + (hidden_in.reshape(-1, model_width), hidden_out), axis=0
+    )
+    gathered = lax.all_gather(packed, "dp", axis=0, tiled=False)
+    in_rows = hidden_in.size // model_width
+    backbone = tuple(
+        gathered[:, i * own_rows : (i + 1) * own_rows].reshape(-1, model_width) for i in range(8)
+    ) + (
+        gathered[:, 8 * own_rows : 8 * own_rows + in_rows].reshape(model_width, -1),
+        gathered[:, 8 * own_rows + in_rows :].reshape(-1, model_width),
     )
     task_state, task_back = jax.vjp(task_network, task_table, task_weight, task_bias)
     task_low = task_state.astype(jnp.bfloat16)
-    whole_down, whole_up, whole_gain = (
-        lax.all_gather(down_maker, "dp", axis=0, tiled=True),
-        lax.all_gather(up_maker, "dp", axis=0, tiled=True),
-        lax.all_gather(gain_maker, "dp", axis=0, tiled=True),
-    )
-    made_down = inner_rows(task_low, whole_down).astype(jnp.bfloat16)
-    made_up = inner_rows(task_low, whole_up).astype(jnp.bfloat16)
-    gain_table = 1.0 + inner_rows(task_low, whole_gain)
+    made = inner_rows(task_low, jnp.concatenate((down_maker, up_maker, gain_maker), axis=0))
+    made = lax.all_gather(made, "dp", axis=0, tiled=False)
+    down_own, gain_own = down_maker.shape[0], gain_maker.shape[0]
+
+    def joined(block):
+        return block.transpose(1, 0, 2).reshape(task_count, -1)
+
+    made_down = joined(made[:, :, :down_own]).astype(jnp.bfloat16)
+    made_up = joined(made[:, :, down_own : 2 * down_own]).astype(jnp.bfloat16)
+    gain_table = 1.0 + joined(made[:, :, 2 * down_own :])
     down_all = (
         made_down.reshape(task_count, model_width, ADA)
         .transpose(1, 0, 2)
@@ -234,30 +241,6 @@
         .astype(jnp.bfloat16)
         .reshape(row_count, seq_len, model_width)
     )
-    backbone = (
-        lax.all_gather(self_query, "dp", axis=0, tiled=True),
-        lax.all_gather(self_key, "dp", axis=0, tiled=True),
-        lax.all_gather(self_value, "dp", axis=0, tiled=True),
-        lax.all_gather(self_output, "dp", axis=0, tiled=True),
-        lax.all_gather(cross_query, "dp", axis=0, tiled=True),
-        lax.all_gather(cross_key, "dp", axis=0, tiled=True),
-        lax.all_gather(cross_value, "dp", axis=0, tiled=True),
-        lax.all_gather(cross_output, "dp", axis=0, tiled=True),
-        lax.all_gather(hidden_in, "dp", axis=0, tiled=True),
-        lax.all_gather(hidden_out, "dp", axis=0, tiled=True),
-    )
-    (
-        self_query_full,
-        self_key_full,
-        self_value_full,
-        self_output_full,
-        cross_query_full,
-        cross_key_full,
-        cross_value_full,
-        cross_output_full,
-        hidden_in_full,
-        hidden_out_full,
-    ) = backbone
     grad_out = cotangent.reshape(token_count, model_width).astype(jnp.float32)
     grad_adapter = cotangent.reshape(token_count, model_width)
     up_all_grad = inner_cols(narrow_low, grad_adapter)
@@ -327,20 +310,27 @@
     input_grad = grad_one + stream_grad_one
     gain_grads = jnp.concatenate((gain_grad_one, gain_grad_two, gain_grad_three), axis=1)
     gain_rows = inner_cols(gain_grads, task_hot, exact_mode)
-    shares = (
-        lax.psum_scatter(self_query_grad, "dp", scatter_dimension=0, tiled=True),
-        lax.psum_scatter(self_key_grad, "dp", scatter_dimension=0, tiled=True),
-        lax.psum_scatter(self_value_grad, "dp", scatter_dimension=0, tiled=True),
-        lax.psum_scatter(self_output_grad, "dp", scatter_dimension=0, tiled=True),
-        lax.psum_scatter(cross_query_grad, "dp", scatter_dimension=0, tiled=True),
-        lax.psum_scatter(cross_key_grad, "dp", scatter_dimension=0, tiled=True),
-        lax.psum_scatter(cross_value_grad, "dp", scatter_dimension=0, tiled=True),
-        lax.psum_scatter(cross_output_grad, "dp", scatter_dimension=0, tiled=True),
-        lax.psum_scatter(hidden_in_grad, "dp", scatter_dimension=0, tiled=True),
-        lax.psum_scatter(hidden_out_grad, "dp", scatter_dimension=0, tiled=True),
-        lax.psum_scatter(down_rows, "dp", scatter_dimension=0, tiled=True),
-        lax.psum_scatter(up_rows, "dp", scatter_dimension=0, tiled=True),
-        lax.psum_scatter(gain_rows, "dp", scatter_dimension=0, tiled=True),
+    def blocks(grad):
+        return grad.reshape(parts, -1, model_width).astype(jnp.bfloat16)
+
+    grads = (
+        self_query_grad, self_key_grad, self_value_grad, self_output_grad,
+        cross_query_grad, cross_key_grad, cross_value_grad, cross_output_grad,
+        hidden_in_grad, hidden_out_grad,
+    )
+    summed = lax.psum_scatter(
+        jnp.concatenate([blocks(g) for g in grads], axis=1), "dp", scatter_dimension=0, tiled=False
+    ).astype(jnp.float32)
+    shares = tuple(summed[i * own_rows : (i + 1) * own_rows] for i in range(8)) + (
+        summed[8 * own_rows : 8 * own_rows + in_rows].reshape(hidden_in.shape),
+        summed[8 * own_rows + in_rows :],
+    )
+    small = jnp.concatenate(
+        [r.reshape(parts, -1, task_count) for r in (down_rows, up_rows, gain_rows)], axis=1
+    )
+    small = lax.psum_scatter(small, "dp", scatter_dimension=0, tiled=False)
+    shares = shares + (
+        small[:down_own], small[down_own : 2 * down_own], small[2 * down_own :],
     )
     own_down = shares[10].astype(jnp.bfloat16)
     own_up = shares[11].astype(jnp.bfloat16)

time: 2470 us -> 1000 us (0.40)
  waiting for transfers between devices: 1830 us -> 403 us
  blocking collectives: 85.3 us -> 36.9 us
  local copies, waits for them, and re-layouts: 152 us -> 199 us
  matrix products: 312 us -> 271 us
    reduce_scatter x8 -> x2, waiting for transfers between devices: 862 us -> 258 us  [the longest x1 166 us: on_device(): lax.psum_scatter(jnp.concatenate([blocks(g) for g in grads], axis=1), 'dp...]
    unnamed x30 -> x4, waiting for transfers between devices: 518 us -> 0.07 us
    all_gather x12 -> x2, waiting for transfers between devices: 451 us -> 145 us  [the longest x1 105 us: on_device(): gathered = lax.all_gather(packed, 'dp', axis=0, tiled=False)]
    all_gather x1 -> x0, blocking collectives: 45.6 us -> none  [on_device(): lax.all_gather(gain_maker, 'dp', axis=0, tiled=True)]
    dot_general x15 -> x13, matrix products: 55 us -> 50.7 us  [inner_rows(): lax.dot_general(left_side, right_side, (((1,), (1,)), ((), ())), preferre...]
  transfers between devices with their start and end apart: 25 -> 4, of which waited for: 24 -> 4; matrix products, arithmetic and copies ran while one was open for 12% -> 8% of each run, Pallas kernels for 0% -> 0%
where the time goes in v1:
time: 1000 us; the launch traced here: 991 us
  waiting for transfers between devices  403 us (40%)
  matrix products  271 us (27%)
  local copies, waits for them, and re-layouts  199 us (20%)
  other arithmetic  63.5 us (6%)
  blocking collectives  36.9 us (4%)
  between operations  15.6 us (2%)
    reduce_scatter x1, waiting for transfers between devices, on_device(): lax.psum_scatter(jnp.concatenate([blocks(g) for g in grads], axis=1), 'dp...  166 us
    all_gather x1, waiting for transfers between devices, on_device(): gathered = lax.all_gather(packed, 'dp', axis=0, tiled=False)  105 us
    reduce_scatter x1, waiting for transfers between devices, on_device(): small = lax.psum_scatter(small, 'dp', scatter_dimension=0, tiled=False)  92.1 us
    dot_general x14, matrix products, plain_dot(): return jnp.dot(left_side, right_side, preferred_element_type=jnp.float32)  67.2 us
    dot_general x13, matrix products, inner_rows(): lax.dot_general(left_side, right_side, (((1,), (1,)), ((), ())), preferre...  50.7 us
    dot_general x16, matrix products, inner_cols(): lax.dot_general(left_side, right_side, (((0,), (0,)), ((), ())), precisio...  41.7 us
    all_gather x1, waiting for transfers between devices, on_device(): made = lax.all_gather(made, 'dp', axis=0, tiled=False)  39.6 us
    unnamed x254, local copies, waits for them, and re-layouts  38.8 us
  transfers between devices with their start and end apart: 4, of which 4 were waited for; matrix products, arithmetic and copies ran while one was open for 8% of the time, Pallas kernels for 0%

profile of v1, /device:TPU:0, one launch (start us, length us, event | category | flops | bytes accessed | tf_op | source)
XLA Modules:
  0.0 990.6 jit_solution(1065772979675741201)
XLA Ops:
  28.9 39.6 %all-gather.5.cloned.1.call-done = f32[256,1224]{1,0:T(8,128)} async-done(((f32[8,1224]{1,0:T(8,128)}), f32[256,1224]{1,0:T(8,128)}) %all-gather.5.cloned.1.call-update) | async-done | bytes 1253392 | tf_op jit(solution)/shard_map/all_gather | solution.py:160
  90.2 105.4 %all-gather.7.cloned.1.call-done = bf16[12288,768]{1,0:T(8,128)(2,1)} async-done(((bf16[384,768]{1,0:T(8,128)(2,1)}), bf16[12288,768]{1,0:T(8,128)(2,1)}) %all-gather.7.cloned.1.call-update) | async-done | bytes 18874384 | tf_op jit(solution)/shard_map/all_gather | solution.py:149
  195.7 6.7 fusion.230
  202.4 8.4 fusion.229
  254.6 24.9 %while.52 = (s32[]{:T(128)}, bf16[2,512,12,64]{1,3,2,0:T(8,128)(2,1)}, f32[2,12,512]{2,1,0:T(8,128)S(1)}, bf16[2,512,12,64]{1,3,2,0:T(8,128)(2,1)}, pred[2,512,5...) while((s32[]{:T(128)}, ...), condition=%wide.region_5.6_spmd, body=%wide.region_2.5_spmd.sunk | while | flops 843442176 | bytes 42428516 | solution.py:217
  261.8 5.5 fusion.352
  274.0 5.5 fusion.352
  299.9 24.5 %while.53 = (s32[]{:T(128)}, bf16[2,512,12,64]{1,3,2,0:T(8,128)(2,1)}, f32[2,12,512]{2,1,0:T(8,128)S(1)}, bf16[2,512,12,64]{1,3,2,0:T(8,128)(2,1)}, pred[2,512,5...) while((s32[]{:T(128)}, ...), condition=%wide.region_10.11_spmd, body=%wide.region_7.10_spmd.sunk | while | flops 843442176 | bytes 42428516 | solution.py:225
  306.6 5.5 fusion.356
  318.9 5.5 fusion.356
  332.3 8.5 reshape.351
  345.0 35.8 %multiply_convert_fusion.6 = (bf16[1024,3072]{1,0:T(8,128)(2,1)S(1)}, f32[1024,3072]{1,0:T(8,128)}, f32[1024,3072]{1,0:T(8,128)}) fusion(bf16[1024,768]{1,0:T(8,128)(2,1)S(1)} %multiply_convert_fusion.7, bf16[768,3072]{1,0:T(8,128)(2,1)S(1)} %copy-done.50), kind=kOutput, calls=%fused_computation.127 | convolution fusion | flops 5036310528 | bytes 37748736 | tf_op jit(solution)/shard_map/dot_general | solution.py:17
  380.8 5.0 fusion.232
  392.5 17.4 %add_convert_fusion = bf16[1024,3072]{1,0:T(8,128)(2,1)} fusion(f32[1024,3072]{1,0:T(8,128)} %get-tuple-element.422, f32[1024,3072]{1,0:T(8,128)} %get-tuple-element.466, bf16[1024,768]{1,0:T(8,128)(2,1)} %fusion.126, bf16[3072,768]{1,0:T(8,128)(2,1)} %bitcast.551), kind=kOutput, calls=%fused_computation.126 | convolution fusion | flops 4875878400 | bytes 37748736 | tf_op jit(solution)/shard_map/dot_general | solution.py:25
  409.9 11.0 %multiply_reduce_fusion.3 = (f32[1024]{0:T(1024)S(1)}, f32[1024,768]{1,0:T(8,128)}) fusion(f32[1024,768]{1,0:T(8,128)S(1)} %copy-done.8, f32[1024,2304]{1,0:T(8,128)} %copy-done.1, bf16[1024,3072]{1,0:T(8,128)(2,1)} %add_convert_fusion, bf16[768,3072]{1,0:T(8,128)(2,1)} %reshape.351), kind=kOutput, calls=%fused_computation.169 | convolution fusion | flops 4834196480 | bytes 20451328 | tf_op jit(solution)/shard_map/dot_general | solution.py:25
  421.0 7.0 convolution_convert_fusion.1
  434.2 8.5 convert_element_type.278
  442.7 5.6 multiply_multiply_fusion.5
  463.4 53.0 %while.54 = (s32[]{:T(128)}, bf16[2,512,12,64]{1,3,2,0:T(8,128)(2,1)}, bf16[2,512,12,64]{1,3,2,0:T(8,128)(2,1)}, bf16[2,512,12,64]{1,3,2,0:T(8,128)(2,1)}, bf16[...) while((s32[]{:T(128)}, ...), condition=%wide.region_15.16_spmd, body=%wide.region_13.15_spmd.sunk | while | flops 2062411776 | bytes 147780944 | solution.py:274
  471.6 6.8 multiply_reduce_fusion.8
  478.4 7.1 multiply_convert_fusion.13
  497.9 6.8 multiply_reduce_fusion.8
  504.8 7.1 multiply_convert_fusion.13
  549.8 52.8 %while.55 = (s32[]{:T(128)}, bf16[2,512,12,64]{1,3,2,0:T(8,128)(2,1)}, bf16[2,512,12,64]{1,3,2,0:T(8,128)(2,1)}, bf16[2,512,12,64]{1,3,2,0:T(8,128)(2,1)}, bf16[...) while((s32[]{:T(128)}, ...), condition=%wide.region_19.20_spmd, body=%wide.region_17.19_spmd.sunk | while | flops 2062411776 | bytes 147780944 | solution.py:295
  557.8 6.8 multiply_reduce_fusion.9
  564.6 7.1 multiply_convert_fusion.14
  584.1 6.8 multiply_reduce_fusion.9
  590.9 7.1 multiply_convert_fusion.14
  659.4 5.9 convolution_convert_fusion
  677.9 92.1 %reduce-scatter.5.cloned.1.call-done = f32[1,1224,8]{1,2,0:T(8,128)} async-done(((f32[32,1224,8]{1,2,0:T(8,128)}), f32[1,1224,8]{1,2,0:T(8,128)}) %reduce-scatter.5.cloned.1.call-update) | async-done | bytes 39184 | tf_op jit(solution)/shard_map/reduce_scatter | solution.py:331
  771.9 36.9 %psum.7 = f32[8,128]{1,0:T(8,128)S(1)} all-reduce(f32[8,128]{1,0:T(8,128)S(1)} %convolution_add_fusion.2), channel_id=1, replica_groups=mesh['dp'=32] {'dp'}, use_global_device_ids=true, to_apply=%region_23.24 | all-reduce | flops 1024 | bytes 8192 | tf_op jit(solution)/shard_map/psum | solution.py:346
  814.5 165.6 %reduce-scatter.3.cloned.1.call-done = bf16[1,384,768]{2,1,0:T(8,128)(2,1)} async-done(((bf16[32,384,768]{2,1,0:T(8,128)(2,1)}), bf16[1,384,768]{2,1,0:T(8,128)(2,1)}) %reduce-scatter.3.cloned.1.call-update) | async-done | bytes 589840 | tf_op jit(solution)/shard_map/reduce_scatter | solution.py:321
  (489 shorter events, 336.8 us)
Async XLA Ops:
  7.2 203.6 %copy-start = (bf16[2,512,768]{2,1,0:T(8,128)(2,1)S(1)}, bf16[2,512,768]{2,1,0:T(8,128)(2,1)}, u32[]{:S(2)}) copy-start(bf16[2,512,768]{2,1,0:T(8,128)(2,1)} %param.31) | copy-start | bytes 4718596
  7.2 20.1 %copy-start.95 = (s32[2,512]{1,0:T(2,128)S(1)}, s32[2,512]{1,0:T(2,128)}, u32[]{:S(2)}) copy-start(s32[2,512]{1,0:T(2,128)} %param.33) | copy-start | bytes 12292
  7.2 18.9 %copy-start.14 = (bf16[2,512,768]{2,1,0:T(8,128)(2,1)S(1)}, bf16[2,512,768]{2,1,0:T(8,128)(2,1)}, u32[]{:S(2)}) copy-start(bf16[2,512,768]{2,1,0:T(8,128)(2,1)} %param.30) | copy-start | bytes 4718596
  7.2 20.1 %copy-start.112 = (s32[2,512]{1,0:T(2,128)S(1)}, s32[2,512]{1,0:T(2,128)}, u32[]{:S(2)}) copy-start(s32[2,512]{1,0:T(2,128)} %param.34) | copy-start | bytes 12292
  7.2 61.3 %all-gather.5.cloned.1.call-start = ((), (), s32[]{:S(2)}) async-start(), calls=%async_computation.4 | async-start | bytes 1351680 | tf_op jit(solution)/shard_map/all_gather | solution.py:160
  10.8 184.8 %all-gather.7.cloned.1.call-start = ((), (), s32[]{:S(2)}) async-start(), calls=%async_computation.5 | async-start | bytes 19464192 | tf_op jit(solution)/shard_map/all_gather | solution.py:149
  25.3 744.7 %reduce-scatter.5.cloned.1.call-start = ((), (), s32[]{:S(2)}) async-start(), calls=%async_computation.3 | async-start | bytes 1351680 | tf_op jit(solution)/shard_map/reduce_scatter | solution.py:331
  26.1 52.4 %copy-start.93 = (s32[1,4,2,128]{3,1,2,0:T(4,128)}, s32[1,4,2,128]{3,1,2,0:T(4,128)S(1)}, u32[]{:S(2)}) copy-start(s32[1,4,2,128]{3,1,2,0:T(4,128)S(1)} %copy.230) | copy-start | bytes 12292
  26.6 42.0 %copy-start.96 = (f32[1,4,2,128]{3,1,2,0:T(4,128)}, f32[1,4,2,128]{3,1,2,0:T(4,128)S(1)}, u32[]{:S(2)}) copy-start(f32[1,4,2,128]{3,1,2,0:T(4,128)S(1)} %copy.229) | copy-start | bytes 12292
  26.6 55.9 %copy-start.102 = (f32[1024]{0:T(1024)}, f32[1024]{0:T(1024)S(1)}, u32[]{:S(2)}) copy-start(f32[1024]{0:T(1024)S(1)} %rsqrt.33) | copy-start | bytes 12292
  202.4 8.4 copy-start.74
  332.3 8.5 copy-start.100
  340.8 40.0 %slice-start.8 = ((s8[4718592]{0:T(1024)(128)(4,1)}), s8[4194304]{0:T(1024)(128)(4,1)S(1)}, s32[]{:S(2)}) async-start(s8[4718592]{0:T(1024)(128)(4,1)} %bitcast.552), calls=%async_computation.14 | async-start | bytes 8388608
  345.0 35.8 %slice-start.9 = ((s8[4718592]{0:T(1024)(128)(4,1)}), s8[524288]{0:T(1024)(128)(4,1)S(1)}, s32[]{:S(2)}) async-start(s8[4718592]{0:T(1024)(128)(4,1)} %bitcast.552), calls=%async_computation.15 | async-start | bytes 1048576
  388.4 42.1 %copy-start.55 = (bf16[1024,192]{0,1:T(8,128)(2,1)}, bf16[1024,192]{0,1:T(8,128)(2,1)S(1)}, u32[]{:S(2)}) copy-start(bf16[1024,192]{0,1:T(8,128)(2,1)S(1)} %get-tuple-element.419) | copy-start | bytes 1179652
  392.5 17.4 %copy-start.8 = (f32[1024,768]{1,0:T(8,128)S(1)}, f32[1024,768]{1,0:T(8,128)}, u32[]{:S(2)}) copy-start(f32[1024,768]{1,0:T(8,128)} %get-tuple-element.465) | copy-start | bytes 9437188
  409.9 11.0 %copy-start.116 = (bf16[1024,3072]{1,0:T(8,128)(2,1)S(1)}, bf16[1024,3072]{1,0:T(8,128)(2,1)}, u32[]{:S(2)}) copy-start(bf16[1024,3072]{1,0:T(8,128)(2,1)} %add_convert_fusion) | copy-start | bytes 18874372
  434.2 8.5 copy-start.111
  434.2 8.5 copy-start.101
  442.7 7.2 copy-start.82
  519.9 9.2 slice-start
  636.6 343.5 %reduce-scatter.3.cloned.1.call-start = ((), (), s32[]{:S(2)}) async-start(), calls=%async_computation.2 | async-start | bytes 19464192 | tf_op jit(solution)/shard_map/reduce_scatter | solution.py:321
  636.7 22.7 %slice-start.10 = ((s8[6291456]{0:T(1024)(128)(4,1)}), s8[4194304]{0:T(1024)(128)(4,1)S(1)}, s32[]{:S(2)}) async-start(s8[6291456]{0:T(1024)(128)(4,1)} %bitcast.601), calls=%async_computation.16 | async-start | bytes 8388608
  646.2 13.2 %slice-start.11 = ((s8[6291456]{0:T(1024)(128)(4,1)}), s8[2097152]{0:T(1024)(128)(4,1)S(1)}, s32[]{:S(2)}) async-start(s8[6291456]{0:T(1024)(128)(4,1)} %bitcast.601), calls=%async_computation.17 | async-start | bytes 4194304
  674.6 96.1 %copy-start.91 = (bf16[576,128]{1,0:T(8,128)(2,1)S(1)}, bf16[576,128]{1,0:T(8,128)(2,1)}, u32[]{:S(2)}) copy-start(bf16[576,128]{1,0:T(8,128)(2,1)} %param.49) | copy-start | bytes 442372
  674.6 96.3 %copy-start.92 = (bf16[576,128]{1,0:T(8,128)(2,1)S(1)}, bf16[576,128]{1,0:T(8,128)(2,1)}, u32[]{:S(2)}) copy-start(bf16[576,128]{1,0:T(8,128)(2,1)} %param.50) | copy-start | bytes 442372
  674.6 96.4 %copy-start.107 = (bf16[72,128]{1,0:T(8,128)(2,1)S(1)}, bf16[72,128]{1,0:T(8,128)(2,1)}, u32[]{:S(2)}) copy-start(bf16[72,128]{1,0:T(8,128)(2,1)} %param.51) | copy-start | bytes 55300
  674.6 134.1 %copy-start.113 = (f32[8,128]{1,0:T(8,128)S(1)}, f32[8,128]{1,0:T(8,128)}, u32[]{:S(2)}) copy-start(f32[8,128]{1,0:T(8,128)} %get-tuple-element.424) | copy-start | bytes 12292
  674.7 134.1 %copy-start.114 = (f32[8,128]{1,0:T(8,128)S(1)}, f32[8,128]{1,0:T(8,128)}, u32[]{:S(2)}) copy-start(f32[8,128]{1,0:T(8,128)} %get-tuple-element.461) | copy-start | bytes 12292
  674.7 134.6 %copy-start.104 = (f32[64,128]{1,0:T(8,128)S(1)}, f32[64,128]{1,0:T(8,128)}, u32[]{:S(2)}) copy-start(f32[64,128]{1,0:T(8,128)} %param.47) | copy-start | bytes 98308
  674.7 135.4 %copy-start.115 = (f32[8,64]{1,0:T(8,128)S(1)}, f32[8,64]{1,0:T(8,128)}, u32[]{:S(2)}) copy-start(f32[8,64]{1,0:T(8,128)} %param.46) | copy-start | bytes 6148
  674.7 136.2 %copy-start.106 = (bf16[8,128]{1,0:T(8,128)(2,1)S(1)}, bf16[8,128]{1,0:T(8,128)(2,1)}, u32[]{:S(2)}) copy-start(bf16[8,128]{1,0:T(8,128)(2,1)} %copy-done.105) | copy-start | bytes 6148
  (116 other events, 348.9 us)
Sparse Core Ops, SparseCore 0:
  11.5 56.9 all-gather.4
  72.0 123.6 all-gather.6
  636.7 133.2 reduce-scatter.4
  777.4 202.6 reduce-scatter.2

commit v2 on v1

v2 whole, which is shorter than its diff:
```python
import functools

import jax
import jax.numpy as jnp
from jax import lax
from jax.experimental import pallas as pl
from jax.experimental.pallas import tpu as pltpu
from jax.sharding import PartitionSpec as P

HEADS = 12
HEAD = 64
ADA = 24
PAIR = 2 * HEAD

exact_mode = lax.Precision.HIGHEST
norm_eps = 1e-06
masked_score = -1e30
bf16 = jnp.bfloat16
f32 = jnp.float32
VMEM_BYTES = 56 << 20


def plain_dot(left_side, right_side):
    return jnp.dot(left_side, right_side, preferred_element_type=f32)


def exact_dot(left_side, right_side):
    return jnp.dot(left_side, right_side, precision=exact_mode, preferred_element_type=f32)


def inner_rows(left_side, right_side):
    return lax.dot_general(
        left_side, right_side, (((1,), (1,)), ((), ())), preferred_element_type=f32
    )


def inner_cols(left_side, right_side, precision_mode=None):
    return lax.dot_general(
        left_side,
        right_side,
        (((0,), (0,)), ((), ())),
        precision=precision_mode,
        preferred_element_type=f32,
    )


def gelu_exact(operand):
    return jax.nn.gelu(operand, approximate=False)


def task_network(table_rows, weight_in, bias_row):
    return gelu_exact(exact_dot(table_rows, weight_in) + bias_row)


def gelu_both(v):
    phi = 0.5 * lax.erf(v * 0.7071067811865476) + 0.5
    slope = phi + v * (jnp.exp(v * v * -0.5) * 0.3989422804014327)
    return v * phi, slope


def token_gain(task_column, gain):
    high = gain.astype(bf16).astype(f32)
    rest = gain - high
    middle = rest.astype(bf16).astype(f32)
    table = jnp.concatenate((high, middle, rest - middle), axis=0).astype(bf16)
    which = lax.broadcasted_iota(jnp.int32, (task_column.shape[0], 24), 1) & 7
    hot = jnp.where(which == task_column, 1.0, 0.0).astype(bf16)
    return plain_dot(hot, table)


def gain_rows(task_column, grads):
    which = lax.broadcasted_iota(jnp.int32, (task_column.shape[0], 8), 1)
    hot = jnp.where(which == task_column, 1.0, 0.0).astype(bf16)
    high = grads.astype(bf16)
    low = (grads - high.astype(f32)).astype(bf16)
    return inner_cols(hot, high) + inner_cols(hot, low)


def inverse_rms(stream):
    return lax.rsqrt(jnp.mean(stream * stream, axis=-1, keepdims=True) + norm_eps)


def norm_back(stream, gain, cotan):
    r = inverse_rms(stream)
    scaled = cotan * gain
    inner = jnp.mean(scaled * stream, axis=-1, keepdims=True)
    return r * (scaled - stream * (r * r * inner)), cotan * (stream * r)


def call(kernel, grid, ins, outs, scratch=(), flops=0, name=None):
    size = sum(a.size * a.dtype.itemsize for a, _, _ in ins)
    size += sum(functools.reduce(lambda p, q: p * q, s, 1) * jnp.dtype(d).itemsize for s, d, _, _ in outs)
    return pl.pallas_call(
        kernel,
        grid=grid,
        in_specs=[pl.BlockSpec(b, m) for _, b, m in ins],
        out_specs=[pl.BlockSpec(b, m) for _, _, b, m in outs],
        out_shape=[jax.ShapeDtypeStruct(s, d) for s, d, _, _ in outs],
        scratch_shapes=list(scratch),
        compiler_params=pltpu.CompilerParams(vmem_limit_bytes=VMEM_BYTES),
        cost_estimate=pl.CostEstimate(flops=flops, bytes_accessed=size, transcendentals=0),
        name=name,
    )(*[a for a, _, _ in ins])


def whole(array):
    return (array, array.shape, lambda *_: (0,) * array.ndim)


def by_row(array, rows):
    return (array, (rows,) + array.shape[1:], lambda i: (i,) + (0,) * (array.ndim - 1))


def out_row(shape, dtype, rows):
    return (shape, dtype, (rows,) + shape[1:], lambda i: (i,) + (0,) * (len(shape) - 1))


def out_whole(shape, dtype):
    return (shape, dtype, shape, lambda *_: (0,) * len(shape))


def pre_kernel(x, task, gain, wq, wk, wv, normed, q, k, v):
    stream = x[...].astype(f32)
    n = (stream * inverse_rms(stream) * token_gain(task[...], gain[...])).astype(bf16)
    normed[...] = n
    q[...] = (plain_dot(n, wq[...]).astype(bf16).astype(f32) * HEAD**-0.5).astype(bf16)
    k[...] = plain_dot(n, wk[...]).astype(bf16)
    v[...] = plain_dot(n, wv[...]).astype(bf16)


def memory_kernel(x, wk, wv, k, v):
    k[...] = plain_dot(x[...], wk[...]).astype(bf16)
    v[...] = plain_dot(x[...], wv[...]).astype(bf16)


def middle_kernel(x, mixed, wo, task, gain, wq, stream_out, normed, q):
    stream = x[...].astype(f32) + plain_dot(mixed[...], wo[...])
    stream_out[...] = stream
    n = (stream * inverse_rms(stream) * token_gain(task[...], gain[...])).astype(bf16)
    normed[...] = n
    q[...] = (plain_dot(n, wq[...]).astype(bf16).astype(f32) * HEAD**-0.5).astype(bf16)


def half_masks():
    lane = lax.broadcasted_iota(jnp.int32, (1, PAIR), 1)
    first = jnp.where(lane < HEAD, 1.0, 0.0)
    return first.astype(bf16), (1.0 - first).astype(bf16)


def attend_forward_kernel(causal, q_ref, k_ref, v_ref, seg_q, seg_k, mixed_ref, p_ref, bias):
    length, keys_all = q_ref.shape[0], k_ref.shape[0]
    step = length // 2 if causal else length

    @pl.when(pl.program_id(1) == 0)
    def _():
        same = seg_q[...] == seg_k[0]
        if causal:
            at_q = lax.broadcasted_iota(jnp.int32, (length, keys_all), 0)
            at_k = lax.broadcasted_iota(jnp.int32, (length, keys_all), 1)
            same = same & (at_q >= at_k)
        bias[...] = jnp.where(same, 0.0, masked_score)

    masks = half_masks()
    for first in range(0, length, step):
        rows = pl.ds(first, step)
        keys = first + step if causal else keys_all
        q = q_ref[rows, :]
        k = k_ref[:keys, :]
        v = v_ref[:keys, :]
        out = None
        for h, mask in enumerate(masks):
            s = inner_rows(q * mask, k) + bias[rows, :keys]
            e = jnp.exp(s - jnp.max(s, axis=-1, keepdims=True))
            p = (e * (1.0 / jnp.sum(e, axis=-1, keepdims=True))).astype(bf16)
            p_ref[0, h, rows, :keys] = p
            part = plain_dot(p, v * mask)
            out = part if out is None else out + part
        mixed_ref[rows, :] = out.astype(bf16)


def attend_backward_kernel(
    causal, q_ref, k_ref, v_ref, mixed_ref, gm_ref, p_ref, gq_ref, gk_ref, gv_ref
):
    length, keys_all = q_ref.shape[0], k_ref.shape[0]
    step = length // 2 if causal else length
    masks = half_masks()
    gk_parts, gv_parts = [], []
    for first in range(0, length, step):
        rows = pl.ds(first, step)
        keys = first + step if causal else keys_all
        q = q_ref[rows, :]
        k = k_ref[:keys, :]
        v = v_ref[:keys, :]
        gm = gm_ref[rows, :]
        product = gm.astype(f32) * mixed_ref[rows, :].astype(f32)
        gq = gk = gv = 0.0
        for h, mask in enumerate(masks):
            inner = jnp.sum(product * mask.astype(f32), axis=-1, keepdims=True)
            p = p_ref[0, h, rows, :keys]
            gm_half = gm * mask
            gw = inner_rows(gm_half, v)
            gs = (p.astype(f32) * (gw - inner)).astype(bf16)
            gv = gv + inner_cols(p, gm_half)
            gq = gq + plain_dot(gs, k * mask)
            gk = gk + inner_cols(gs, q * mask)
        gq_ref[rows, :] = (gq * HEAD**-0.5).astype(bf16)
        gk_parts.append(gk)
        gv_parts.append(gv)
    for ref, terms in ((gk_ref, gk_parts), (gv_ref, gv_parts)):
        if not causal:
            ref[...] = terms[0].astype(bf16)
        else:
            ref[:step, :] = (terms[0] + terms[1][:step]).astype(bf16)
            ref[step:, :] = terms[1][step:].astype(bf16)


def attention_specs(rows, length, arrays):
    return [(a, (length, PAIR), lambda r, p: (r, p)) for a in arrays]


def attend_forward(causal, rows, length, q, k, v, seg_q, seg_k):
    mem_len = k.shape[0] // rows
    mixed, probs = call(
        functools.partial(attend_forward_kernel, causal),
        (rows, HEADS // 2),
        attention_specs(rows, length, (q,))
        + attention_specs(rows, mem_len, (k, v))
        + [
            (seg_q.reshape(rows * length, 1), (length, 1), lambda r, p: (r, 0)),
            (seg_k.reshape(rows, 1, mem_len), (1, 1, mem_len), lambda r, p: (r, 0, 0)),
        ],
        [
            (q.shape, bf16, (length, PAIR), lambda r, p: (r, p)),
            (
                (rows, HEADS, length, mem_len),
                bf16,
                (1, 2, length, mem_len),
                lambda r, p: (r, p, 0, 0),
            ),
        ],
        scratch=[pltpu.VMEM((length, mem_len), f32)],
        flops=4 * rows * HEADS * length * mem_len * PAIR,
        name="attend_forward",
    )
    return mixed, probs


def attend_backward(causal, rows, length, q, k, v, mixed, grad_mixed, probs):
    mem_len = k.shape[0] // rows
    return call(
        functools.partial(attend_backward_kernel, causal),
        (rows, HEADS // 2),
        attention_specs(rows, length, (q,))
        + attention_specs(rows, mem_len, (k, v))
        + attention_specs(rows, length, (mixed, grad_mixed))
        + [(probs, (1, 2, length, mem_len), lambda r, p: (r, p, 0, 0))],
        [
            (q.shape, bf16, (length, PAIR), lambda r, p: (r, p)),
            (k.shape, bf16, (mem_len, PAIR), lambda r, p: (r, p)),
            (k.shape, bf16, (mem_len, PAIR), lambda r, p: (r, p)),
        ],
        flops=8 * rows * HEADS * length * mem_len * PAIR,
        name="attend_backward",
    )


CHUNK = 768


def feed_kernel(
    s1, mixed, wo, task, gain, w_in, w_out, down_all, up_all, cot,
    output, n3, act, gu, gfeed, g2, g2_low, gmix, up_grad, down_grad, gain_grad,
    slope, total,
):
    first = pl.program_id(0) == 0
    units = w_in.shape[1]
    stream = s1[...] + plain_dot(mixed[...], wo[...])
    picked = token_gain(task[...], gain[...])
    n3[...] = (stream * inverse_rms(stream) * picked).astype(bf16)
    total[...] = jnp.zeros_like(total)

    @pl.loop(0, units // CHUNK)
    def _(j):
        cols = pl.ds(pl.multiple_of(j * CHUNK, CHUNK), CHUNK)
        value, rate = gelu_both(plain_dot(n3[...], w_in[:, cols]))
        value = value.astype(bf16)
        act[:, cols] = value
        slope[:, cols] = rate.astype(bf16)
        total[...] += plain_dot(value, w_out[cols, :])

    feed = total[...]
    feed_low = feed.astype(bf16)
    tokens, wide = stream.shape[0], down_all.shape[1]
    owner = lax.broadcasted_iota(jnp.int32, (tokens, wide), 1) - task[...] * ADA
    mask = jnp.where((owner >= 0) & (owner < ADA), 1.0, 0.0)
    narrow, narrow_slope = gelu_both(plain_dot(feed_low, down_all[...]) * mask)
    narrow = narrow.astype(bf16)
    output[...] = (stream + feed + plain_dot(narrow, up_all[...])).astype(bf16)
    cotan = cot[...]
    gb = (narrow_slope * inner_rows(cotan, up_all[...]) * mask).astype(bf16)
    grad_feed = (cotan.astype(f32) + inner_rows(gb, down_all[...])).astype(bf16)
    gfeed[...] = grad_feed
    up_now = inner_cols(narrow, cotan)
    down_now = inner_cols(feed_low, gb)
    total[...] = jnp.zeros_like(total)

    @pl.loop(0, units // CHUNK)
    def _(j):
        cols = pl.ds(pl.multiple_of(j * CHUNK, CHUNK), CHUNK)
        grad = slope[:, cols].astype(f32) * inner_rows(gfeed[...], w_out[cols, :])
        grad = grad.astype(bf16)
        gu[:, cols] = grad
        total[...] += inner_rows(grad, w_in[:, cols])

    stream_grad, gain_tokens = norm_back(stream, picked, total[...])
    grad_two = cotan.astype(f32) + stream_grad
    g2[...] = grad_two
    low = grad_two.astype(bf16)
    g2_low[...] = low
    gmix[...] = inner_rows(low, wo[...]).astype(bf16)
    gain_now = gain_rows(task[...], gain_tokens)

    @pl.when(first)
    def _():
        up_grad[...] = up_now
        down_grad[...] = down_now
        gain_grad[...] = gain_now

    @pl.when(jnp.logical_not(first))
    def _():
        up_grad[...] += up_now
        down_grad[...] += down_now
        gain_grad[...] += gain_now


def cross_back_kernel(gq, wq, s1, task, gain, g2, wo, g1, g1_low, gmix, gain_grad):
    stream = s1[...]
    picked = token_gain(task[...], gain[...])
    stream_grad, gain_tokens = norm_back(stream, picked, inner_rows(gq[...], wq[...]))
    grad_one = g2[...] + stream_grad
    g1[...] = grad_one
    low = grad_one.astype(bf16)
    g1_low[...] = low
    gmix[...] = inner_rows(low, wo[...]).astype(bf16)
    accumulate(gain_grad, gain_rows(task[...], gain_tokens))


def accumulate(ref, value):
    @pl.when(pl.program_id(0) == 0)
    def _():
        ref[...] = value

    @pl.when(pl.program_id(0) != 0)
    def _():
        ref[...] += value


def memory_back_kernel(gk, gv, wk, wv, out):
    out[...] = inner_rows(gk[...], wk[...]) + inner_rows(gv[...], wv[...])


def input_back_kernel(gq, gk, gv, wq, wk, wv, x, task, gain, g1, out, gain_grad):
    stream = x[...].astype(f32)
    picked = token_gain(task[...], gain[...])
    cotan = inner_rows(gq[...], wq[...]) + inner_rows(gk[...], wk[...])
    cotan = cotan + inner_rows(gv[...], wv[...])
    stream_grad, gain_tokens = norm_back(stream, picked, cotan)
    out[...] = g1[...] + stream_grad
    accumulate(gain_grad, gain_rows(task[...], gain_tokens))


def outer_kernel(which, sources, *refs):
    left = refs[:sources]
    right = refs[sources : sources + len(which)]
    outs = refs[sources + len(which) :]
    for source, grad, out in zip(which, right, outs):
        for first in range(0, out.shape[1], CHUNK):
            cols = slice(first, first + CHUNK)
            out[:, cols] = inner_cols(left[source][...], grad[:, cols]).astype(bf16)


def outers(sources, grads, which, name):
    tokens, width = sources[0].shape
    block = 256
    return call(
        functools.partial(outer_kernel, which, len(sources)),
        (width // block,),
        [(s, (tokens, block), lambda i: (0, i)) for s in sources] + [whole(g) for g in grads],
        [((width, g.shape[1]), bf16, (block, g.shape[1]), lambda i: (i, 0)) for g in grads],
        flops=sum(2 * tokens * width * g.shape[1] for g in grads),
        name=name,
    )


def layer(x, mem, cot, segments, mem_segments, task, weights, gain_table, down_all, up_all):
    rows, length = segments.shape
    mem_len = mem_segments.shape[1]
    tokens, width = x.shape
    wq1, wk1, wv1, wo1, wq2, wk2, wv2, wo2, w_in, w_out = weights
    gain_one, gain_two, gain_three = (gain_table[:, i * width : (i + 1) * width] for i in range(3))
    block = 512
    grid = (tokens // block,)
    act_shape = (tokens, width)

    def low_out():
        return out_row(act_shape, bf16, block)

    def full_out():
        return out_row(act_shape, f32, block)

    square = 2 * tokens * width * width
    n1, q1, k1, v1 = call(
        pre_kernel,
        grid,
        [by_row(x, block), by_row(task, block)] + [whole(a) for a in (gain_one, wq1, wk1, wv1)],
        [low_out() for _ in range(4)],
        flops=3 * square,
        name="self_projections",
    )
    m1, p1 = attend_forward(True, rows, length, q1, k1, v1, segments, segments)
    s1, n2, q2 = call(
        middle_kernel,
        grid,
        [by_row(x, block), by_row(m1, block), whole(wo1), by_row(task, block), whole(gain_two), whole(wq2)],
        [full_out(), low_out(), low_out()],
        flops=2 * square,
        name="middle",
    )
    k2, v2 = call(
        memory_kernel,
        grid,
        [by_row(mem, block), whole(wk2), whole(wv2)],
        [low_out(), low_out()],
        flops=2 * square,
        name="memory_projections",
    )
    m2, p2 = attend_forward(False, rows, length, q2, k2, v2, segments, mem_segments)
    units = w_in.shape[1]
    wide = up_all.shape[0]
    tasks = gain_table.shape[0]
    output, n3, act, gu, gfeed, g2, g2_low, gmix2, up_grad, down_grad, gain3 = call(
        feed_kernel,
        grid,
        [
            by_row(s1, block), by_row(m2, block), whole(wo2), by_row(task, block), whole(gain_three),
            whole(w_in), whole(w_out), whole(down_all), whole(up_all), by_row(cot, block),
        ],
        [
            low_out(), low_out(), out_row((tokens, units), bf16, block), out_row((tokens, units), bf16, block),
            low_out(), full_out(), low_out(), low_out(),
            out_whole((wide, width), f32), out_whole((width, wide), f32), out_whole((tasks, width), f32),
        ],
        scratch=[pltpu.VMEM((block, units), bf16), pltpu.VMEM((block, width), f32)],
        flops=2 * square + 8 * tokens * width * units,
        name="feed_forward_and_back",
    )
    (hidden_in_grad,) = outers((n3,), (gu,), (0,), "hidden_in_grad")
    (hidden_out_grad,) = outers((act,), (gfeed,), (0,), "hidden_out_grad")
    gq2, gk2, gv2 = attend_backward(False, rows, length, q2, k2, v2, m2, gmix2, p2)
    g1, g1_low, gmix1, gain2 = call(
        cross_back_kernel,
        grid,
        [
            by_row(gq2, block), whole(wq2), by_row(s1, block), by_row(task, block), whole(gain_two),
            by_row(g2, block), whole(wo1),
        ],
        [full_out(), low_out(), low_out(), out_whole((tasks, width), f32)],
        flops=2 * square,
        name="cross_back",
    )
    (mem_grad,) = call(
        memory_back_kernel,
        grid,
        [by_row(gk2, block), by_row(gv2, block), whole(wk2), whole(wv2)],
        [full_out()],
        flops=2 * square,
        name="memory_back",
    )
    wo2_grad, wq2_grad, wk2_grad, wv2_grad = outers(
        (m2, n2, mem), (g2_low, gq2, gk2, gv2), (0, 1, 2, 2), "cross_grads"
    )
    gq1, gk1, gv1 = attend_backward(True, rows, length, q1, k1, v1, m1, gmix1, p1)
    input_grad, gain1 = call(
        input_back_kernel,
        grid,
        [
            by_row(gq1, block), by_row(gk1, block), by_row(gv1, block), whole(wq1), whole(wk1), whole(wv1),
            by_row(x, block), by_row(task, block), whole(gain_one), by_row(g1, block),
        ],
        [full_out(), out_whole((tasks, width), f32)],
        flops=3 * square,
        name="input_back",
    )
    wo1_grad, wq1_grad, wk1_grad, wv1_grad = outers(
        (m1, n1), (g1_low, gq1, gk1, gv1), (0, 1, 1, 1), "self_grads"
    )
    gain_grad = jnp.concatenate((gain1, gain2, gain3), axis=1)
    grads = (
        wq1_grad, wk1_grad, wv1_grad, wo1_grad, wq2_grad, wk2_grad, wv2_grad, wo2_grad,
        hidden_in_grad, hidden_out_grad,
    )
    return output, input_grad, mem_grad, grads, up_grad, down_grad, gain_grad


def on_device(
    block_input, memory, cotangent, segments, memory_segments, task_of_segment,
    self_query, self_key, self_value, self_output,
    cross_query, cross_key, cross_value, cross_output,
    hidden_in, hidden_out, task_table, task_weight, task_bias,
    down_maker, up_maker, gain_maker,
):
    row_count, seq_len, model_width = block_input.shape
    mem_len = memory.shape[1]
    task_count = task_table.shape[0]
    token_count = row_count * seq_len
    parts = lax.axis_size("dp")
    own_rows = self_query.shape[0]
    squares = (
        self_query, self_key, self_value, self_output,
        cross_query, cross_key, cross_value, cross_output,
    )
    packed = jnp.concatenate(
        squares + (hidden_in.reshape(-1, model_width), hidden_out), axis=0
    )
    gathered = lax.all_gather(packed, "dp", axis=0, tiled=False)
    in_rows = hidden_in.size // model_width
    backbone = tuple(
        gathered[:, i * own_rows : (i + 1) * own_rows].reshape(-1, model_width) for i in range(8)
    ) + (
        gathered[:, 8 * own_rows : 8 * own_rows + in_rows].reshape(model_width, -1),
        gathered[:, 8 * own_rows + in_rows :].reshape(-1, model_width),
    )
    task_state, task_back = jax.vjp(task_network, task_table, task_weight, task_bias)
    task_low = task_state.astype(bf16)
    made = inner_rows(task_low, jnp.concatenate((down_maker, up_maker, gain_maker), axis=0))
    made = lax.all_gather(made, "dp", axis=0, tiled=False)
    down_own = down_maker.shape[0]

    def joined(block):
        return block.transpose(1, 0, 2).reshape(task_count, -1)

    made_down = joined(made[:, :, :down_own]).astype(bf16)
    made_up = joined(made[:, :, down_own : 2 * down_own]).astype(bf16)
    gain_table = 1.0 + joined(made[:, :, 2 * down_own :])
    down_all = (
        made_down.reshape(task_count, model_width, ADA)
        .transpose(1, 0, 2)
        .reshape(model_width, task_count * ADA)
    )
    up_all = made_up.reshape(task_count * ADA, model_width)
    seg_match = (
        segments[:, :, None] == jnp.arange(task_of_segment.shape[1], dtype=jnp.int32)[None, None, :]
    )
    token_task = jnp.sum(jnp.where(seg_match, task_of_segment[:, None, :], 0), axis=-1).reshape(
        token_count, 1
    )
    output, input_grad, mem_grad, grads, up_all_grad, down_all_grad, gain_grad = layer(
        block_input.reshape(token_count, model_width),
        memory.reshape(row_count * mem_len, model_width),
        cotangent.reshape(token_count, model_width),
        segments, memory_segments, token_task, backbone, gain_table, down_all, up_all,
    )
    down_rows = (
        down_all_grad.reshape(model_width, task_count, ADA)
        .transpose(0, 2, 1)
        .reshape(model_width * ADA, task_count)
    )
    up_rows = (
        up_all_grad.reshape(task_count, ADA, model_width)
        .transpose(1, 2, 0)
        .reshape(ADA * model_width, task_count)
    )
    gain_rows_all = gain_grad.T

    def blocks(grad):
        return grad.reshape(parts, -1, model_width)

    summed = lax.psum_scatter(
        jnp.concatenate([blocks(g) for g in grads], axis=1), "dp", scatter_dimension=0, tiled=False
    ).astype(f32)
    shares = tuple(summed[i * own_rows : (i + 1) * own_rows] for i in range(8)) + (
        summed[8 * own_rows : 8 * own_rows + in_rows].reshape(hidden_in.shape),
        summed[8 * own_rows + in_rows :],
    )
    small = jnp.concatenate(
        [r.reshape(parts, -1, task_count) for r in (down_rows, up_rows, gain_rows_all)], axis=1
    )
    small = lax.psum_scatter(small, "dp", scatter_dimension=0, tiled=False)
    own_down = small[:down_own].astype(bf16)
    own_up = small[down_own : 2 * down_own].astype(bf16)
    own_gain = small[2 * down_own :]
    down_maker_grad = plain_dot(own_down, task_low)
    up_maker_grad = plain_dot(own_up, task_low)
    gain_maker_grad = exact_dot(own_gain, task_low.astype(f32))
    state_partial = (
        inner_cols(own_down, down_maker)
        + inner_cols(own_up, up_maker)
        + inner_cols(own_gain, gain_maker.astype(f32), exact_mode)
    )
    state_grad = lax.psum(state_partial, "dp")
    table_grad, weight_grad, bias_grad = task_back(state_grad)
    return (
        output.reshape(row_count, seq_len, model_width),
        input_grad.reshape(row_count, seq_len, model_width),
        mem_grad.reshape(row_count, mem_len, model_width),
        *shares,
        table_grad,
        weight_grad,
        bias_grad,
        down_maker_grad,
        up_maker_grad,
        gain_maker_grad,
    )


def solution(mesh):
    rows, whole_copy = P("dp"), P()
    return jax.shard_map(
        on_device,
        mesh=mesh,
        in_specs=(rows,) * 16 + (whole_copy,) * 3 + (rows,) * 3,
        out_specs=(rows,) * 13 + (whole_copy,) * 3 + (rows,) * 3,
        check_vma=False,
    )
```

time: 1000 us -> 756 us (0.76)
  matrix products: 271 us -> 8.97 us
  Pallas kernels: 0 us -> 215 us
  local copies, waits for them, and re-layouts: 199 us -> 81 us
  other arithmetic: 63.5 us -> 3.44 us
  waiting for transfers between devices: 403 us -> 390 us
    pallas_call x0 -> x15, Pallas kernels: none -> 215 us  [call(): pl.pallas_call(kernel, grid=grid, in_specs=[pl.BlockSpec(b, m) for _, b,...]
    dot_general x42 -> x2, matrix products: 170 us -> 2 us  [plain_dot(): return jnp.dot(left_side, right_side, preferred_element_type=f32)]
    dot_general x13 -> x1, matrix products: 50.7 us -> 1.83 us  [inner_rows(): lax.dot_general(left_side, right_side, (((1,), (1,)), ((), ())), preferre...]
    while x72 -> x0, local copies, waits for them, and re-layouts: 42.8 us -> none  [the longest x4 11.3 us: on_device(): lax.map(attend_forward, (queries_one, keys_one, values_one, self_allow))]
    dot_general x16 -> x3, matrix products: 41.7 us -> 1.14 us  [inner_cols(): lax.dot_general(left_side, right_side, (((0,), (0,)), ((), ())), precisio...]
    convert_element_type x8 -> x0, other arithmetic: 36.7 us -> none  [the longest x4 28.4 us: attend_backward(): (weights_full * (grad_weights - inner_sum)).astype(jnp.bfloat16)]
    reduce_scatter x1, waiting for transfers between devices: 92.1 us -> 56.8 us  [on_device(): small = lax.psum_scatter(small, 'dp', scatter_dimension=0, tiled=False)]
    convert_element_type x10 -> x3, local copies, waits for them, and re-layouts: 23.9 us -> 2.64 us  [the longest x2 1.34 us: on_device(): made_up = joined(made[:, :, down_own:2 * down_own]).astype(bf16)]
  transfers between devices with their start and end apart: 4 -> 4, of which waited for: 4 -> 4; matrix products, arithmetic and copies ran while one was open for 8% -> 7% of each run, Pallas kernels for 0% -> 6%
where the time goes in v2:
time: 756 us; the launch traced here: 750 us
  waiting for transfers between devices  390 us (52%)
  Pallas kernels  215 us (28%)
  local copies, waits for them, and re-layouts  81 us (11%)
  blocking collectives  36.8 us (5%)
  between operations  14.6 us (2%)
  matrix products  8.97 us (1%)
    pallas_call x15, Pallas kernels, call(): pl.pallas_call(kernel, grid=grid, in_specs=[pl.BlockSpec(b, m) for _, b,...  215 us
    reduce_scatter x1, waiting for transfers between devices, on_device(): lax.psum_scatter(jnp.concatenate([blocks(g) for g in grads], axis=1), 'dp...  166 us
    all_gather x1, waiting for transfers between devices, on_device(): gathered = lax.all_gather(packed, 'dp', axis=0, tiled=False)  120 us
    reduce_scatter x1, waiting for transfers between devices, on_device(): small = lax.psum_scatter(small, 'dp', scatter_dimension=0, tiled=False)  56.8 us
    all_gather x1, waiting for transfers between devices, on_device(): made = lax.all_gather(made, 'dp', axis=0, tiled=False)  47.8 us
    psum x1, blocking collectives, on_device(): state_grad = lax.psum(state_partial, 'dp')  36.8 us
    unnamed x76, local copies, waits for them, and re-layouts  22.9 us
  transfers between devices with their start and end apart: 4, of which 4 were waited for; matrix products, arithmetic and copies ran while one was open for 7% of the time, Pallas kernels for 6%

profile of v2, /device:TPU:0, one launch (start us, length us, event | category | flops | bytes accessed | tf_op | source)
XLA Modules:
  0.0 750.0 jit_solution(5488982060797368680)
XLA Ops:
  8.8 1.8 fusion
  20.7 47.8 %all-gather.5.cloned.1.call-done = f32[256,1224]{1,0:T(8,128)} async-done(((f32[8,1224]{1,0:T(8,128)}), f32[256,1224]{1,0:T(8,128)}) %all-gather.5.cloned.1.call-update) | async-done | bytes 1253392 | tf_op jit(solution)/shard_map/all_gather | solution.py:536
  68.5 1.8 copy.90
  75.9 119.8 %all-gather.7.cloned.1.call-done = bf16[12288,768]{1,0:T(8,128)(2,1)} async-done(((bf16[384,768]{1,0:T(8,128)(2,1)}), bf16[12288,768]{1,0:T(8,128)(2,1)}) %all-gather.7.cloned.1.call-update) | async-done | bytes 18874384 | tf_op jit(solution)/shard_map/all_gather | solution.py:525
  195.7 6.9 fusion.21
  202.6 8.0 %fusion.20 = (bf16[32,96,768]{2,1,0:T(8,128)(2,1)}, bf16[32,96,768]{2,1,0:T(8,128)(2,1)}) fusion(bf16[32,384,768]{2,1,0:T(8,128)(2,1)} %bitcast.102), kind=kLoop, calls=%fused_computation.73 | loop fusion | bytes 18874368 | tf_op jit(solution)/shard_map/slice | solution.py:531
  210.5 8.5 %reshape.196.w_in = bf16[768,3072]{1,0:T(8,128)(2,1)} reshape(bf16[32,96,768]{2,1,0:T(8,128)(2,1)} %get-tuple-element.112) | data formatting | bytes 9437184 | tf_op jit(solution)/shard_map/reshape | solution.py:530
  219.0 5.6 memory_projections.1
  224.6 7.8 %self_projections.1 = (bf16[1024,768]{1,0:T(8,128)(2,1)}, bf16[1024,768]{1,0:T(8,128)(2,1)}, bf16[1024,768]{1,0:T(8,128)(2,1)}, bf16[1024,768]{1,0:T(8,128)(2,1)}) custom-call(bf16[1024,768]{1,0:T(8,128)(2,1)} %bitcast.126, s32[1024,1]{1,0:T(8,128)} %bitcast.118, f32[8,768]{1,0:T(8,128)} %get-tuple-element.133.gain, bf16[768,768]{1,0:T(8,128)(2,1)} %bitcast.112, ...), custom_call_target="tpu_custom_call" | custom-call | flops 3623878656 | bytes 11431936 | tf_op jit(solution)/shard_map/self_projections/pallas_call | solution.py:93
  232.5 17.6 %attend_forward.2 = (bf16[1024,768]{1,0:T(8,128)(2,1)}, bf16[2,12,512,512]{3,2,1,0:T(8,128)(2,1)}) custom-call(bf16[1024,768]{1,0:T(8,128)(2,1)} %get-tuple-element.63.q_ref, bf16[1024,768]{1,0:T(8,128)(2,1)} %get-tuple-element.64.k_ref, bf16[1024,768]{1,0:T(8,128)(2,1)} %get-tuple-element.65.v_ref, s32[1024,1]{1,0:T(8,128)} %bitcast.144, ...), custom_call_target="tpu_custom_call" | custom-call | flops 3221225472 | bytes 18882560 | tf_op jit(solution)/shard_map/attend_forward/pallas_call | solution.py:93
  250.0 6.9 middle.1
  256.9 21.8 %attend_forward.3 = (bf16[1024,768]{1,0:T(8,128)(2,1)}, bf16[2,12,512,512]{3,2,1,0:T(8,128)(2,1)}) custom-call(bf16[1024,768]{1,0:T(8,128)(2,1)} %get-tuple-element.68.q_ref, bf16[1024,768]{1,0:T(8,128)(2,1)} %get-tuple-element.69.k_ref, bf16[1024,768]{1,0:T(8,128)(2,1)} %get-tuple-element.70.v_ref, s32[1024,1]{1,0:T(8,128)} %bitcast.145, ...), custom_call_target="tpu_custom_call" | custom-call | flops 3221225472 | bytes 18882560 | tf_op jit(solution)/shard_map/attend_forward/pallas_call | solution.py:93
  278.7 47.1 %feed_forward_and_back.1 = (bf16[1024,768]{1,0:T(8,128)(2,1)}, bf16[1024,768]{1,0:T(8,128)(2,1)}, bf16[1024,3072]{1,0:T(8,128)(2,1)}, bf16[1024,3072]{1,0:T(8,12...) custom-call(f32[1024,768]{1,0:T(8,128)} %get-tuple-element.67.s1, ...), custom_call_target="tpu_custom_call" | custom-call | flops 21743271936 | bytes 42323968 | tf_op jit(solution)/shard_map/feed_forward_and_back/pallas_call | solution.py:93
  325.8 20.2 %attend_backward.2 = (bf16[1024,768]{1,0:T(8,128)(2,1)}, bf16[1024,768]{1,0:T(8,128)(2,1)}, bf16[1024,768]{1,0:T(8,128)(2,1)}) custom-call(bf16[1024,768]{1,0:T(8,128)(2,1)} %get-tuple-element.68.q_ref, bf16[1024,768]{1,0:T(8,128)(2,1)} %get-tuple-element.69.k_ref, bf16[1024,768]{1,0:T(8,128)(2,1)} %get-tuple-element.70.v_ref, ...), custom_call_target="tpu_custom_call" | custom-call | flops 6442450944 | bytes 25165824 | tf_op jit(solution)/shard_map/attend_backward/pallas_call | solution.py:93
  345.9 9.8 %cross_back.1 = (f32[1024,768]{1,0:T(8,128)}, bf16[1024,768]{1,0:T(8,128)(2,1)}, bf16[1024,768]{1,0:T(8,128)(2,1)}, f32[8,768]{1,0:T(8,128)}) custom-call(bf16[1024,768]{1,0:T(8,128)(2,1)} %get-tuple-element.75.gq.refs_4_, bf16[768,768]{1,0:T(8,128)(2,1)} %bitcast.115, f32[1024,768]{1,0:T(8,128)} %get-tuple-element.67.s1, s32[1024,1]{1,0:T(8,128)} %bitcast.121, ...), custom_call_target="tpu_custom_call" | custom-call | flops 2415919104 | bytes 16568320 | tf_op jit(solution)/shard_map/cross_back/pallas_call | solution.py:93
  355.7 18.3 %attend_backward.3 = (bf16[1024,768]{1,0:T(8,128)(2,1)}, bf16[1024,768]{1,0:T(8,128)(2,1)}, bf16[1024,768]{1,0:T(8,128)(2,1)}) custom-call(bf16[1024,768]{1,0:T(8,128)(2,1)} %get-tuple-element.63.q_ref, bf16[1024,768]{1,0:T(8,128)(2,1)} %get-tuple-element.64.k_ref, bf16[1024,768]{1,0:T(8,128)(2,1)} %get-tuple-element.65.v_ref, ...), custom_call_target="tpu_custom_call" | custom-call | flops 6442450944 | bytes 25165824 | tf_op jit(solution)/shard_map/attend_backward/pallas_call | solution.py:93
  374.0 11.3 %input_back.1 = (f32[1024,768]{1,0:T(8,128)}, f32[8,768]{1,0:T(8,128)}) custom-call(bf16[1024,768]{1,0:T(8,128)(2,1)} %get-tuple-element.79.gq.refs_3_, bf16[1024,768]{1,0:T(8,128)(2,1)} %get-tuple-element.80.gk.refs_4_, bf16[1024,768]{1,0:T(8,128)(2,1)} %get-tuple-element.81.gv.refs_5_, bf16[768,768]{1,0:T(8,128)(2,1)} %bitcast.113, ...), custom_call_target="tpu_custom_call" | custom-call | flops 3623878656 | bytes 16175104 | tf_op jit(solution)/shard_map/input_back/pallas_call | solution.py:93
  388.7 1.9 copy.83
  390.6 1.8 reshape_reshape.6
  393.9 1.9 copy.84
  395.9 9.5 %self_grads.1 = (bf16[768,768]{1,0:T(8,128)(2,1)}, bf16[768,768]{1,0:T(8,128)(2,1)}, bf16[768,768]{1,0:T(8,128)(2,1)}, bf16[768,768]{1,0:T(8,128)(2,1)}) custom-call(bf16[1024,768]{1,0:T(8,128)(2,1)} %get-tuple-element.66.mixed.mixed_ref.refs_0_, bf16[1024,768]{1,0:T(8,128)(2,1)} %get-tuple-element.86.refs_1_, bf16[1024,768]{1,0:T(8,128)(2,1)} %get-tuple-element.87.refs_2_, ...), custom_call_target="tpu_custom_call" | custom-call | flops 4831838208 | bytes 14155776 | tf_op jit(solution)/shard_map/self_grads/pallas_call | solution.py:93
  405.4 9.7 %hidden_in_grad.1 = bf16[768,3072]{1,0:T(8,128)(2,1)} custom-call(bf16[1024,768]{1,0:T(8,128)(2,1)} %get-tuple-element.98.refs_0_, bf16[1024,3072]{1,0:T(8,128)(2,1)} %get-tuple-element.99.refs_1_), custom_call_target="tpu_custom_call" | custom-call | flops 4831838208 | bytes 12582912 | tf_op jit(solution)/shard_map/hidden_in_grad/pallas_call | solution.py:93
  415.1 8.6 %reshape.211 = bf16[32,96,768]{2,1,0:T(8,128)(2,1)} reshape(bf16[768,3072]{1,0:T(8,128)(2,1)} %hidden_in_grad.1) | data formatting | bytes 9437184 | tf_op jit(solution)/shard_map/reshape | solution.py:576
  429.4 10.4 %cross_grads.1 = (bf16[768,768]{1,0:T(8,128)(2,1)}, bf16[768,768]{1,0:T(8,128)(2,1)}, bf16[768,768]{1,0:T(8,128)(2,1)}, bf16[768,768]{1,0:T(8,128)(2,1)}) custom-call(bf16[1024,768]{1,0:T(8,128)(2,1)} %get-tuple-element.71.mixed.mixed_ref.refs_0_, bf16[1024,768]{1,0:T(8,128)(2,1)} %get-tuple-element.92.refs_1_, bf16[1024,768]{1,0:T(8,128)(2,1)} %bitcast.153, ...), custom_call_target="tpu_custom_call" | custom-call | flops 4831838208 | bytes 15728640 | tf_op jit(solution)/shard_map/cross_grads/pallas_call | solution.py:93
  439.7 2.5 constant_dynamic-update-slice_fusion.15
  446.2 2.4 constant_dynamic-update-slice_fusion.11
  448.6 12.9 %hidden_out_grad.1 = bf16[3072,768]{1,0:T(8,128)(2,1)} custom-call(bf16[1024,3072]{1,0:T(8,128)(2,1)} %get-tuple-element.100.refs_0_, bf16[1024,768]{1,0:T(8,128)(2,1)} %get-tuple-element.101.refs_1_), custom_call_target="tpu_custom_call" | custom-call | flops 4831838208 | bytes 12582912 | tf_op jit(solution)/shard_map/hidden_out_grad/pallas_call | solution.py:93
  461.5 4.8 constant_dynamic-update-slice_fusion.10
  466.3 6.2 memory_back.1
  472.6 56.8 %reduce-scatter.5.cloned.1.call-done = f32[1,1224,8]{1,2,0:T(8,128)} async-done(((f32[32,1224,8]{1,2,0:T(8,128)}), f32[1,1224,8]{1,2,0:T(8,128)}) %reduce-scatter.5.cloned.1.call-update) | async-done | bytes 39184 | tf_op jit(solution)/shard_map/reduce_scatter | solution.py:588
  531.3 36.8 %psum.7 = f32[8,128]{1,0:T(8,128)S(1)} all-reduce(f32[8,128]{1,0:T(8,128)S(1)} %convolution_add_fusion), channel_id=1, replica_groups=mesh['dp'=32] {'dp'}, use_global_device_ids=true, to_apply=%region_3.4 | all-reduce | flops 1024 | bytes 8192 | tf_op jit(solution)/shard_map/psum | solution.py:600
  573.8 165.6 %reduce-scatter.3.cloned.1.call-done = bf16[1,384,768]{2,1,0:T(8,128)(2,1)} async-done(((bf16[32,384,768]{2,1,0:T(8,128)(2,1)}), bf16[1,384,768]{2,1,0:T(8,128)(2,1)}) %reduce-scatter.3.cloned.1.call-update) | async-done | bytes 589840 | tf_op jit(solution)/shard_map/reduce_scatter | solution.py:578
  (118 shorter events, 42.8 us)
Async XLA Ops:
  7.2 0.8 copy-start
  7.2 9.2 %copy-start.16 = (bf16[24,768]{1,0:T(8,128)(2,1)S(1)}, bf16[24,768]{1,0:T(8,128)(2,1)}, u32[]{:S(2)}) copy-start(bf16[24,768]{1,0:T(8,128)(2,1)} %param.34) | copy-start | bytes 110596
  7.2 9.2 %copy-start.17 = (bf16[24,768]{1,0:T(8,128)(2,1)S(1)}, bf16[24,768]{1,0:T(8,128)(2,1)}, u32[]{:S(2)}) copy-start(bf16[24,768]{1,0:T(8,128)(2,1)} %param.35) | copy-start | bytes 110596
  7.2 9.2 %copy-start.13 = (bf16[96,768]{1,0:T(8,128)(2,1)S(1)}, bf16[96,768]{1,0:T(8,128)(2,1)}, u32[]{:S(2)}) copy-start(bf16[96,768]{1,0:T(8,128)(2,1)} %param.37) | copy-start | bytes 442372
  7.2 10.1 %copy-start.22 = (s32[2,512]{1,0:T(2,128)S(1)}, s32[2,512]{1,0:T(2,128)}, u32[]{:S(2)}) copy-start(s32[2,512]{1,0:T(2,128)} %param.26) | copy-start | bytes 12292
  7.2 10.7 %copy-start.18 = (s32[2,512]{1,0:T(2,128)S(1)}, s32[2,512]{1,0:T(2,128)}, u32[]{:S(2)}) copy-start(s32[2,512]{1,0:T(2,128)} %param.25) | copy-start | bytes 12292
  7.3 11.3 %copy-start.23 = (s32[2,4]{1,0:T(2,128)S(1)}, s32[2,4]{1,0:T(2,128)}, u32[]{:S(2)}) copy-start(s32[2,4]{1,0:T(2,128)} %param.27) | copy-start | bytes 100
  7.3 61.3 %all-gather.5.cloned.1.call-start = ((), (), s32[]{:S(2)}) async-start(), calls=%async_computation.4 | async-start | bytes 1351680 | tf_op jit(solution)/shard_map/all_gather | solution.py:536
  10.7 185.0 %all-gather.7.cloned.1.call-start = ((), (), s32[]{:S(2)}) async-start(), calls=%async_computation.5 | async-start | bytes 19464192 | tf_op jit(solution)/shard_map/all_gather | solution.py:525
  16.5 0.8 copy-start.11
  17.3 512.1 %reduce-scatter.5.cloned.1.call-start = ((), (), s32[]{:S(2)}) async-start(), calls=%async_computation.3 | async-start | bytes 1351680 | tf_op jit(solution)/shard_map/reduce_scatter | solution.py:588
  68.5 1.8 copy-start.1
  374.0 11.4 %copy-start.19 = (f32[8,768]{1,0:T(8,128)S(1)}, f32[8,768]{1,0:T(8,128)}, u32[]{:S(2)}) copy-start(f32[8,768]{1,0:T(8,128)} %get-tuple-element.106) | copy-start | bytes 73732
  374.0 11.4 %copy-start.20 = (f32[8,768]{1,0:T(8,128)S(1)}, f32[8,768]{1,0:T(8,128)}, u32[]{:S(2)}) copy-start(f32[8,768]{1,0:T(8,128)} %get-tuple-element.105) | copy-start | bytes 73732
  374.0 12.3 %copy-start.10 = (f32[768,192]{1,0:T(8,128)S(1)}, f32[768,192]{1,0:T(8,128)}, u32[]{:S(2)}) copy-start(f32[768,192]{1,0:T(8,128)} %get-tuple-element.102) | copy-start | bytes 1769476
  385.4 2.1 copy-start.12
  395.9 343.6 %reduce-scatter.3.cloned.1.call-start = ((), (), s32[]{:S(2)}) async-start(), calls=%async_computation.2 | async-start | bytes 19464192 | tf_op jit(solution)/shard_map/reduce_scatter | solution.py:578
  415.1 8.6 %copy-start.6 = (bf16[768,768]{1,0:T(8,128)(2,1)S(1)}, bf16[768,768]{1,0:T(8,128)(2,1)}, u32[]{:S(2)}) copy-start(bf16[768,768]{1,0:T(8,128)(2,1)} %get-tuple-element.88) | copy-start | bytes 3538948
  423.6 1.7 copy-start.5
  424.8 1.8 copy-start.4
  426.5 1.7 copy-start.3
  428.2 17.9 %slice-start = ((s8[4718592]{0:T(1024)(128)(4,1)}), s8[4194304]{0:T(1024)(128)(4,1)S(1)}, s32[]{:S(2)}) async-start(s8[4718592]{0:T(1024)(128)(4,1)} %bitcast.103), calls=%async_computation.6 | async-start | bytes 8388608
  429.4 16.8 %slice-start.1 = ((s8[4718592]{0:T(1024)(128)(4,1)}), s8[524288]{0:T(1024)(128)(4,1)S(1)}, s32[]{:S(2)}) async-start(s8[4718592]{0:T(1024)(128)(4,1)} %bitcast.103), calls=%async_computation.7 | async-start | bytes 1048576
  439.7 2.5 copy-start.9
  442.2 1.7 copy-start.8
  443.4 1.7 copy-start.7
  466.3 63.9 %copy-start.14 = (bf16[576,128]{1,0:T(8,128)(2,1)S(1)}, bf16[576,128]{1,0:T(8,128)(2,1)}, u32[]{:S(2)}) copy-start(bf16[576,128]{1,0:T(8,128)(2,1)} %param.41) | copy-start | bytes 442372
  466.3 64.0 %copy-start.15 = (bf16[576,128]{1,0:T(8,128)(2,1)S(1)}, bf16[576,128]{1,0:T(8,128)(2,1)}, u32[]{:S(2)}) copy-start(bf16[576,128]{1,0:T(8,128)(2,1)} %param.42) | copy-start | bytes 442372
  466.3 64.2 %copy-start.21 = (bf16[72,128]{1,0:T(8,128)(2,1)S(1)}, bf16[72,128]{1,0:T(8,128)(2,1)}, u32[]{:S(2)}) copy-start(bf16[72,128]{1,0:T(8,128)(2,1)} %param.43) | copy-start | bytes 55300
  466.3 103.1 %copy-start.24 = (f32[8,64]{1,0:T(8,128)S(1)}, f32[8,64]{1,0:T(8,128)}, u32[]{:S(2)}) copy-start(f32[8,64]{1,0:T(8,128)} %param.38) | copy-start | bytes 6148
  739.4 2.8 copy-start.2
Sparse Core Ops, SparseCore 0:
  11.5 56.9 all-gather.4
  72.0 123.6 all-gather.6
  396.0 133.3 reduce-scatter.4
  536.8 202.6 reduce-scatter.2

commit v3 on v2

--- a/solution.py
+++ b/solution.py
@@ -502,6 +502,349 @@
     return output, input_grad, mem_grad, grads, up_grad, down_grad, gain_grad
 
 
+LINE = 4
+MESH = pl.DeviceIdType.MESH
+
+
+class Place:
+    def __init__(self):
+        me = lax.axis_index("dp")
+        self.core = lax.rem(me, 2)
+        self.x = lax.rem(me // 2, 2)
+        self.y = lax.rem(me // 4, 2)
+        self.z = me // 8
+
+    def at(self, z=None, y=None, x=None, core=None):
+        z = self.z if z is None else z
+        y = self.y if y is None else y
+        x = self.x if x is None else x
+        core = self.core if core is None else core
+        return (((z * 2 + y) * 2 + x) * 2 + core,)
+
+    def sibling(self):
+        return self.at(core=1 - self.core)
+
+    def over_x(self):
+        return self.at(x=1 - self.x)
+
+    def over_y(self):
+        return self.at(y=1 - self.y)
+
+    def along_z(self, k):
+        return self.at(z=lax.rem(self.z + k, LINE))
+
+    def partners(self):
+        return [self.sibling(), self.over_x(), self.over_y()] + [self.along_z(k) for k in (1, 2, 3)]
+
+
+def meet(place):
+    barrier = pltpu.get_barrier_semaphore()
+    partners = place.partners()
+    for partner in partners:
+        pl.semaphore_signal(barrier, inc=1, device_id=partner, device_id_type=MESH)
+    pl.semaphore_wait(barrier, len(partners))
+
+
+class Copies:
+    def __init__(self, send, recv):
+        self.send, self.recv, self.used, self.open = send, recv, 0, []
+
+    def remote(self, source, target, device):
+        copy = pltpu.make_async_remote_copy(
+            src_ref=source,
+            dst_ref=target,
+            send_sem=self.send.at[self.used],
+            recv_sem=self.recv.at[self.used],
+            device_id=device,
+            device_id_type=MESH,
+        )
+        self.used += 1
+        copy.start()
+        self.open.append(copy)
+        return copy
+
+    def local(self, source, target):
+        copy = pltpu.make_async_copy(source, target, self.recv.at[self.used])
+        self.used += 1
+        copy.start()
+        return copy
+
+    def finish(self):
+        for copy in self.open:
+            copy.wait_send()
+
+
+def shares(rows, turn):
+    cut = rows // 2 if rows % 32 == 0 else (rows // 32 + turn % 2) * 16
+    return slice(0, cut), slice(cut, rows)
+
+
+def stepped(count, stages):
+    for turn in range(count + len(stages) - 1):
+        for late, stage in enumerate(stages):
+            if 0 <= turn - late < count:
+                stage(turn - late)
+
+
+def gather_kernel(count, *refs):
+    own, made = refs[:count], refs[count]
+    outs, made_out = refs[count + 1 : 2 * count + 1], refs[2 * count + 1]
+    scratch = refs[2 * count + 2 :]
+    whole_rows, halves, blocks = scratch[:count], scratch[count : 2 * count], scratch[2 * count : 3 * count]
+    send, recv = scratch[3 * count :]
+    here = Place()
+    copies = Copies(send, recv)
+    z, y, x, c = here.z, here.y, here.x, here.core
+
+    def half(i, core):
+        width = outs[i].shape[-1] // 2
+        return pl.ds(pl.multiple_of(core * width, 128), width)
+
+    for i in range(count):
+        whole_rows[i][...] = own[i][...].astype(f32)
+    meet(here)
+    pair, first, second, third, last = {}, {}, {}, {}, {}
+    half_made = made_out.shape[-1] // 2
+    made_cols = (pl.ds(0, half_made), pl.ds(half_made, half_made))
+    made_first = [copies.local(made, made_out.at[z, y, x, c])]
+    made_first += [
+        copies.remote(made, made_out.at[z, y, x, c], here.along_z(k)) for k in (1, 2, 3)
+    ]
+    for i in range(count):
+        rows = own[i].shape[0]
+        mine = pl.ds(pl.multiple_of(c * rows, 8), rows)
+        pair[i] = copies.remote(
+            whole_rows[i].at[:, half(i, 1 - c)], halves[i].at[mine, :], here.sibling()
+        )
+        halves[i][mine, :] = whole_rows[i][:, half(i, c)]
+    for i in range(count):
+        pair[i].wait_recv()
+        blocks[i][...] = halves[i][...].astype(bf16)
+        target = outs[i].at[z, y, x, :, half(i, c)]
+        first[i] = [copies.remote(blocks[i], target, here.along_z(k)) for k in (1, 2, 3)]
+        first[i].append(copies.local(blocks[i], target))
+
+    made_first[0].wait()
+    for copy in made_first[1:]:
+        copy.wait_recv()
+    made_second = []
+    for cols, device in zip(made_cols, (here.over_x(), here.over_y())):
+        part = made_out.at[:, y, x, c, :, cols]
+        made_second.append(copies.remote(part, part, device))
+    for copy in made_second:
+        copy.wait_recv()
+    made_third = []
+    for part, device in (
+        (made_out.at[:, y, :, c, :, made_cols[0]], here.over_y()),
+        (made_out.at[:, :, x, c, :, made_cols[1]], here.over_x()),
+    ):
+        made_third.append(copies.remote(part, part, device))
+
+    def along_first(i):
+        for copy in first[i][:3]:
+            copy.wait_recv()
+        first[i][3].wait()
+        second[i] = []
+        for rows, device in zip(shares(outs[i].shape[3], i), (here.over_x(), here.over_y())):
+            part = outs[i].at[:, y, x, rows, half(i, c)]
+            second[i].append(copies.remote(part, part, device))
+
+    def along_second(i):
+        for copy in second[i]:
+            copy.wait_recv()
+        one, two = shares(outs[i].shape[3], i)
+        third[i] = []
+        for part, device in (
+            (outs[i].at[:, y, :, one, half(i, c)], here.over_y()),
+            (outs[i].at[:, :, x, two, half(i, c)], here.over_x()),
+        ):
+            third[i].append(copies.remote(part, part, device))
+
+    def to_sibling(i):
+        for copy in third[i]:
+            copy.wait_recv()
+        part = outs[i].at[:, :, :, :, half(i, c)]
+        last[i] = copies.remote(part, part, here.sibling())
+
+    stepped(count, (along_first, along_second, to_sibling))
+    for copy in made_third:
+        copy.wait_recv()
+    part = made_out.at[:, :, :, c]
+    made_last = copies.remote(part, part, here.sibling())
+    for i in range(count):
+        last[i].wait_recv()
+    made_last.wait_recv()
+    copies.finish()
+
+
+def gather(own, made):
+    count = len(own)
+    spaces = LINE, 2, 2
+    copies = 10 * count + 12
+    any_space = pl.BlockSpec(memory_space=pl.ANY)
+    vmem = pl.BlockSpec(memory_space=pltpu.VMEM)
+    return pl.pallas_call(
+        functools.partial(gather_kernel, count),
+        in_specs=[vmem] * (count + 1),
+        out_specs=[any_space] * (count + 1),
+        out_shape=[
+            jax.ShapeDtypeStruct(spaces + (2 * a.shape[0], a.shape[1]), bf16) for a in own
+        ]
+        + [jax.ShapeDtypeStruct(spaces + (2,) + made.shape, f32)],
+        scratch_shapes=[pltpu.VMEM(a.shape, f32) for a in own]
+        + [pltpu.VMEM((2 * a.shape[0], a.shape[1] // 2), f32) for a in own]
+        + [pltpu.VMEM((2 * a.shape[0], a.shape[1] // 2), bf16) for a in own]
+        + [pltpu.SemaphoreType.DMA((copies,)), pltpu.SemaphoreType.DMA((copies,))],
+        compiler_params=pltpu.CompilerParams(
+            collective_id=0, has_side_effects=True, vmem_limit_bytes=VMEM_BYTES
+        ),
+        name="gather_weights",
+    )(*own, made)
+
+
+def scatter_kernel(count, makers, *refs):
+    grads, maker_refs = refs[:count], refs[count : count + makers]
+    outs, state_out = refs[count + makers : 2 * count + makers], refs[2 * count + makers]
+    scratch = refs[2 * count + makers + 1 :]
+    held, from_core, from_a, from_b, from_c, from_d, from_z, final = (
+        scratch[k * count : (k + 1) * count] for k in range(8)
+    )
+    totals, arriving, send, recv = scratch[8 * count :]
+    here = Place()
+    copies = Copies(send, recv)
+    z, y, x, c = here.z, here.y, here.x, here.core
+    local, core, one, two, three, last = {}, {}, {}, {}, {}, {}
+
+    def half(i, which):
+        width = grads[i].shape[-1] // 2
+        return pl.ds(pl.multiple_of(which * width, 128), width)
+
+    for i in range(count):
+        local[i] = copies.local(grads[i].at[:, :, :, :, half(i, c)], held[i])
+    meet(here)
+    for i in range(count):
+        core[i] = copies.remote(
+            grads[i].at[:, :, :, :, half(i, 1 - c)], from_core[i], here.sibling()
+        )
+
+    def cuts(i):
+        return shares(grads[i].shape[3], i)
+
+    def over_first(i):
+        local[i].wait()
+        core[i].wait_recv()
+        held[i][...] += from_core[i][...]
+        first, second = cuts(i)
+        one[i] = (
+            copies.remote(held[i].at[:, 1 - y, :, first, :], from_a[i], here.over_y()),
+            copies.remote(held[i].at[:, :, 1 - x, second, :], from_b[i], here.over_x()),
+        )
+
+    def over_second(i):
+        first, second = cuts(i)
+        one[i][0].wait_recv()
+        held[i][:, y, :, first, :] += from_a[i][...]
+        one[i][1].wait_recv()
+        held[i][:, :, x, second, :] += from_b[i][...]
+        two[i] = (
+            copies.remote(held[i].at[:, y, 1 - x, first, :], from_c[i], here.over_x()),
+            copies.remote(held[i].at[:, 1 - y, x, second, :], from_d[i], here.over_y()),
+        )
+
+    def over_line(i):
+        first, second = cuts(i)
+        two[i][0].wait_recv()
+        held[i][:, y, x, first, :] += from_c[i][...]
+        two[i][1].wait_recv()
+        held[i][:, y, x, second, :] += from_d[i][...]
+        three[i] = [
+            copies.remote(
+                held[i].at[lax.rem(z + k, LINE), y, x], from_z[i].at[k - 1], here.along_z(k)
+            )
+            for k in (1, 2, 3)
+        ]
+
+    def to_owner(i):
+        total = held[i][z, y, x].astype(f32)
+        for k, copy in enumerate(three[i]):
+            copy.wait_recv()
+            total = total + from_z[i][k].astype(f32)
+        final[i][...] = total
+        rows = outs[i].shape[0]
+        theirs = pl.ds(pl.multiple_of((1 - c) * rows, 8), rows)
+        last[i] = copies.remote(
+            final[i].at[theirs, :], outs[i].at[:, half(i, c)], here.sibling()
+        )
+        outs[i][:, half(i, c)] = final[i][pl.ds(pl.multiple_of(c * rows, 8), rows), :]
+
+    stepped(count, (over_first, over_second, over_line, to_owner))
+    last[count - 1].wait_recv()
+    down, up, gain = maker_refs
+    small = outs[count - 1]
+    made = down.shape[0]
+    gains = gain.shape[0]
+    state = plain_dot(small[0:8, :made].astype(bf16), down[...])
+    state = state + plain_dot(small[8:16, :made].astype(bf16), up[...])
+    state = state + exact_dot(small[0:8, made : made + gains], gain[...].astype(f32))
+    for turn, device in enumerate((here.sibling(), here.over_x(), here.over_y())):
+        totals[turn] = state
+        copy = copies.remote(totals.at[turn], arriving.at[turn], device)
+        copy.wait_recv()
+        state = state + arriving[turn]
+    totals[3] = state
+    around = [copies.remote(totals.at[3], arriving.at[2 + k], here.along_z(k)) for k in (1, 2, 3)]
+    terms = {}
+    for k, copy in enumerate(around):
+        copy.wait_recv()
+    total = jnp.zeros_like(state)
+    for line in range(LINE):
+        for k in range(LINE):
+            term = state if k == 0 else arriving[2 + k]
+            total = total + jnp.where(lax.rem(z - k + LINE, LINE) == line, term, 0.0)
+    state_out[...] = total
+    for i in range(count - 1):
+        last[i].wait_recv()
+    copies.finish()
+
+
+def scatter(grads, makers):
+    count = len(grads)
+    copies = 12 * count + 8
+    any_space = pl.BlockSpec(memory_space=pl.ANY)
+    vmem = pl.BlockSpec(memory_space=pltpu.VMEM)
+
+    def slots(shape_of):
+        return [pltpu.VMEM(shape_of(g, i), bf16) for i, g in enumerate(grads)]
+
+    def rows_of(g, i, which):
+        cut = shares(g.shape[3], i)[which]
+        return cut.stop - cut.start
+
+    scratch = slots(lambda g, i: g.shape[:4] + (g.shape[4] // 2,)) * 1
+    scratch += slots(lambda g, i: g.shape[:4] + (g.shape[4] // 2,))
+    scratch += slots(lambda g, i: (LINE, 2, rows_of(g, i, 0), g.shape[4] // 2))
+    scratch += slots(lambda g, i: (LINE, 2, rows_of(g, i, 1), g.shape[4] // 2))
+    scratch += slots(lambda g, i: (LINE, rows_of(g, i, 0), g.shape[4] // 2))
+    scratch += slots(lambda g, i: (LINE, rows_of(g, i, 1), g.shape[4] // 2))
+    scratch += slots(lambda g, i: (LINE - 1, g.shape[3], g.shape[4] // 2))
+    scratch += [pltpu.VMEM((g.shape[3], g.shape[4] // 2), f32) for g in grads]
+    tasks, hidden = 8, makers[0].shape[1]
+    scratch += [pltpu.VMEM((4, tasks, hidden), f32), pltpu.VMEM((6, tasks, hidden), f32)]
+    scratch += [pltpu.SemaphoreType.DMA((copies,)), pltpu.SemaphoreType.DMA((copies,))]
+    return pl.pallas_call(
+        functools.partial(scatter_kernel, count, len(makers)),
+        in_specs=[any_space] * count + [vmem] * len(makers),
+        out_specs=[vmem] * (count + 1),
+        out_shape=[jax.ShapeDtypeStruct((g.shape[3] // 2, g.shape[4]), f32) for g in grads]
+        + [jax.ShapeDtypeStruct((tasks, hidden), f32)],
+        scratch_shapes=scratch,
+        compiler_params=pltpu.CompilerParams(
+            collective_id=1, has_side_effects=True, vmem_limit_bytes=60 << 20
+        ),
+        name="scatter_gradients",
+    )(*grads, *makers)
+
+
 def on_device(
     block_input, memory, cotangent, segments, memory_segments, task_of_segment,
     self_query, self_key, self_value, self_output,
@@ -514,34 +857,29 @@
     task_count = task_table.shape[0]
     token_count = row_count * seq_len
     parts = lax.axis_size("dp")
-    own_rows = self_query.shape[0]
-    squares = (
+    weights = (
         self_query, self_key, self_value, self_output,
-        cross_query, cross_key, cross_value, cross_output,
-    )
-    packed = jnp.concatenate(
-        squares + (hidden_in.reshape(-1, model_width), hidden_out), axis=0
-    )
-    gathered = lax.all_gather(packed, "dp", axis=0, tiled=False)
-    in_rows = hidden_in.size // model_width
-    backbone = tuple(
-        gathered[:, i * own_rows : (i + 1) * own_rows].reshape(-1, model_width) for i in range(8)
-    ) + (
-        gathered[:, 8 * own_rows : 8 * own_rows + in_rows].reshape(model_width, -1),
-        gathered[:, 8 * own_rows + in_rows :].reshape(-1, model_width),
+        cross_query, cross_key, cross_value, cross_output, hidden_in, hidden_out,
     )
     task_state, task_back = jax.vjp(task_network, task_table, task_weight, task_bias)
     task_low = task_state.astype(bf16)
     made = inner_rows(task_low, jnp.concatenate((down_maker, up_maker, gain_maker), axis=0))
-    made = lax.all_gather(made, "dp", axis=0, tiled=False)
-    down_own = down_maker.shape[0]
+    down_own, gain_own = down_maker.shape[0], gain_maker.shape[0]
+    if parts == 32:
+        made = jnp.pad(made, ((0, 0), (0, -made.shape[1] % 256)))
+        *backbone, made = gather(weights, made)
+        backbone = [w.reshape(-1, w.shape[-1]) for w in backbone]
+        made = made.reshape((parts,) + made.shape[4:])
+    else:
+        backbone = [lax.all_gather(w, "dp", axis=0, tiled=True) for w in weights]
+        made = lax.all_gather(made, "dp", axis=0, tiled=False)
 
     def joined(block):
         return block.transpose(1, 0, 2).reshape(task_count, -1)
 
     made_down = joined(made[:, :, :down_own]).astype(bf16)
     made_up = joined(made[:, :, down_own : 2 * down_own]).astype(bf16)
-    gain_table = 1.0 + joined(made[:, :, 2 * down_own :])
+    gain_table = 1.0 + joined(made[:, :, 2 * down_own : 2 * down_own + gain_own])
     down_all = (
         made_down.reshape(task_count, model_width, ADA)
         .transpose(1, 0, 2)
@@ -561,49 +899,54 @@
         segments, memory_segments, token_task, backbone, gain_table, down_all, up_all,
     )
     down_rows = (
-        down_all_grad.reshape(model_width, task_count, ADA)
-        .transpose(0, 2, 1)
-        .reshape(model_width * ADA, task_count)
-    )
-    up_rows = (
-        up_all_grad.reshape(task_count, ADA, model_width)
-        .transpose(1, 2, 0)
-        .reshape(ADA * model_width, task_count)
-    )
-    gain_rows_all = gain_grad.T
-
-    def blocks(grad):
-        return grad.reshape(parts, -1, model_width)
-
-    summed = lax.psum_scatter(
-        jnp.concatenate([blocks(g) for g in grads], axis=1), "dp", scatter_dimension=0, tiled=False
-    ).astype(f32)
-    shares = tuple(summed[i * own_rows : (i + 1) * own_rows] for i in range(8)) + (
-        summed[8 * own_rows : 8 * own_rows + in_rows].reshape(hidden_in.shape),
-        summed[8 * own_rows + in_rows :],
-    )
-    small = jnp.concatenate(
-        [r.reshape(parts, -1, task_count) for r in (down_rows, up_rows, gain_rows_all)], axis=1
-    )
-    small = lax.psum_scatter(small, "dp", scatter_dimension=0, tiled=False)
-    own_down = small[:down_own].astype(bf16)
-    own_up = small[down_own : 2 * down_own].astype(bf16)
-    own_gain = small[2 * down_own :]
-    down_maker_grad = plain_dot(own_down, task_low)
-    up_maker_grad = plain_dot(own_up, task_low)
-    gain_maker_grad = exact_dot(own_gain, task_low.astype(f32))
-    state_partial = (
-        inner_cols(own_down, down_maker)
-        + inner_cols(own_up, up_maker)
-        + inner_cols(own_gain, gain_maker.astype(f32), exact_mode)
-    )
-    state_grad = lax.psum(state_partial, "dp")
+        down_all_grad.reshape(parts, -1, task_count, ADA)
+        .transpose(0, 2, 1, 3)
+        .reshape(parts, task_count, down_own)
+    )
+    up_rows = up_all_grad.reshape(task_count, parts, -1).transpose(1, 0, 2)
+    gain_rows_all = gain_grad.reshape(task_count, parts, -1).transpose(1, 0, 2)
+    if parts == 32:
+        small = jnp.concatenate((down_rows, gain_rows_all), axis=2)
+        wide = small.shape[2] + (-small.shape[2] % 256)
+        small = jnp.concatenate(
+            (
+                jnp.pad(small, ((0, 0), (0, 0), (0, wide - small.shape[2]))),
+                jnp.pad(up_rows, ((0, 0), (0, 0), (0, wide - up_rows.shape[2]))),
+            ),
+            axis=1,
+        ).astype(bf16)
+        units = [
+            g.reshape((LINE, 2, 2, 2 * w.shape[0], w.shape[1])) for g, w in zip(grads, weights)
+        ]
+        units.append(small.reshape(LINE, 2, 2, 4 * task_count, wide))
+        *shared, small, state_grad = scatter(units, (down_maker, up_maker, gain_maker))
+        own_down = small[:task_count, :down_own].astype(bf16)
+        own_up = small[task_count:, :down_own].astype(bf16)
+        own_gain = small[:task_count, down_own : down_own + gain_own]
+    else:
+        shared = [
+            lax.psum_scatter(g, "dp", scatter_dimension=0, tiled=True).astype(f32) for g in grads
+        ]
+        small = jnp.concatenate((down_rows, up_rows, gain_rows_all), axis=2)
+        small = lax.psum_scatter(small, "dp", scatter_dimension=0, tiled=False)
+        own_down = small[:, :down_own].astype(bf16)
+        own_up = small[:, down_own : 2 * down_own].astype(bf16)
+        own_gain = small[:, 2 * down_own :]
+        state_grad = lax.psum(
+            plain_dot(own_down, down_maker)
+            + plain_dot(own_up, up_maker)
+            + exact_dot(own_gain, gain_maker.astype(f32)),
+            "dp",
+        )
+    down_maker_grad = inner_cols(own_down, task_low)
+    up_maker_grad = inner_cols(own_up, task_low)
+    gain_maker_grad = inner_cols(own_gain, task_low.astype(f32), exact_mode)
     table_grad, weight_grad, bias_grad = task_back(state_grad)
     return (
         output.reshape(row_count, seq_len, model_width),
         input_grad.reshape(row_count, seq_len, model_width),
         mem_grad.reshape(row_count, mem_len, model_width),
-        *shares,
+        *shared,
         table_grad,
         weight_grad,
         bias_grad,

time: 756 us -> 497 us (0.66)
  waiting for transfers between devices: 390 us -> 0 us
  Pallas kernels: 215 us -> 447 us
  local copies, waits for them, and re-layouts: 81 us -> 31.7 us
  blocking collectives: 36.8 us -> 0 us
  between operations: 14.6 us -> 1.26 us
    pallas_call x0 -> x2, Pallas kernels: none -> 233 us  [the longest x1 124 us: scatter(): pl.pallas_call(functools.partial(scatter_kernel, count, len(makers)), in_...]
    reduce_scatter x2 -> x0, waiting for transfers between devices: 222 us -> none  [the longest x1 166 us: on_device(): lax.psum_scatter(jnp.concatenate([blocks(g) for g in grads], axis=1), 'dp...]
    all_gather x2 -> x0, waiting for transfers between devices: 168 us -> none  [the longest x1 120 us: on_device(): gathered = lax.all_gather(packed, 'dp', axis=0, tiled=False)]
    psum x1 -> x0, blocking collectives: 36.8 us -> none  [on_device(): state_grad = lax.psum(state_partial, 'dp')]
    slice x5 -> x0, local copies, waits for them, and re-layouts: 16.4 us -> none  [the longest x1 7.96 us: on_device(): gathered[:, 8 * own_rows + in_rows:].reshape(-1, model_width)]
    reshape x5 -> x8, local copies, waits for them, and re-layouts: 19 us -> 7.2 us  [the longest x1 2.54 us: on_device(): down_all_grad.reshape(parts, -1, task_count, ADA).transpose(0, 2, 1, 3)]
    unnamed x76 -> x42, local copies, waits for them, and re-layouts: 22.9 us -> 13.8 us
    concatenate x4 -> x0, local copies, waits for them, and re-layouts: 8.23 us -> none  [the longest x1 4.78 us: on_device(): jnp.concatenate([blocks(g) for g in grads], axis=1)]
  transfers between devices with their start and end apart: 4 -> 0, of which waited for: 4 -> 0; matrix products, arithmetic and copies ran while one was open for 7% -> 0% of each run, Pallas kernels for 6% -> 0%
where the time goes in v3:
time: 497 us; the launch traced here: 491 us
  Pallas kernels  447 us (90%)
  local copies, waits for them, and re-layouts  31.7 us (6%)
  matrix products  7.22 us (1%)
    pallas_call x15, Pallas kernels, call(): pl.pallas_call(kernel, grid=grid, in_specs=[pl.BlockSpec(b, m) for _, b,...  214 us
    pallas_call x1, Pallas kernels, scatter(): pl.pallas_call(functools.partial(scatter_kernel, count, len(makers)), in_...  124 us
    pallas_call x1, Pallas kernels, gather(): pl.pallas_call(functools.partial(gather_kernel, count), in_specs=[vmem] *...  108 us
    unnamed x42, local copies, waits for them, and re-layouts  13.8 us

profile of v3, /device:TPU:0, one launch (start us, length us, event | category | flops | bytes accessed | tf_op | source)
XLA Modules:
  0.0 491.2 jit_solution(6780224079039957017)
XLA Ops:
  0.7 1.3 reshape.184.seg_k
  3.5 1.3 reshape.178.seg_k
  5.6 1.2 fusion.5
  9.5 108.4 %gather_weights.1 = (bf16[4,2,2,48,768]{4,3,2,1,0:T(8,128)(2,1)}, bf16[4,2,2,48,768]{4,3,2,1,0:T(8,128)(2,1)}, bf16[4,2,2,48,768]{4,3,2,1,0:T(8,128)(2,1)}, bf16...) custom-call(bf16[24,768]{1,0:T(8,128)(2,1)} %refs_0_.1, ...), custom_call_target="tpu_custom_call" | custom-call | tf_op jit(solution)/shard_map/gather_weights/pallas_call | solution.py:686
  118.0 1.8 copy.84
  121.1 1.2 convert_element_type.37.up_all
  122.3 1.3 convert_element_type.35
  125.7 5.6 %memory_projections.1 = (bf16[1024,768]{1,0:T(8,128)(2,1)}, bf16[1024,768]{1,0:T(8,128)(2,1)}) custom-call(bf16[1024,768]{1,0:T(8,128)(2,1)} %bitcast.113, bf16[768,768]{1,0:T(8,128)(2,1)} %bitcast.115, bf16[768,768]{1,0:T(8,128)(2,1)} %bitcast.117), custom_call_target="tpu_custom_call" | custom-call | flops 2415919104 | bytes 7077888 | tf_op jit(solution)/shard_map/memory_projections/pallas_call | solution.py:93
  131.3 7.8 %self_projections.1 = (bf16[1024,768]{1,0:T(8,128)(2,1)}, bf16[1024,768]{1,0:T(8,128)(2,1)}, bf16[1024,768]{1,0:T(8,128)(2,1)}, bf16[1024,768]{1,0:T(8,128)(2,1)}) custom-call(bf16[1024,768]{1,0:T(8,128)(2,1)} %bitcast.79, s32[1024,1]{1,0:T(8,128)} %bitcast.71, f32[8,768]{1,0:T(8,128)} %get-tuple-element.161.gain, bf16[768,768]{1,0:T(8,128)(2,1)} %bitcast.83, ...), custom_call_target="tpu_custom_call" | custom-call | flops 3623878656 | bytes 11431936 | tf_op jit(solution)/shard_map/self_projections/pallas_call | solution.py:93
  139.1 17.6 %attend_forward.2 = (bf16[1024,768]{1,0:T(8,128)(2,1)}, bf16[2,12,512,512]{3,2,1,0:T(8,128)(2,1)}) custom-call(bf16[1024,768]{1,0:T(8,128)(2,1)} %get-tuple-element.90.q_ref, bf16[1024,768]{1,0:T(8,128)(2,1)} %get-tuple-element.91.k_ref, bf16[1024,768]{1,0:T(8,128)(2,1)} %get-tuple-element.92.v_ref, s32[1024,1]{1,0:T(8,128)} %bitcast.102, ...), custom_call_target="tpu_custom_call" | custom-call | flops 3221225472 | bytes 18882560 | tf_op jit(solution)/shard_map/attend_forward/pallas_call | solution.py:93
  156.7 6.9 %middle.1 = (f32[1024,768]{1,0:T(8,128)}, bf16[1024,768]{1,0:T(8,128)(2,1)}, bf16[1024,768]{1,0:T(8,128)(2,1)}) custom-call(bf16[1024,768]{1,0:T(8,128)(2,1)} %bitcast.80, bf16[1024,768]{1,0:T(8,128)(2,1)} %get-tuple-element.93.mixed.mixed_ref.refs_0_, bf16[768,768]{1,0:T(8,128)(2,1)} %bitcast.93, s32[1024,1]{1,0:T(8,128)} %bitcast.72, ...), custom_call_target="tpu_custom_call" | custom-call | flops 2415919104 | bytes 11825152 | tf_op jit(solution)/shard_map/middle/pallas_call | solution.py:93
  163.5 21.8 %attend_forward.3 = (bf16[1024,768]{1,0:T(8,128)(2,1)}, bf16[2,12,512,512]{3,2,1,0:T(8,128)(2,1)}) custom-call(bf16[1024,768]{1,0:T(8,128)(2,1)} %get-tuple-element.97.q_ref, bf16[1024,768]{1,0:T(8,128)(2,1)} %get-tuple-element.100.k_ref, bf16[1024,768]{1,0:T(8,128)(2,1)} %get-tuple-element.101.v_ref, s32[1024,1]{1,0:T(8,128)} %bitcast.103, ...), custom_call_target="tpu_custom_call" | custom-call | flops 3221225472 | bytes 18882560 | tf_op jit(solution)/shard_map/attend_forward/pallas_call | solution.py:93
  185.3 47.0 %feed_forward_and_back.1 = (bf16[1024,768]{1,0:T(8,128)(2,1)}, bf16[1024,768]{1,0:T(8,128)(2,1)}, bf16[1024,3072]{1,0:T(8,128)(2,1)}, bf16[1024,3072]{1,0:T(8,12...) custom-call(f32[1024,768]{1,0:T(8,128)} %get-tuple-element.96.s1, ...), custom_call_target="tpu_custom_call" | custom-call | flops 21743271936 | bytes 42323968 | tf_op jit(solution)/shard_map/feed_forward_and_back/pallas_call | solution.py:93
  232.3 20.2 %attend_backward.2 = (bf16[1024,768]{1,0:T(8,128)(2,1)}, bf16[1024,768]{1,0:T(8,128)(2,1)}, bf16[1024,768]{1,0:T(8,128)(2,1)}) custom-call(bf16[1024,768]{1,0:T(8,128)(2,1)} %get-tuple-element.97.q_ref, bf16[1024,768]{1,0:T(8,128)(2,1)} %get-tuple-element.100.k_ref, bf16[1024,768]{1,0:T(8,128)(2,1)} %get-tuple-element.101.v_ref, ...), custom_call_target="tpu_custom_call" | custom-call | flops 6442450944 | bytes 25165824 | tf_op jit(solution)/shard_map/attend_backward/pallas_call | solution.py:93
  252.5 9.8 %cross_back.1 = (f32[1024,768]{1,0:T(8,128)}, bf16[1024,768]{1,0:T(8,128)(2,1)}, bf16[1024,768]{1,0:T(8,128)(2,1)}, f32[8,768]{1,0:T(8,128)}) custom-call(bf16[1024,768]{1,0:T(8,128)(2,1)} %get-tuple-element.109.gq.refs_4_, bf16[768,768]{1,0:T(8,128)(2,1)} %bitcast.96, f32[1024,768]{1,0:T(8,128)} %get-tuple-element.96.s1, s32[1024,1]{1,0:T(8,128)} %bitcast.74, ...), custom_call_target="tpu_custom_call" | custom-call | flops 2415919104 | bytes 16568320 | tf_op jit(solution)/shard_map/cross_back/pallas_call | solution.py:93
  262.3 9.8 %cross_grads.1 = (bf16[768,768]{1,0:T(8,128)(2,1)}, bf16[768,768]{1,0:T(8,128)(2,1)}, bf16[768,768]{1,0:T(8,128)(2,1)}, bf16[768,768]{1,0:T(8,128)(2,1)}) custom-call(bf16[1024,768]{1,0:T(8,128)(2,1)} %get-tuple-element.102.mixed.mixed_ref.refs_0_, bf16[1024,768]{1,0:T(8,128)(2,1)} %get-tuple-element.126.refs_1_, bf16[1024,768]{1,0:T(8,128)(2,1)} %bitcast.114, ...), custom_call_target="tpu_custom_call" | custom-call | flops 4831838208 | bytes 15728640 | tf_op jit(solution)/shard_map/cross_grads/pallas_call | solution.py:93
  272.1 6.3 %memory_back.1 = f32[1024,768]{1,0:T(8,128)} custom-call(bf16[1024,768]{1,0:T(8,128)(2,1)} %get-tuple-element.118.gk.refs_5_, bf16[1024,768]{1,0:T(8,128)(2,1)} %get-tuple-element.119.gv.refs_6_, bf16[768,768]{1,0:T(8,128)(2,1)} %bitcast.116, bf16[768,768]{1,0:T(8,128)(2,1)} %bitcast.118), custom_call_target="tpu_custom_call" | custom-call | flops 2415919104 | bytes 8650752 | tf_op jit(solution)/shard_map/memory_back/pallas_call | solution.py:93
  278.4 18.3 %attend_backward.3 = (bf16[1024,768]{1,0:T(8,128)(2,1)}, bf16[1024,768]{1,0:T(8,128)(2,1)}, bf16[1024,768]{1,0:T(8,128)(2,1)}) custom-call(bf16[1024,768]{1,0:T(8,128)(2,1)} %get-tuple-element.90.q_ref, bf16[1024,768]{1,0:T(8,128)(2,1)} %get-tuple-element.91.k_ref, bf16[1024,768]{1,0:T(8,128)(2,1)} %get-tuple-element.92.v_ref, ...), custom_call_target="tpu_custom_call" | custom-call | flops 6442450944 | bytes 25165824 | tf_op jit(solution)/shard_map/attend_backward/pallas_call | solution.py:93
  296.7 11.1 %input_back.1 = (f32[1024,768]{1,0:T(8,128)}, f32[8,768]{1,0:T(8,128)}) custom-call(bf16[1024,768]{1,0:T(8,128)(2,1)} %get-tuple-element.113.gq.refs_3_, bf16[1024,768]{1,0:T(8,128)(2,1)} %get-tuple-element.114.gk.refs_4_, bf16[1024,768]{1,0:T(8,128)(2,1)} %get-tuple-element.115.gv.refs_5_, bf16[768,768]{1,0:T(8,128)(2,1)} %bitcast.84, ...), custom_call_target="tpu_custom_call" | custom-call | flops 3623878656 | bytes 16175104 | tf_op jit(solution)/shard_map/input_back/pallas_call | solution.py:93
  307.8 9.6 %self_grads.1 = (bf16[768,768]{1,0:T(8,128)(2,1)}, bf16[768,768]{1,0:T(8,128)(2,1)}, bf16[768,768]{1,0:T(8,128)(2,1)}, bf16[768,768]{1,0:T(8,128)(2,1)}) custom-call(bf16[1024,768]{1,0:T(8,128)(2,1)} %get-tuple-element.93.mixed.mixed_ref.refs_0_, bf16[1024,768]{1,0:T(8,128)(2,1)} %get-tuple-element.120.refs_1_, ...), custom_call_target="tpu_custom_call" | custom-call | flops 4831838208 | bytes 14155776 | tf_op jit(solution)/shard_map/self_grads/pallas_call | solution.py:93
  319.2 2.5 reshape.203
  321.7 1.9 copy.74
  325.7 9.9 %hidden_in_grad.1 = bf16[768,3072]{1,0:T(8,128)(2,1)} custom-call(bf16[1024,768]{1,0:T(8,128)(2,1)} %get-tuple-element.132.refs_0_, bf16[1024,3072]{1,0:T(8,128)(2,1)} %get-tuple-element.133.refs_1_), custom_call_target="tpu_custom_call" | custom-call | flops 4831838208 | bytes 12582912 | tf_op jit(solution)/shard_map/hidden_in_grad/pallas_call | solution.py:93
  335.7 12.9 %hidden_out_grad.1 = bf16[3072,768]{1,0:T(8,128)(2,1)} custom-call(bf16[1024,3072]{1,0:T(8,128)(2,1)} %get-tuple-element.134.refs_0_, bf16[1024,768]{1,0:T(8,128)(2,1)} %get-tuple-element.135.refs_1_), custom_call_target="tpu_custom_call" | custom-call | flops 4831838208 | bytes 12582912 | tf_op jit(solution)/shard_map/hidden_out_grad/pallas_call | solution.py:93
  348.5 124.1 %scatter_gradients.1 = (f32[24,768]{1,0:T(8,128)}, f32[24,768]{1,0:T(8,128)}, f32[24,768]{1,0:T(8,128)}, f32[24,768]{1,0:T(8,128)}, f32[24,768]{1,0:T(8,128)}, /...) custom-call(bf16[4,2,2,48,768]{4,3,2,1,0:T(8,128)(2,1)} %bitcast.98,, ...), custom_call_target="tpu_custom_call" | custom-call | tf_op jit(solution)/shard_map/scatter_gradients/pallas_call | solution.py:834
  472.7 1.3 fusion.25
  475.6 1.6 fusion.17
  480.0 1.5 copy.97
  481.5 1.5 copy.98
  483.0 1.5 copy.99
  484.6 1.5 copy.100
  486.1 1.5 copy.101
  (66 shorter events, 20.0 us)
Async XLA Ops:
  0.7 4.1 copy-start
  118.0 1.8 copy-start.1
  307.8 9.6 %copy-start.12 = (f32[8,768]{1,0:T(8,128)S(1)}, f32[8,768]{1,0:T(8,128)}, u32[]{:S(2)}) copy-start(f32[8,768]{1,0:T(8,128)} %get-tuple-element.137) | copy-start | bytes 73732
  307.8 9.6 %copy-start.11 = (f32[8,768]{1,0:T(8,128)S(1)}, f32[8,768]{1,0:T(8,128)}, u32[]{:S(2)}) copy-start(f32[8,768]{1,0:T(8,128)} %get-tuple-element.138) | copy-start | bytes 73732
  307.8 9.6 %copy-start.10 = (f32[8,768]{1,0:T(8,128)S(1)}, f32[8,768]{1,0:T(8,128)}, u32[]{:S(2)}) copy-start(f32[8,768]{1,0:T(8,128)} %get-tuple-element.139) | copy-start | bytes 73732
  307.8 10.5 %copy-start.3 = (f32[192,768]{1,0:T(8,128)S(1)}, f32[192,768]{1,0:T(8,128)}, u32[]{:S(2)}) copy-start(f32[192,768]{1,0:T(8,128)} %get-tuple-element.140) | copy-start | bytes 1769476
  317.4 1.6 copy-start.2
  323.6 1.1 copy-start.6
  348.5 128.7 %copy-start.13 = (f32[8,64]{1,0:T(8,128)S(1)}, f32[8,64]{1,0:T(8,128)}, u32[]{:S(2)}) copy-start(f32[8,64]{1,0:T(8,128)} %param.38) | copy-start | bytes 6148
  472.7 14.9 %copy-start.9 = (f32[24,768]{1,0:T(8,128)S(1)}, f32[24,768]{1,0:T(8,128)}, u32[]{:S(2)}) copy-start(f32[24,768]{1,0:T(8,128)} %get-tuple-element.190) | copy-start | bytes 221188
  472.7 15.5 %copy-start.8 = (f32[24,768]{1,0:T(8,128)S(1)}, f32[24,768]{1,0:T(8,128)}, u32[]{:S(2)}) copy-start(f32[24,768]{1,0:T(8,128)} %get-tuple-element.191) | copy-start | bytes 221188
  472.7 16.2 %copy-start.7 = (f32[24,768]{1,0:T(8,128)S(1)}, f32[24,768]{1,0:T(8,128)}, u32[]{:S(2)}) copy-start(f32[24,768]{1,0:T(8,128)} %get-tuple-element.192) | copy-start | bytes 221188
  472.7 16.8 %copy-start.5 = (f32[24,3072]{1,0:T(8,128)S(1)}, f32[24,3072]{1,0:T(8,128)}, u32[]{:S(2)}) copy-start(f32[24,3072]{1,0:T(8,128)} %get-tuple-element.193) | copy-start | bytes 884740
  472.7 17.5 %copy-start.4 = (f32[96,768]{1,0:T(8,128)S(1)}, f32[96,768]{1,0:T(8,128)}, u32[]{:S(2)}) copy-start(f32[96,768]{1,0:T(8,128)} %get-tuple-element.194) | copy-start | bytes 884740

commit v4 on v3

--- a/solution.py
+++ b/solution.py
@@ -392,28 +392,31 @@
     )
 
 
-def layer(x, mem, cot, segments, mem_segments, task, weights, gain_table, down_all, up_all):
+BLOCK = 512
+
+
+def low_out(shape):
+    return out_row(shape, bf16, BLOCK)
+
+
+def full_out(shape):
+    return out_row(shape, f32, BLOCK)
+
+
+def attention_layers(x, mem, segments, mem_segments, task, weights, gain_table):
     rows, length = segments.shape
-    mem_len = mem_segments.shape[1]
     tokens, width = x.shape
-    wq1, wk1, wv1, wo1, wq2, wk2, wv2, wo2, w_in, w_out = weights
-    gain_one, gain_two, gain_three = (gain_table[:, i * width : (i + 1) * width] for i in range(3))
-    block = 512
+    wq1, wk1, wv1, wo1, wq2, wk2, wv2 = weights[:7]
+    gain_one, gain_two = (gain_table[:, i * width : (i + 1) * width] for i in range(2))
+    block = BLOCK
     grid = (tokens // block,)
     act_shape = (tokens, width)
-
-    def low_out():
-        return out_row(act_shape, bf16, block)
-
-    def full_out():
-        return out_row(act_shape, f32, block)
-
     square = 2 * tokens * width * width
     n1, q1, k1, v1 = call(
         pre_kernel,
         grid,
         [by_row(x, block), by_row(task, block)] + [whole(a) for a in (gain_one, wq1, wk1, wv1)],
-        [low_out() for _ in range(4)],
+        [low_out(act_shape) for _ in range(4)],
         flops=3 * square,
         name="self_projections",
     )
@@ -422,7 +425,7 @@
         middle_kernel,
         grid,
         [by_row(x, block), by_row(m1, block), whole(wo1), by_row(task, block), whole(gain_two), whole(wq2)],
-        [full_out(), low_out(), low_out()],
+        [full_out(act_shape), low_out(act_shape), low_out(act_shape)],
         flops=2 * square,
         name="middle",
     )
@@ -430,11 +433,24 @@
         memory_kernel,
         grid,
         [by_row(mem, block), whole(wk2), whole(wv2)],
-        [low_out(), low_out()],
+        [low_out(mem.shape), low_out(mem.shape)],
         flops=2 * square,
         name="memory_projections",
     )
     m2, p2 = attend_forward(False, rows, length, q2, k2, v2, segments, mem_segments)
+    return (n1, q1, k1, v1, m1, s1, n2, q2, k2, v2, m2), p1, p2
+
+
+def feed_and_back(x, mem, cot, rows, task, weights, gain_table, down_all, up_all, saved, p1, p2):
+    n1, q1, k1, v1, m1, s1, n2, q2, k2, v2, m2 = saved
+    tokens, width = x.shape
+    length = tokens // rows
+    wq1, wk1, wv1, wo1, wq2, wk2, wv2, wo2, w_in, w_out = weights
+    gain_one, gain_two, gain_three = (gain_table[:, i * width : (i + 1) * width] for i in range(3))
+    block = BLOCK
+    grid = (tokens // block,)
+    act_shape = (tokens, width)
+    square = 2 * tokens * width * width
     units = w_in.shape[1]
     wide = up_all.shape[0]
     tasks = gain_table.shape[0]
@@ -446,8 +462,8 @@
             whole(w_in), whole(w_out), whole(down_all), whole(up_all), by_row(cot, block),
         ],
         [
-            low_out(), low_out(), out_row((tokens, units), bf16, block), out_row((tokens, units), bf16, block),
-            low_out(), full_out(), low_out(), low_out(),
+            low_out(act_shape), low_out(act_shape), out_row((tokens, units), bf16, block), out_row((tokens, units), bf16, block),
+            low_out(act_shape), full_out(act_shape), low_out(act_shape), low_out(act_shape),
             out_whole((wide, width), f32), out_whole((width, wide), f32), out_whole((tasks, width), f32),
         ],
         scratch=[pltpu.VMEM((block, units), bf16), pltpu.VMEM((block, width), f32)],
@@ -464,7 +480,7 @@
             by_row(gq2, block), whole(wq2), by_row(s1, block), by_row(task, block), whole(gain_two),
             by_row(g2, block), whole(wo1),
         ],
-        [full_out(), low_out(), low_out(), out_whole((tasks, width), f32)],
+        [full_out(act_shape), low_out(act_shape), low_out(act_shape), out_whole((tasks, width), f32)],
         flops=2 * square,
         name="cross_back",
     )
@@ -472,7 +488,7 @@
         memory_back_kernel,
         grid,
         [by_row(gk2, block), by_row(gv2, block), whole(wk2), whole(wv2)],
-        [full_out()],
+        [full_out(act_shape)],
         flops=2 * square,
         name="memory_back",
     )
@@ -487,7 +503,7 @@
             by_row(gq1, block), by_row(gk1, block), by_row(gv1, block), whole(wq1), whole(wk1), whole(wv1),
             by_row(x, block), by_row(task, block), whole(gain_one), by_row(g1, block),
         ],
-        [full_out(), out_whole((tasks, width), f32)],
+        [full_out(act_shape), out_whole((tasks, width), f32)],
         flops=3 * square,
         name="input_back",
     )
@@ -584,122 +600,6 @@
         for late, stage in enumerate(stages):
             if 0 <= turn - late < count:
                 stage(turn - late)
-
-
-def gather_kernel(count, *refs):
-    own, made = refs[:count], refs[count]
-    outs, made_out = refs[count + 1 : 2 * count + 1], refs[2 * count + 1]
-    scratch = refs[2 * count + 2 :]
-    whole_rows, halves, blocks = scratch[:count], scratch[count : 2 * count], scratch[2 * count : 3 * count]
-    send, recv = scratch[3 * count :]
-    here = Place()
-    copies = Copies(send, recv)
-    z, y, x, c = here.z, here.y, here.x, here.core
-
-    def half(i, core):
-        width = outs[i].shape[-1] // 2
-        return pl.ds(pl.multiple_of(core * width, 128), width)
-
-    for i in range(count):
-        whole_rows[i][...] = own[i][...].astype(f32)
-    meet(here)
-    pair, first, second, third, last = {}, {}, {}, {}, {}
-    half_made = made_out.shape[-1] // 2
-    made_cols = (pl.ds(0, half_made), pl.ds(half_made, half_made))
-    made_first = [copies.local(made, made_out.at[z, y, x, c])]
-    made_first += [
-        copies.remote(made, made_out.at[z, y, x, c], here.along_z(k)) for k in (1, 2, 3)
-    ]
-    for i in range(count):
-        rows = own[i].shape[0]
-        mine = pl.ds(pl.multiple_of(c * rows, 8), rows)
-        pair[i] = copies.remote(
-            whole_rows[i].at[:, half(i, 1 - c)], halves[i].at[mine, :], here.sibling()
-        )
-        halves[i][mine, :] = whole_rows[i][:, half(i, c)]
-    for i in range(count):
-        pair[i].wait_recv()
-        blocks[i][...] = halves[i][...].astype(bf16)
-        target = outs[i].at[z, y, x, :, half(i, c)]
-        first[i] = [copies.remote(blocks[i], target, here.along_z(k)) for k in (1, 2, 3)]
-        first[i].append(copies.local(blocks[i], target))
-
-    made_first[0].wait()
-    for copy in made_first[1:]:
-        copy.wait_recv()
-    made_second = []
-    for cols, device in zip(made_cols, (here.over_x(), here.over_y())):
-        part = made_out.at[:, y, x, c, :, cols]
-        made_second.append(copies.remote(part, part, device))
-    for copy in made_second:
-        copy.wait_recv()
-    made_third = []
-    for part, device in (
-        (made_out.at[:, y, :, c, :, made_cols[0]], here.over_y()),
-        (made_out.at[:, :, x, c, :, made_cols[1]], here.over_x()),
-    ):
-        made_third.append(copies.remote(part, part, device))
-
-    def along_first(i):
-        for copy in first[i][:3]:
-            copy.wait_recv()
-        first[i][3].wait()
-        second[i] = []
-        for rows, device in zip(shares(outs[i].shape[3], i), (here.over_x(), here.over_y())):
-            part = outs[i].at[:, y, x, rows, half(i, c)]
-            second[i].append(copies.remote(part, part, device))
-
-    def along_second(i):
-        for copy in second[i]:
-            copy.wait_recv()
-        one, two = shares(outs[i].shape[3], i)
-        third[i] = []
-        for part, device in (
-            (outs[i].at[:, y, :, one, half(i, c)], here.over_y()),
-            (outs[i].at[:, :, x, two, half(i, c)], here.over_x()),
-        ):
-            third[i].append(copies.remote(part, part, device))
-
-    def to_sibling(i):
-        for copy in third[i]:
-            copy.wait_recv()
-        part = outs[i].at[:, :, :, :, half(i, c)]
-        last[i] = copies.remote(part, part, here.sibling())
-
-    stepped(count, (along_first, along_second, to_sibling))
-    for copy in made_third:
-        copy.wait_recv()
-    part = made_out.at[:, :, :, c]
-    made_last = copies.remote(part, part, here.sibling())
-    for i in range(count):
-        last[i].wait_recv()
-    made_last.wait_recv()
-    copies.finish()
-
-
-def gather(own, made):
-    count = len(own)
-    spaces = LINE, 2, 2
-    copies = 10 * count + 12
-    any_space = pl.BlockSpec(memory_space=pl.ANY)
-    vmem = pl.BlockSpec(memory_space=pltpu.VMEM)
-    return pl.pallas_call(
-        functools.partial(gather_kernel, count),
-        in_specs=[vmem] * (count + 1),
-        out_specs=[any_space] * (count + 1),
-        out_shape=[
-            jax.ShapeDtypeStruct(spaces + (2 * a.shape[0], a.shape[1]), bf16) for a in own
-        ]
-        + [jax.ShapeDtypeStruct(spaces + (2,) + made.shape, f32)],
-        scratch_shapes=[pltpu.VMEM(a.shape, f32) for a in own]
-        + [pltpu.VMEM((2 * a.shape[0], a.shape[1] // 2), f32) for a in own]
-        + [pltpu.VMEM((2 * a.shape[0], a.shape[1] // 2), bf16) for a in own]
-        + [pltpu.SemaphoreType.DMA((copies,)), pltpu.SemaphoreType.DMA((copies,))],
-        compiler_params=pltpu.CompilerParams(
-            collective_id=0, has_side_effects=True, vmem_limit_bytes=VMEM_BYTES
-        ),
-        name="gather_weights",
-    )(*own, made)
 
 
 def scatter_kernel(count, makers, *refs):
@@ -845,6 +745,381 @@
     )(*grads, *makers)
 
 
+class Unit:
+    def __init__(self, here, copies, source, whole_array, index, first, second):
+        self.here, self.copies = here, copies
+        self.source, self.array = source, whole_array
+        self.index, self.shares = index, (first, second)
+        self.going = {}
+
+    def window(self, zs, ys, xs, share=None):
+        return self.array.at[(zs, ys, xs) + (self.index if share is None else self.shares[share])]
+
+    def depart(self):
+        here, copies = self.here, self.copies
+        source = self.source()
+        target = self.window(here.z, here.y, here.x)
+        self.going["z"] = [copies.remote(source, target, here.along_z(k)) for k in (1, 2, 3)]
+        self.own = copies.local(source, target)
+
+    def turn(self):
+        here = self.here
+        for copy in self.going["z"]:
+            copy.wait_recv()
+        self.own.wait()
+        one = self.window(slice(None), here.y, here.x, 0)
+        two = self.window(slice(None), here.y, here.x, 1)
+        self.going["1"] = [
+            self.copies.remote(one, one, here.over_x()),
+            self.copies.remote(two, two, here.over_y()),
+        ]
+
+    def turn_again(self):
+        here = self.here
+        for copy in self.going["1"]:
+            copy.wait_recv()
+        one = self.window(slice(None), here.y, slice(None), 0)
+        two = self.window(slice(None), slice(None), here.x, 1)
+        self.going["2"] = [
+            self.copies.remote(one, one, here.over_y()),
+            self.copies.remote(two, two, here.over_x()),
+        ]
+
+    def cross(self):
+        for copy in self.going["2"]:
+            copy.wait_recv()
+        part = self.window(slice(None), slice(None), slice(None))
+        self.going["c"] = self.copies.remote(part, part, self.here.sibling())
+
+    def settle(self):
+        self.going["c"].wait_recv()
+
+    def stages(self):
+        return (self.depart, self.turn, self.turn_again, self.cross, self.settle)
+
+
+def column_of(row):
+    length = row.shape[1]
+    at_q = lax.broadcasted_iota(jnp.int32, (length, length), 0)
+    at_k = lax.broadcasted_iota(jnp.int32, (length, length), 1)
+    picked = jnp.where(at_q == at_k, row.astype(f32), 0.0)
+    return jnp.sum(picked, axis=1, keepdims=True).astype(jnp.int32)
+
+
+def forward_kernel(*refs):
+    (
+        x, mem, segments, mem_segments, tasks,
+        sq, sk, sv, so, cq, ck, cv, co, w_in, w_out,
+        table, weight, bias_row, down, up, gain,
+    ) = refs[:21]
+    outs, made_out, gains_out = refs[21:31], refs[31], refs[32]
+    low_out, gain_out, task_out = refs[33:36]
+    saved_out = refs[36:47]
+    p1_out, p2_out = refs[47:49]
+    scratch = refs[49:]
+    wide, halves, blocks = scratch[:10], scratch[10:20], scratch[20:30]
+    local_w = scratch[30:38]
+    saved = scratch[38:49]
+    n1, q1, k1, v1, m1, s1, n2, q2, k2, v2, m2 = saved
+    made, gain_rows_all, bias, probs, send, recv, p_sem, load_sem, save_sem, gain_full = scratch[49:]
+    own = (sq, sk, sv, so, cq, ck, cv, co, w_in, w_out)
+    rows_total, length = segments.shape
+    mem_len = mem_segments.shape[1]
+    here = Place()
+    copies = Copies(send, recv)
+    c = here.core
+
+    def half(i, core, first=0, width=None):
+        full = own[i].shape[1] // 2
+        width = full if width is None else width
+        return pl.ds(pl.multiple_of(core * full + first, 128), width)
+
+    for i in range(10):
+        wide[i][...] = own[i][...].astype(f32)
+    gain_rows_all[...] = gain[...].astype(f32)
+    probs[...] = jnp.zeros_like(probs)
+    meet(here)
+    pair = {}
+    order = (0, 1, 2, 5, 6, 3, 4, 7, 8, 9)
+    for i in order:
+        rows = own[i].shape[0]
+        mine = pl.ds(pl.multiple_of(c * rows, 8), rows)
+        pair[i] = copies.remote(
+            wide[i].at[:, half(i, 1 - c)], halves[i].at[mine, :], here.sibling()
+        )
+        halves[i][mine, :] = wide[i][:, half(i, c)]
+
+    opened = set()
+
+    def piece(i, rows, first, width):
+        def source():
+            if i not in opened:
+                opened.add(i)
+                pair[i].wait_recv()
+                blocks[i][...] = halves[i][...].astype(bf16)
+            return blocks[i].at[rows, pl.ds(first, width)]
+
+        at = half(i, c, first, width)
+        count = rows.stop - rows.start
+        if (width // 2) % 128 == 0:
+            one = (rows, half(i, c, first, width // 2))
+            two = (rows, half(i, c, first + width // 2, width // 2))
+        else:
+            cut = rows.start + (count // 2 if count % 32 == 0 else (count // 32 + i % 2) * 16)
+            one = (slice(rows.start, cut), at)
+            two = (slice(cut, rows.stop), at)
+        return Unit(here, copies, source, outs[i], (rows, at), one, two)
+
+    def square(i):
+        return piece(i, slice(0, outs[i].shape[3]), 0, own[i].shape[1] // 2)
+
+    gain_own = gain.shape[0]
+    gain_cut = gain_own // 16 * 8
+    made_cut = made.shape[1] // 2
+    gain_unit = Unit(
+        here, copies, lambda: gain_rows_all, gains_out, (c,),
+        (c, pl.ds(0, gain_cut)), (c, pl.ds(gain_cut, gain_own - gain_cut)),
+    )
+    made_unit = Unit(
+        here, copies, lambda: made, made_out, (c,),
+        (c, slice(None), pl.ds(0, made_cut)), (c, slice(None), pl.ds(made_cut, made_cut)),
+    )
+    in_half = w_in.shape[1] // 4
+    out_rows = outs[9].shape[3]
+    units = [gain_unit] + [square(i) for i in (0, 1, 2, 5, 6, 3, 4, 7)]
+    units += [piece(8, slice(0, outs[8].shape[3]), k * in_half, in_half) for k in (0, 1)]
+    units += [made_unit]
+    units += [
+        piece(9, slice(k * out_rows // 2, (k + 1) * out_rows // 2), 0, w_out.shape[1] // 2)
+        for k in (0, 1)
+    ]
+    loads = {}
+    landing = {1: (0,), 2: (1,), 3: (2,), 4: (5,), 5: (6,), 6: (3,), 7: (4,), 8: (7,)}
+
+    def tick(turn):
+        for late in range(5):
+            u = turn - late
+            if 0 <= u < len(units):
+                units[u].stages()[late]()
+                if late == 4 and u in landing:
+                    (i,) = landing[u]
+                    loads[i] = pltpu.make_async_copy(outs[i], local_w[i], load_sem.at[i])
+                    loads[i].start()
+                if late == 4 and u == 0:
+                    loads["gain"] = pltpu.make_async_copy(gains_out, gain_full, load_sem.at[8])
+                    loads["gain"].start()
+
+
+    def matrix(i):
+        return local_w[i][...].reshape(-1, own[i].shape[1])
+
+    state = gelu_in_kernel(exact_dot(table[...], weight[...]) + bias_row[...])
+    low = state.astype(bf16)
+    low_out[...] = low
+    made[...] = jnp.zeros_like(made)
+    made[:, : down.shape[0]] = inner_rows(low, down[...])
+    made_at = made.shape[1] // 2
+    made[:, made_at : made_at + up.shape[0]] = inner_rows(low, up[...])
+
+    for now in range(8):
+        tick(now)
+    ticks = iter(range(8, len(units) + 4))
+
+    def between():
+        turn = next(ticks, None)
+        if turn is not None:
+            tick(turn)
+
+    stores = []
+
+    def store(which, part=None):
+        source, target = saved[which], saved_out[which]
+        copy = pltpu.make_async_copy(source, target, save_sem.at[which])
+        copy.start()
+        stores.append(copy)
+
+    for r in range(rows_total):
+        column = column_of(segments[r : r + 1, :])
+        task = jnp.zeros_like(column)
+        for s in range(tasks.shape[1]):
+            task = task + jnp.where(column == s, tasks[r : r + 1, s : s + 1], 0)
+        task_out[r * length : (r + 1) * length, :] = task
+    loads["gain"].wait()
+    width = x.shape[1]
+    gain_out[...] = 1.0 + inner_rows(low, gain_full[...].reshape(-1, gain.shape[1]).astype(bf16))
+
+    def picked(r, which):
+        task = task_out[r * length : (r + 1) * length, :]
+        return token_gain(task, gain_out[:, which * width : (which + 1) * width])
+
+    def row(r, size=None):
+        size = length if size is None else size
+        return slice(r * size, (r + 1) * size)
+
+    for i in (0, 1, 2):
+        loads[i].wait()
+    for r in range(rows_total):
+        stream = x[row(r), :].astype(f32)
+        n = (stream * inverse_rms(stream) * picked(r, 0)).astype(bf16)
+        n1[row(r), :] = n
+        q1[row(r), :] = (plain_dot(n, matrix(0)).astype(bf16).astype(f32) * HEAD**-0.5).astype(bf16)
+        k1[row(r), :] = plain_dot(n, matrix(1)).astype(bf16)
+        v1[row(r), :] = plain_dot(n, matrix(2)).astype(bf16)
+        between()
+    for which in (0, 1, 2, 3):
+        store(which)
+
+
+    def attend(causal, q, k, v, mixed, p_out, r, keys_row):
+        column = column_of(segments[r : r + 1, :])
+        same = column == keys_row
+        if causal:
+            at_q = lax.broadcasted_iota(jnp.int32, same.shape, 0)
+            at_k = lax.broadcasted_iota(jnp.int32, same.shape, 1)
+            same = same & (at_q >= at_k)
+        bias[...] = jnp.where(same, 0.0, masked_score)
+        keys_total = keys_row.shape[1]
+        per_group = HEADS // 4
+        for group in range(2):
+            @pl.loop(group * per_group, (group + 1) * per_group)
+            def _(p):
+                slot = lax.rem(p, 2)
+                at = pl.ds(pl.multiple_of(p * PAIR, PAIR), PAIR)
+
+                @pl.when(p >= 2)
+                def _():
+                    pltpu.make_async_copy(
+                        probs.at[slot], p_out.at[r, pl.ds(2 * p - 4, 2)], p_sem.at[slot]
+                    ).wait()
+
+                attend_pair(causal, q, k, v, mixed, probs.at[slot], bias, row(r), row(r, keys_total), at)
+                pltpu.make_async_copy(
+                    probs.at[slot], p_out.at[r, pl.ds(2 * p, 2)], p_sem.at[slot]
+                ).start()
+
+            between()
+        for p in (HEADS // 2 - 2, HEADS // 2 - 1):
+            pltpu.make_async_copy(
+                probs.at[p % 2], p_out.at[r, pl.ds(2 * p, 2)], p_sem.at[p % 2]
+            ).wait()
+
+    for r in range(rows_total):
+        attend(True, q1, k1, v1, m1, p1_out, r, segments[r : r + 1, :])
+    store(4)
+    for i in (5, 6):
+        loads[i].wait()
+    for r in range(rows_total):
+        mine = row(r, mem_len)
+        k2[mine, :] = plain_dot(mem[mine, :], matrix(5)).astype(bf16)
+        v2[mine, :] = plain_dot(mem[mine, :], matrix(6)).astype(bf16)
+        between()
+    store(8)
+    store(9)
+    for i in (3, 4):
+        loads[i].wait()
+    for r in range(rows_total):
+        stream = x[row(r), :].astype(f32) + plain_dot(m1[row(r), :], matrix(3))
+        s1[row(r), :] = stream
+        n = (stream * inverse_rms(stream) * picked(r, 1)).astype(bf16)
+        n2[row(r), :] = n
+        q2[row(r), :] = (plain_dot(n, matrix(4)).astype(bf16).astype(f32) * HEAD**-0.5).astype(bf16)
+        between()
+    for which in (5, 6, 7):
+        store(which)
+    for r in range(rows_total):
+        attend(False, q2, k2, v2, m2, p2_out, r, mem_segments[r : r + 1, :])
+    store(10)
+    for turn in ticks:
+        tick(turn)
+    loads[7].wait()
+    for copy in stores:
+        copy.wait()
+    copies.finish()
+
+
+def gelu_in_kernel(v):
+    return v * (0.5 * lax.erf(v * 0.7071067811865476) + 0.5)
+
+
+def attend_pair(causal, q_ref, k_ref, v_ref, mixed_ref, p_ref, bias, q_rows, k_rows, at):
+    length = q_rows.stop - q_rows.start
+    keys_all = k_rows.stop - k_rows.start
+    step = length // 2 if causal else length
+    masks = half_masks()
+    for first in range(0, length, step):
+        rows = slice(q_rows.start + first, q_rows.start + first + step)
+        keys = first + step if causal else keys_all
+        q = q_ref[rows, at]
+        k = k_ref[k_rows.start : k_rows.start + keys, at]
+        v = v_ref[k_rows.start : k_rows.start + keys, at]
+        out = None
+        for h, mask in enumerate(masks):
+            s = inner_rows(q * mask, k) + bias[first : first + step, :keys]
+            e = jnp.exp(s - jnp.max(s, axis=-1, keepdims=True))
+            p = (e * (1.0 / jnp.sum(e, axis=-1, keepdims=True))).astype(bf16)
+            p_ref[h, first : first + step, :keys] = p
+            part = plain_dot(p, v * mask)
+            out = part if out is None else out + part
+        mixed_ref[rows, at] = out.astype(bf16)
+
+
+def forward(x, mem, segments, mem_segments, tasks, weights, table, weight, bias_row, makers):
+    down, up, gain = makers
+    own = weights
+    tokens, width = x.shape
+    mem_tokens = mem.shape[0]
+    rows, length = segments.shape
+    mem_len = mem_segments.shape[1]
+    spaces = (LINE, 2, 2)
+    any_space = pl.BlockSpec(memory_space=pl.ANY)
+    vmem = pl.BlockSpec(memory_space=pltpu.VMEM)
+    made_half = down.shape[0] + (-down.shape[0] % 128)
+    n_tasks = table.shape[0]
+    chip = [spaces + (2 * a.shape[0], a.shape[1]) for a in own]
+    t_low, m_low, t_full = ((tokens, width), bf16), ((mem_tokens, width), bf16), ((tokens, width), f32)
+    kept = [t_low, t_low, t_low, t_low, t_low, t_full, t_low, t_low, m_low, m_low, t_low]
+    shape = jax.ShapeDtypeStruct
+    probs = (rows, HEADS, length, mem_len)
+    copies = 11 * 16 + 16
+    outs = pl.pallas_call(
+        forward_kernel,
+        in_specs=[vmem] * 21,
+        out_specs=[any_space] * 12 + [vmem] * 3 + [any_space] * 13,
+        out_shape=[shape(s, bf16) for s in chip]
+        + [
+            shape(spaces + (2, n_tasks, 2 * made_half), f32),
+            shape(spaces + (2,) + gain.shape, f32),
+            shape((n_tasks, weight.shape[1]), bf16),
+            shape((n_tasks, 3 * width), f32),
+            shape((tokens, 1), jnp.int32),
+        ]
+        + [shape(s, d) for s, d in kept]
+        + [shape((rows, HEADS, length, length), bf16), shape(probs, bf16)],
+        scratch_shapes=[pltpu.VMEM(a.shape, f32) for a in own]
+        + [pltpu.VMEM((2 * a.shape[0], a.shape[1] // 2), f32) for a in own]
+        + [pltpu.VMEM((2 * a.shape[0], a.shape[1] // 2), bf16) for a in own]
+        + [pltpu.VMEM(s, bf16) for s in chip[:8]]
+        + [pltpu.VMEM(s, d) for s, d in kept]
+        + [
+            pltpu.VMEM((n_tasks, 2 * made_half), f32),
+            pltpu.VMEM(gain.shape, f32),
+            pltpu.VMEM((length, max(length, mem_len)), f32),
+            pltpu.VMEM((2, 2, length, max(length, mem_len)), bf16),
+            pltpu.SemaphoreType.DMA((copies,)),
+            pltpu.SemaphoreType.DMA((copies,)),
+            pltpu.SemaphoreType.DMA((2,)),
+            pltpu.SemaphoreType.DMA((9,)),
+            pltpu.SemaphoreType.DMA((11,)),
+            pltpu.VMEM(spaces + (2,) + gain.shape, f32),
+        ],
+        compiler_params=pltpu.CompilerParams(
+            collective_id=0, has_side_effects=True, vmem_limit_bytes=VMEM_BYTES
+        ),
+        name="forward_as_weights_arrive",
+    )(x, mem, segments, mem_segments, tasks, *own, table, weight, bias_row, down, up, gain)
+    return outs
+
+
 def on_device(
     block_input, memory, cotangent, segments, memory_segments, task_of_segment,
     self_query, self_key, self_value, self_output,
@@ -863,40 +1138,53 @@
     )
     task_state, task_back = jax.vjp(task_network, task_table, task_weight, task_bias)
     task_low = task_state.astype(bf16)
-    made = inner_rows(task_low, jnp.concatenate((down_maker, up_maker, gain_maker), axis=0))
     down_own, gain_own = down_maker.shape[0], gain_maker.shape[0]
-    if parts == 32:
-        made = jnp.pad(made, ((0, 0), (0, -made.shape[1] % 256)))
-        *backbone, made = gather(weights, made)
-        backbone = [w.reshape(-1, w.shape[-1]) for w in backbone]
-        made = made.reshape((parts,) + made.shape[4:])
-    else:
-        backbone = [lax.all_gather(w, "dp", axis=0, tiled=True) for w in weights]
-        made = lax.all_gather(made, "dp", axis=0, tiled=False)
+    makers = (down_maker, up_maker, gain_maker)
+    x = block_input.reshape(token_count, model_width)
+    mem = memory.reshape(row_count * mem_len, model_width)
 
     def joined(block):
         return block.transpose(1, 0, 2).reshape(task_count, -1)
 
+    if parts == 32:
+        outs = forward(
+            x, mem, segments, memory_segments, task_of_segment, weights,
+            task_table, task_weight, task_bias.reshape(1, -1), makers,
+        )
+        backbone = [w.reshape(-1, w.shape[-1]) for w in outs[:10]]
+        made = outs[10].reshape(parts, task_count, -1)
+        task_low, gain_table, token_task = outs[12:15]
+        saved, probs_one, probs_two = outs[15:26], outs[26], outs[27]
+        made_up = joined(made[:, :, made.shape[2] // 2 :][:, :, :down_own]).astype(bf16)
+    else:
+        packed = jnp.concatenate([w.reshape(-1, model_width) for w in weights], axis=0)
+        packed = lax.all_gather(packed, "dp", axis=0, tiled=False)
+        backbone, at = [], 0
+        for w in weights:
+            count = w.size // model_width
+            backbone.append(packed[:, at : at + count].reshape(-1, w.shape[1]))
+            at += count
+        made = inner_rows(task_low, jnp.concatenate(makers, axis=0))
+        made = lax.all_gather(made, "dp", axis=0, tiled=False)
+        gain_table = 1.0 + joined(made[:, :, 2 * down_own :])
+        seg_match = segments[:, :, None] == jnp.arange(task_of_segment.shape[1], dtype=jnp.int32)
+        token_task = jnp.sum(
+            jnp.where(seg_match, task_of_segment[:, None, :], 0), axis=-1
+        ).reshape(token_count, 1)
+        saved, probs_one, probs_two = attention_layers(
+            x, mem, segments, memory_segments, token_task, backbone, gain_table
+        )
+        made_up = joined(made[:, :, down_own : 2 * down_own]).astype(bf16)
     made_down = joined(made[:, :, :down_own]).astype(bf16)
-    made_up = joined(made[:, :, down_own : 2 * down_own]).astype(bf16)
-    gain_table = 1.0 + joined(made[:, :, 2 * down_own : 2 * down_own + gain_own])
     down_all = (
         made_down.reshape(task_count, model_width, ADA)
         .transpose(1, 0, 2)
         .reshape(model_width, task_count * ADA)
     )
     up_all = made_up.reshape(task_count * ADA, model_width)
-    seg_match = (
-        segments[:, :, None] == jnp.arange(task_of_segment.shape[1], dtype=jnp.int32)[None, None, :]
-    )
-    token_task = jnp.sum(jnp.where(seg_match, task_of_segment[:, None, :], 0), axis=-1).reshape(
-        token_count, 1
-    )
-    output, input_grad, mem_grad, grads, up_all_grad, down_all_grad, gain_grad = layer(
-        block_input.reshape(token_count, model_width),
-        memory.reshape(row_count * mem_len, model_width),
-        cotangent.reshape(token_count, model_width),
-        segments, memory_segments, token_task, backbone, gain_table, down_all, up_all,
+    output, input_grad, mem_grad, grads, up_all_grad, down_all_grad, gain_grad = feed_and_back(
+        x, mem, cotangent.reshape(token_count, model_width), row_count, token_task,
+        backbone, gain_table, down_all, up_all, saved, probs_one, probs_two,
     )
     down_rows = (
         down_all_grad.reshape(parts, -1, task_count, ADA)
@@ -924,9 +1212,13 @@
         own_up = small[task_count:, :down_own].astype(bf16)
         own_gain = small[:task_count, down_own : down_own + gain_own]
     else:
-        shared = [
-            lax.psum_scatter(g, "dp", scatter_dimension=0, tiled=True).astype(f32) for g in grads
-        ]
+        packed = jnp.concatenate([g.reshape(parts, -1, model_width) for g in grads], axis=1)
+        packed = lax.psum_scatter(packed, "dp", scatter_dimension=0, tiled=False).astype(f32)
+        shared, at = [], 0
+        for w in weights:
+            count = w.size // model_width
+            shared.append(packed[at : at + count].reshape(w.shape))
+            at += count
         small = jnp.concatenate((down_rows, up_rows, gain_rows_all), axis=2)
         small = lax.psum_scatter(small, "dp", scatter_dimension=0, tiled=False)
         own_down = small[:, :down_own].astype(bf16)

time: 497 us -> 455 us (0.915)
  Pallas kernels: 447 us -> 416 us
  local copies, waits for them, and re-layouts: 31.7 us -> 22.2 us
    pallas_call x15 -> x10, Pallas kernels: 214 us -> 155 us  [call(): pl.pallas_call(kernel, grid=grid, in_specs=[pl.BlockSpec(b, m) for _, b,...]
    pallas_call x1, Pallas kernels: 108 us -> 137 us  [forward(): pl.pallas_call(forward_kernel, in_specs=[vmem] * 21, out_specs=[any_space...]
    unnamed x42 -> x40, local copies, waits for them, and re-layouts: 13.8 us -> 10.3 us
where the time goes in v4:
time: 455 us; the launch traced here: 449 us
  Pallas kernels  416 us (91%)
  local copies, waits for them, and re-layouts  22.2 us (5%)
  matrix products  6.65 us (1%)
    pallas_call x10, Pallas kernels, call(): pl.pallas_call(kernel, grid=grid, in_specs=[pl.BlockSpec(b, m) for _, b,...  155 us
    pallas_call x1, Pallas kernels, forward(): pl.pallas_call(forward_kernel, in_specs=[vmem] * 21, out_specs=[any_space...  137 us
    pallas_call x1, Pallas kernels, scatter(): pl.pallas_call(functools.partial(scatter_kernel, count, len(makers)), in_...  124 us
    unnamed x40, local copies, waits for them, and re-layouts  10.3 us

profile of v4, /device:TPU:0, one launch (start us, length us, event | category | flops | bytes accessed | tf_op | source)
XLA Modules:
  0.0 449.1 jit_solution(9922531252326201502)
XLA Ops:
  0.7 136.7 %forward_as_weights_arrive.1 = (bf16[4,2,2,48,768]{4,3,2,1,0:T(8,128)(2,1)}, bf16[4,2,2,48,768]{4,3,2,1,0:T(8,128)(2,1)}, bf16[4,2,2,48,768]{4,3,2,1,0:T(8,128)(...) custom-call(bf16[1024,768]{1,0:T(8,128)(2,1)} %bitcast.59, ...), custom_call_target="tpu_custom_call" | custom-call | tf_op jit(solution)/shard_map/forward_as_weights_arrive/pallas_call | solution.py:1084
  137.4 1.4 fusion.23
  138.8 1.4 convert.43
  140.3 1.2 convert_element_type.31.up_all
  141.5 1.3 convert_element_type.29
  143.4 0.9 copy.48.down_all
  144.3 47.0 %feed_forward_and_back.1 = (bf16[1024,768]{1,0:T(8,128)(2,1)}, bf16[1024,768]{1,0:T(8,128)(2,1)}, bf16[1024,3072]{1,0:T(8,128)(2,1)}, bf16[1024,3072]{1,0:T(8,12...) custom-call(f32[1024,768]{1,0:T(8,128)} %get-tuple-element.89.s1, ...), custom_call_target="tpu_custom_call" | custom-call | flops 21743271936 | bytes 42323968 | tf_op jit(solution)/shard_map/feed_forward_and_back/pallas_call | solution.py:93
  191.4 20.1 %attend_backward.2 = (bf16[1024,768]{1,0:T(8,128)(2,1)}, bf16[1024,768]{1,0:T(8,128)(2,1)}, bf16[1024,768]{1,0:T(8,128)(2,1)}) custom-call(bf16[1024,768]{1,0:T(8,128)(2,1)} %get-tuple-element.102.q_ref, bf16[1024,768]{1,0:T(8,128)(2,1)} %get-tuple-element.103.k_ref, bf16[1024,768]{1,0:T(8,128)(2,1)} %get-tuple-element.104.v_ref, ...), custom_call_target="tpu_custom_call" | custom-call | flops 6442450944 | bytes 25165824 | tf_op jit(solution)/shard_map/attend_backward/pallas_call | solution.py:93
  211.5 9.8 %cross_back.1 = (f32[1024,768]{1,0:T(8,128)}, bf16[1024,768]{1,0:T(8,128)(2,1)}, bf16[1024,768]{1,0:T(8,128)(2,1)}, f32[8,768]{1,0:T(8,128)}) custom-call(bf16[1024,768]{1,0:T(8,128)(2,1)} %get-tuple-element.107.gq.refs_4_, bf16[768,768]{1,0:T(8,128)(2,1)} %bitcast.76, f32[1024,768]{1,0:T(8,128)} %get-tuple-element.89.s1, s32[1024,1]{1,0:T(8,128)} %get-tuple-element.92.task, ...), custom_call_target="tpu_custom_call" | custom-call | flops 2415919104 | bytes 16568320 | tf_op jit(solution)/shard_map/cross_back/pallas_call | solution.py:93
  221.3 9.9 %cross_grads.1 = (bf16[768,768]{1,0:T(8,128)(2,1)}, bf16[768,768]{1,0:T(8,128)(2,1)}, bf16[768,768]{1,0:T(8,128)(2,1)}, bf16[768,768]{1,0:T(8,128)(2,1)}) custom-call(bf16[1024,768]{1,0:T(8,128)(2,1)} %get-tuple-element.90.mixed.mixed_ref.refs_0_, bf16[1024,768]{1,0:T(8,128)(2,1)} %get-tuple-element.131.refs_1_, bf16[1024,768]{1,0:T(8,128)(2,1)} %bitcast.66, ...), custom_call_target="tpu_custom_call" | custom-call | flops 4831838208 | bytes 15728640 | tf_op jit(solution)/shard_map/cross_grads/pallas_call | solution.py:93
  231.2 6.5 %memory_back.1 = f32[1024,768]{1,0:T(8,128)} custom-call(bf16[1024,768]{1,0:T(8,128)(2,1)} %get-tuple-element.121.gk.refs_5_, bf16[1024,768]{1,0:T(8,128)(2,1)} %get-tuple-element.122.gv.refs_6_, bf16[768,768]{1,0:T(8,128)(2,1)} %bitcast.88, bf16[768,768]{1,0:T(8,128)(2,1)} %bitcast.89), custom_call_target="tpu_custom_call" | custom-call | flops 2415919104 | bytes 8650752 | tf_op jit(solution)/shard_map/memory_back/pallas_call | solution.py:93
  237.7 18.3 %attend_backward.3 = (bf16[1024,768]{1,0:T(8,128)(2,1)}, bf16[1024,768]{1,0:T(8,128)(2,1)}, bf16[1024,768]{1,0:T(8,128)(2,1)}) custom-call(bf16[1024,768]{1,0:T(8,128)(2,1)} %get-tuple-element.98.q_ref, bf16[1024,768]{1,0:T(8,128)(2,1)} %get-tuple-element.99.k_ref, bf16[1024,768]{1,0:T(8,128)(2,1)} %get-tuple-element.100.v_ref, ...), custom_call_target="tpu_custom_call" | custom-call | flops 6442450944 | bytes 25165824 | tf_op jit(solution)/shard_map/attend_backward/pallas_call | solution.py:93
  256.0 11.1 %input_back.1 = (f32[1024,768]{1,0:T(8,128)}, f32[8,768]{1,0:T(8,128)}) custom-call(bf16[1024,768]{1,0:T(8,128)(2,1)} %get-tuple-element.113.gq.refs_3_, bf16[1024,768]{1,0:T(8,128)(2,1)} %get-tuple-element.114.gk.refs_4_, bf16[1024,768]{1,0:T(8,128)(2,1)} %get-tuple-element.115.gv.refs_5_, bf16[768,768]{1,0:T(8,128)(2,1)} %bitcast.68, ...), custom_call_target="tpu_custom_call" | custom-call | flops 3623878656 | bytes 16175104 | tf_op jit(solution)/shard_map/input_back/pallas_call | solution.py:93
  267.1 9.6 %self_grads.1 = (bf16[768,768]{1,0:T(8,128)(2,1)}, bf16[768,768]{1,0:T(8,128)(2,1)}, bf16[768,768]{1,0:T(8,128)(2,1)}, bf16[768,768]{1,0:T(8,128)(2,1)}) custom-call(bf16[1024,768]{1,0:T(8,128)(2,1)} %get-tuple-element.101.mixed_ref.refs_0_, bf16[1024,768]{1,0:T(8,128)(2,1)} %get-tuple-element.125.refs_1_, bf16[1024,768]{1,0:T(8,128)(2,1)} %get-tuple-element.126.refs_2_, ...), custom_call_target="tpu_custom_call" | custom-call | flops 4831838208 | bytes 14155776 | tf_op jit(solution)/shard_map/self_grads/pallas_call | solution.py:93
  278.0 2.5 reshape.185
  280.6 1.9 copy.50
  282.4 1.0 reshape.186
  283.6 0.9 fusion.1
  284.5 9.8 %hidden_in_grad.1 = bf16[768,3072]{1,0:T(8,128)(2,1)} custom-call(bf16[1024,768]{1,0:T(8,128)(2,1)} %get-tuple-element.137.refs_0_, bf16[1024,3072]{1,0:T(8,128)(2,1)} %get-tuple-element.138.refs_1_), custom_call_target="tpu_custom_call" | custom-call | flops 4831838208 | bytes 12582912 | tf_op jit(solution)/shard_map/hidden_in_grad/pallas_call | solution.py:93
  294.3 12.9 %hidden_out_grad.1 = bf16[3072,768]{1,0:T(8,128)(2,1)} custom-call(bf16[1024,3072]{1,0:T(8,128)(2,1)} %get-tuple-element.139.refs_0_, bf16[1024,768]{1,0:T(8,128)(2,1)} %get-tuple-element.140.refs_1_), custom_call_target="tpu_custom_call" | custom-call | flops 4831838208 | bytes 12582912 | tf_op jit(solution)/shard_map/hidden_out_grad/pallas_call | solution.py:93
  307.2 124.1 %scatter_gradients.1 = (f32[24,768]{1,0:T(8,128)}, f32[24,768]{1,0:T(8,128)}, f32[24,768]{1,0:T(8,128)}, f32[24,768]{1,0:T(8,128)}, f32[24,768]{1,0:T(8,128)}, /...) custom-call(bf16[4,2,2,48,768]{4,3,2,1,0:T(8,128)(2,1)} %bitcast.78,, ...), custom_call_target="tpu_custom_call" | custom-call | tf_op jit(solution)/shard_map/scatter_gradients/pallas_call | solution.py:734
  431.4 1.5 fusion.24
  432.9 0.8 fusion.25
  433.7 0.8 convert.42
  434.5 1.6 fusion.13
  436.1 0.8 convolution_bitcast_fusion
  436.9 1.0 fusion.5
  437.9 1.0 fusion.7
  438.9 1.5 copy.71
  440.4 1.5 copy.72
  441.9 1.5 copy.73
  443.4 1.5 copy.74
  (51 shorter events, 6.1 us)
Async XLA Ops:
  267.1 9.6 %copy-start.11 = (f32[8,768]{1,0:T(8,128)S(1)}, f32[8,768]{1,0:T(8,128)}, u32[]{:S(2)}) copy-start(f32[8,768]{1,0:T(8,128)} %get-tuple-element.142) | copy-start | bytes 73732
  267.1 9.6 %copy-start.10 = (f32[8,768]{1,0:T(8,128)S(1)}, f32[8,768]{1,0:T(8,128)}, u32[]{:S(2)}) copy-start(f32[8,768]{1,0:T(8,128)} %get-tuple-element.143) | copy-start | bytes 73732
  267.1 9.6 %copy-start.9 = (f32[8,768]{1,0:T(8,128)S(1)}, f32[8,768]{1,0:T(8,128)}, u32[]{:S(2)}) copy-start(f32[8,768]{1,0:T(8,128)} %get-tuple-element.144) | copy-start | bytes 73732
  267.1 9.8 %copy-start.1 = (f32[192,768]{1,0:T(8,128)S(1)}, f32[192,768]{1,0:T(8,128)}, u32[]{:S(2)}) copy-start(f32[192,768]{1,0:T(8,128)} %get-tuple-element.145) | copy-start | bytes 1769476
  276.7 1.1 copy-start
  307.2 124.2 %copy-start.4 = (f32[64,128]{1,0:T(8,128)S(1)}, f32[64,128]{1,0:T(8,128)}, u32[]{:S(2)}) copy-start(f32[64,128]{1,0:T(8,128)} %refs_16_.1) | copy-start | bytes 98308
  307.2 124.2 %copy-start.13 = (f32[8,64]{1,0:T(8,128)S(1)}, f32[8,64]{1,0:T(8,128)}, u32[]{:S(2)}) copy-start(f32[8,64]{1,0:T(8,128)} %refs_15_.1) | copy-start | bytes 6148
  307.2 124.2 %copy-start.14 = (f32[128]{0:T(128)S(1)}, f32[128]{0:T(128)}, u32[]{:S(2)}) copy-start(f32[128]{0:T(128)} %param.40) | copy-start | bytes 1540
  307.2 127.3 %copy-start.12 = (bf16[8,128]{1,0:T(8,128)(2,1)S(1)}, bf16[8,128]{1,0:T(8,128)(2,1)}, u32[]{:S(2)}) copy-start(bf16[8,128]{1,0:T(8,128)(2,1)} %get-tuple-element.158) | copy-start | bytes 6148
  431.3 13.6 %copy-start.8 = (f32[24,768]{1,0:T(8,128)S(1)}, f32[24,768]{1,0:T(8,128)}, u32[]{:S(2)}) copy-start(f32[24,768]{1,0:T(8,128)} %get-tuple-element.194) | copy-start | bytes 221188
  431.3 14.3 %copy-start.7 = (f32[24,768]{1,0:T(8,128)S(1)}, f32[24,768]{1,0:T(8,128)}, u32[]{:S(2)}) copy-start(f32[24,768]{1,0:T(8,128)} %get-tuple-element.195) | copy-start | bytes 221188
  431.4 14.9 %copy-start.6 = (f32[24,768]{1,0:T(8,128)S(1)}, f32[24,768]{1,0:T(8,128)}, u32[]{:S(2)}) copy-start(f32[24,768]{1,0:T(8,128)} %get-tuple-element.196) | copy-start | bytes 221188
  431.4 15.5 %copy-start.5 = (f32[24,768]{1,0:T(8,128)S(1)}, f32[24,768]{1,0:T(8,128)}, u32[]{:S(2)}) copy-start(f32[24,768]{1,0:T(8,128)} %get-tuple-element.197) | copy-start | bytes 221188
  431.4 16.1 %copy-start.3 = (f32[24,3072]{1,0:T(8,128)S(1)}, f32[24,3072]{1,0:T(8,128)}, u32[]{:S(2)}) copy-start(f32[24,3072]{1,0:T(8,128)} %get-tuple-element.198) | copy-start | bytes 884740
  431.4 16.8 %copy-start.2 = (f32[96,768]{1,0:T(8,128)S(1)}, f32[96,768]{1,0:T(8,128)}, u32[]{:S(2)}) copy-start(f32[96,768]{1,0:T(8,128)} %get-tuple-element.199) | copy-start | bytes 884740

commit v5 on v4

--- a/solution.py
+++ b/solution.py
@@ -441,12 +441,10 @@
     return (n1, q1, k1, v1, m1, s1, n2, q2, k2, v2, m2), p1, p2
 
 
-def feed_and_back(x, mem, cot, rows, task, weights, gain_table, down_all, up_all, saved, p1, p2):
-    n1, q1, k1, v1, m1, s1, n2, q2, k2, v2, m2 = saved
-    tokens, width = x.shape
-    length = tokens // rows
-    wq1, wk1, wv1, wo1, wq2, wk2, wv2, wo2, w_in, w_out = weights
-    gain_one, gain_two, gain_three = (gain_table[:, i * width : (i + 1) * width] for i in range(3))
+def feed_forward(s1, m2, cot, task, weights, gain_table, down_all, up_all):
+    tokens, width = s1.shape
+    wo2, w_in, w_out = weights[7:]
+    gain_three = gain_table[:, 2 * width :]
     block = BLOCK
     grid = (tokens // block,)
     act_shape = (tokens, width)
@@ -472,6 +470,20 @@
     )
     (hidden_in_grad,) = outers((n3,), (gu,), (0,), "hidden_in_grad")
     (hidden_out_grad,) = outers((act,), (gfeed,), (0,), "hidden_out_grad")
+    return output, g2, g2_low, gmix2, hidden_in_grad, hidden_out_grad, up_grad, down_grad, gain3
+
+
+def attention_back(x, mem, rows, task, weights, gain_table, saved, p1, p2, g2, g2_low, gmix2):
+    n1, q1, k1, v1, m1, s1, n2, q2, k2, v2, m2 = saved
+    tokens, width = x.shape
+    length = tokens // rows
+    wq1, wk1, wv1, wo1, wq2, wk2, wv2 = weights[:7]
+    gain_one, gain_two = (gain_table[:, i * width : (i + 1) * width] for i in range(2))
+    tasks = gain_table.shape[0]
+    block = BLOCK
+    grid = (tokens // block,)
+    act_shape = (tokens, width)
+    square = 2 * tokens * width * width
     gq2, gk2, gv2 = attend_backward(False, rows, length, q2, k2, v2, m2, gmix2, p2)
     g1, g1_low, gmix1, gain2 = call(
         cross_back_kernel,
@@ -510,12 +522,8 @@
     wo1_grad, wq1_grad, wk1_grad, wv1_grad = outers(
         (m1, n1), (g1_low, gq1, gk1, gv1), (0, 1, 1, 1), "self_grads"
     )
-    gain_grad = jnp.concatenate((gain1, gain2, gain3), axis=1)
-    grads = (
-        wq1_grad, wk1_grad, wv1_grad, wo1_grad, wq2_grad, wk2_grad, wv2_grad, wo2_grad,
-        hidden_in_grad, hidden_out_grad,
-    )
-    return output, input_grad, mem_grad, grads, up_grad, down_grad, gain_grad
+    grads = (wq1_grad, wk1_grad, wv1_grad, wo1_grad, wq2_grad, wk2_grad, wv2_grad, wo2_grad)
+    return input_grad, mem_grad, grads, gain1, gain2
 
 
 LINE = 4
@@ -585,164 +593,13 @@
         copy.start()
         return copy
 
+    def close(self, copy):
+        copy.wait_send()
+        self.open = [other for other in self.open if other is not copy]
+
     def finish(self):
         for copy in self.open:
             copy.wait_send()
-
-
-def shares(rows, turn):
-    cut = rows // 2 if rows % 32 == 0 else (rows // 32 + turn % 2) * 16
-    return slice(0, cut), slice(cut, rows)
-
-
-def stepped(count, stages):
-    for turn in range(count + len(stages) - 1):
-        for late, stage in enumerate(stages):
-            if 0 <= turn - late < count:
-                stage(turn - late)
-
-
-def scatter_kernel(count, makers, *refs):
-    grads, maker_refs = refs[:count], refs[count : count + makers]
-    outs, state_out = refs[count + makers : 2 * count + makers], refs[2 * count + makers]
-    scratch = refs[2 * count + makers + 1 :]
-    held, from_core, from_a, from_b, from_c, from_d, from_z, final = (
-        scratch[k * count : (k + 1) * count] for k in range(8)
-    )
-    totals, arriving, send, recv = scratch[8 * count :]
-    here = Place()
-    copies = Copies(send, recv)
-    z, y, x, c = here.z, here.y, here.x, here.core
-    local, core, one, two, three, last = {}, {}, {}, {}, {}, {}
-
-    def half(i, which):
-        width = grads[i].shape[-1] // 2
-        return pl.ds(pl.multiple_of(which * width, 128), width)
-
-    for i in range(count):
-        local[i] = copies.local(grads[i].at[:, :, :, :, half(i, c)], held[i])
-    meet(here)
-    for i in range(count):
-        core[i] = copies.remote(
-            grads[i].at[:, :, :, :, half(i, 1 - c)], from_core[i], here.sibling()
-        )
-
-    def cuts(i):
-        return shares(grads[i].shape[3], i)
-
-    def over_first(i):
-        local[i].wait()
-        core[i].wait_recv()
-        held[i][...] += from_core[i][...]
-        first, second = cuts(i)
-        one[i] = (
-            copies.remote(held[i].at[:, 1 - y, :, first, :], from_a[i], here.over_y()),
-            copies.remote(held[i].at[:, :, 1 - x, second, :], from_b[i], here.over_x()),
-        )
-
-    def over_second(i):
-        first, second = cuts(i)
-        one[i][0].wait_recv()
-        held[i][:, y, :, first, :] += from_a[i][...]
-        one[i][1].wait_recv()
-        held[i][:, :, x, second, :] += from_b[i][...]
-        two[i] = (
-            copies.remote(held[i].at[:, y, 1 - x, first, :], from_c[i], here.over_x()),
-            copies.remote(held[i].at[:, 1 - y, x, second, :], from_d[i], here.over_y()),
-        )
-
-    def over_line(i):
-        first, second = cuts(i)
-        two[i][0].wait_recv()
-        held[i][:, y, x, first, :] += from_c[i][...]
-        two[i][1].wait_recv()
-        held[i][:, y, x, second, :] += from_d[i][...]
-        three[i] = [
-            copies.remote(
-                held[i].at[lax.rem(z + k, LINE), y, x], from_z[i].at[k - 1], here.along_z(k)
-            )
-            for k in (1, 2, 3)
-        ]
-
-    def to_owner(i):
-        total = held[i][z, y, x].astype(f32)
-        for k, copy in enumerate(three[i]):
-            copy.wait_recv()
-            total = total + from_z[i][k].astype(f32)
-        final[i][...] = total
-        rows = outs[i].shape[0]
-        theirs = pl.ds(pl.multiple_of((1 - c) * rows, 8), rows)
-        last[i] = copies.remote(
-            final[i].at[theirs, :], outs[i].at[:, half(i, c)], here.sibling()
-        )
-        outs[i][:, half(i, c)] = final[i][pl.ds(pl.multiple_of(c * rows, 8), rows), :]
-
-    stepped(count, (over_first, over_second, over_line, to_owner))
-    last[count - 1].wait_recv()
-    down, up, gain = maker_refs
-    small = outs[count - 1]
-    made = down.shape[0]
-    gains = gain.shape[0]
-    state = plain_dot(small[0:8, :made].astype(bf16), down[...])
-    state = state + plain_dot(small[8:16, :made].astype(bf16), up[...])
-    state = state + exact_dot(small[0:8, made : made + gains], gain[...].astype(f32))
-    for turn, device in enumerate((here.sibling(), here.over_x(), here.over_y())):
-        totals[turn] = state
-        copy = copies.remote(totals.at[turn], arriving.at[turn], device)
-        copy.wait_recv()
-        state = state + arriving[turn]
-    totals[3] = state
-    around = [copies.remote(totals.at[3], arriving.at[2 + k], here.along_z(k)) for k in (1, 2, 3)]
-    terms = {}
-    for k, copy in enumerate(around):
-        copy.wait_recv()
-    total = jnp.zeros_like(state)
-    for line in range(LINE):
-        for k in range(LINE):
-            term = state if k == 0 else arriving[2 + k]
-            total = total + jnp.where(lax.rem(z - k + LINE, LINE) == line, term, 0.0)
-    state_out[...] = total
-    for i in range(count - 1):
-        last[i].wait_recv()
-    copies.finish()
-
-
-def scatter(grads, makers):
-    count = len(grads)
-    copies = 12 * count + 8
-    any_space = pl.BlockSpec(memory_space=pl.ANY)
-    vmem = pl.BlockSpec(memory_space=pltpu.VMEM)
-
-    def slots(shape_of):
-        return [pltpu.VMEM(shape_of(g, i), bf16) for i, g in enumerate(grads)]
-
-    def rows_of(g, i, which):
-        cut = shares(g.shape[3], i)[which]
-        return cut.stop - cut.start
-
-    scratch = slots(lambda g, i: g.shape[:4] + (g.shape[4] // 2,)) * 1
-    scratch += slots(lambda g, i: g.shape[:4] + (g.shape[4] // 2,))
-    scratch += slots(lambda g, i: (LINE, 2, rows_of(g, i, 0), g.shape[4] // 2))
-    scratch += slots(lambda g, i: (LINE, 2, rows_of(g, i, 1), g.shape[4] // 2))
-    scratch += slots(lambda g, i: (LINE, rows_of(g, i, 0), g.shape[4] // 2))
-    scratch += slots(lambda g, i: (LINE, rows_of(g, i, 1), g.shape[4] // 2))
-    scratch += slots(lambda g, i: (LINE - 1, g.shape[3], g.shape[4] // 2))
-    scratch += [pltpu.VMEM((g.shape[3], g.shape[4] // 2), f32) for g in grads]
-    tasks, hidden = 8, makers[0].shape[1]
-    scratch += [pltpu.VMEM((4, tasks, hidden), f32), pltpu.VMEM((6, tasks, hidden), f32)]
-    scratch += [pltpu.SemaphoreType.DMA((copies,)), pltpu.SemaphoreType.DMA((copies,))]
-    return pl.pallas_call(
-        functools.partial(scatter_kernel, count, len(makers)),
-        in_specs=[any_space] * count + [vmem] * len(makers),
-        out_specs=[vmem] * (count + 1),
-        out_shape=[jax.ShapeDtypeStruct((g.shape[3] // 2, g.shape[4]), f32) for g in grads]
-        + [jax.ShapeDtypeStruct((tasks, hidden), f32)],
-        scratch_shapes=scratch,
-        compiler_params=pltpu.CompilerParams(
-            collective_id=1, has_side_effects=True, vmem_limit_bytes=60 << 20
-        ),
-        name="scatter_gradients",
-    )(*grads, *makers)
 
 
 class Unit:
@@ -1120,6 +977,555 @@
     return outs
 
 
+class Stepwise:
+    def __init__(self, stages):
+        self.stages = list(stages)
+
+    def advance(self):
+        self.stages.pop(0)()
+
+
+class Traffic:
+    def __init__(self):
+        self.ready, self.flying = [], []
+
+    def add(self, item):
+        self.ready.append(item)
+
+    def tick(self):
+        for item in list(self.flying):
+            item.advance()
+            if not item.stages:
+                self.flying.remove(item)
+        if self.ready:
+            item = self.ready.pop(0)
+            item.advance()
+            self.flying.append(item)
+
+    def drain(self):
+        while self.ready or self.flying:
+            self.tick()
+
+
+class Summed(Stepwise):
+    def __init__(self, here, copies, theirs, mine, shares, slots, out, out_first, fetch=None):
+        super().__init__(
+            [self.begin, self.over_first, self.over_second, self.over_line, self.to_owner, self.end]
+        )
+        self.here, self.copies = here, copies
+        self.theirs, self.mine, self.fetch = theirs, mine, fetch
+        self.shares, self.slots, self.out, self.out_first = shares, slots, out, out_first
+        self.landed = None
+
+    def begin(self):
+        self.core = self.copies.remote(self.theirs, self.slots[0], self.here.sibling())
+        if self.fetch is not None:
+            self.local = self.copies.local(*self.fetch)
+
+    def over_first(self):
+        here, held = self.here, self.slots[0]
+        if self.fetch is not None:
+            self.local.wait()
+        self.core.wait_recv()
+        held[...] += self.mine()
+        one, two = self.shares
+        self.first = (
+            self.copies.remote(held.at[(slice(None), 1 - here.y, slice(None)) + one], self.slots[1], here.over_y()),
+            self.copies.remote(held.at[(slice(None), slice(None), 1 - here.x) + two], self.slots[2], here.over_x()),
+        )
+
+    def over_second(self):
+        here, held = self.here, self.slots[0]
+        one, two = self.shares
+        self.first[0].wait_recv()
+        held[(slice(None), here.y, slice(None)) + one] += self.slots[1][...]
+        self.first[1].wait_recv()
+        held[(slice(None), slice(None), here.x) + two] += self.slots[2][...]
+        self.second = (
+            self.copies.remote(held.at[(slice(None), here.y, 1 - here.x) + one], self.slots[3], here.over_x()),
+            self.copies.remote(held.at[(slice(None), 1 - here.y, here.x) + two], self.slots[4], here.over_y()),
+        )
+
+    def over_line(self):
+        here, held = self.here, self.slots[0]
+        one, two = self.shares
+        self.second[0].wait_recv()
+        held[(slice(None), here.y, here.x) + one] += self.slots[3][...]
+        self.second[1].wait_recv()
+        held[(slice(None), here.y, here.x) + two] += self.slots[4][...]
+        self.third = [
+            self.copies.remote(
+                held.at[lax.rem(here.z + k, LINE), here.y, here.x],
+                self.slots[5].at[k - 1],
+                here.along_z(k),
+            )
+            for k in (1, 2, 3)
+        ]
+
+    def window(self, core, width, full):
+        return pl.ds(pl.multiple_of(core * full + self.out_first, 128), width)
+
+    def to_owner(self):
+        here, held, final = self.here, self.slots[0], self.slots[6]
+        total = held[here.z, here.y, here.x].astype(f32)
+        for k, copy in enumerate(self.third):
+            copy.wait_recv()
+            total = total + self.slots[5][k].astype(f32)
+        final[...] = total
+        rows, full = self.out.shape[0], self.out.shape[1] // 2
+        c = here.core
+        at = self.window(c, final.shape[1], full)
+        theirs = pl.ds(pl.multiple_of((1 - c) * rows, 8), rows)
+        self.last = self.copies.remote(final.at[theirs, :], self.out.at[:, at], here.sibling())
+        self.out[:, at] = final[pl.ds(pl.multiple_of(c * rows, 8), rows), :]
+
+    def end(self):
+        self.last.wait_recv()
+        if self.landed is not None:
+            self.landed()
+
+
+class Everywhere(Stepwise):
+    def __init__(self, here, copies, value, sent, arriving, out):
+        super().__init__([self.begin, self.step_x, self.step_y, self.step_z, self.end])
+        self.here, self.copies, self.value = here, copies, value
+        self.sent, self.arriving, self.out = sent, arriving, out
+
+    def send(self, turn, device):
+        self.sent[turn] = self.total
+        self.copy = self.copies.remote(self.sent.at[turn], self.arriving.at[turn], device)
+
+    def add(self, turn):
+        self.copy.wait_recv()
+        self.total = self.total + self.arriving[turn]
+
+    def begin(self):
+        self.total = self.value()
+        self.send(0, self.here.sibling())
+
+    def step_x(self):
+        self.add(0)
+        self.send(1, self.here.over_x())
+
+    def step_y(self):
+        self.add(1)
+        self.send(2, self.here.over_y())
+
+    def step_z(self):
+        self.add(2)
+        self.sent[3] = self.total
+        self.around = [
+            self.copies.remote(self.sent.at[3], self.arriving.at[2 + k], self.here.along_z(k))
+            for k in (1, 2, 3)
+        ]
+
+    def end(self):
+        for copy in self.around:
+            copy.wait_recv()
+        total = jnp.zeros_like(self.total)
+        for line in range(LINE):
+            for k in range(LINE):
+                term = self.total if k == 0 else self.arriving[2 + k]
+                here_now = lax.rem(self.here.z - k + LINE, LINE) == line
+                total = total + jnp.where(here_now, term, 0.0)
+        self.out[...] = total
+
+
+def attend_pair_back(causal, q_ref, k_ref, v_ref, mixed_ref, gm_ref, p_ref, gq_ref, gk_ref, gv_ref, start, k_start, at, length, keys_all):
+    step = length // 2 if causal else length
+    masks = half_masks()
+    gk_parts, gv_parts = [], []
+    for first in range(0, length, step):
+        rows = pl.ds(start + first, step)
+        keys = first + step if causal else keys_all
+        key_rows = pl.ds(k_start, keys)
+        q, k, v = q_ref[rows, at], k_ref[key_rows, at], v_ref[key_rows, at]
+        gm = gm_ref[rows, at]
+        product = gm.astype(f32) * mixed_ref[rows, at].astype(f32)
+        gq = gk = gv = 0.0
+        for h, mask in enumerate(masks):
+            inner = jnp.sum(product * mask.astype(f32), axis=-1, keepdims=True)
+            p = p_ref[h, first : first + step, :keys]
+            gm_half = gm * mask
+            gw = inner_rows(gm_half, v)
+            gs = (p.astype(f32) * (gw - inner)).astype(bf16)
+            gv = gv + inner_cols(p, gm_half)
+            gq = gq + plain_dot(gs, k * mask)
+            gk = gk + inner_cols(gs, q * mask)
+        gq_ref[rows, at] = (gq * HEAD**-0.5).astype(bf16)
+        gk_parts.append(gk)
+        gv_parts.append(gv)
+    for ref, terms in ((gk_ref, gk_parts), (gv_ref, gv_parts)):
+        if not causal:
+            ref[pl.ds(k_start, keys_all), at] = terms[0].astype(bf16)
+        else:
+            ref[pl.ds(k_start, step), at] = (terms[0] + terms[1][:step]).astype(bf16)
+            ref[pl.ds(k_start + step, step), at] = terms[1][step:].astype(bf16)
+
+
+SUM_NAMES = ("q1", "k1", "v1", "o1", "q2", "k2", "v2", "o2", "in0", "in1", "out0", "out1", "small")
+
+
+def sum_pieces(width, units, own):
+    rows = 2 * own
+    half = width // 2
+    pieces = {}
+    for turn, name in enumerate(SUM_NAMES[:8]):
+        cut = rows // 2 if rows % 32 == 0 else (rows // 32 + turn % 2) * 16
+        pieces[name] = (rows, half, 0, (slice(0, cut), slice(0, half)), (slice(cut, rows), slice(0, half)))
+    part = units // 4
+    for k in (0, 1):
+        pieces[f"in{k}"] = (
+            rows, part, k * part,
+            (slice(0, rows), slice(0, part // 2)), (slice(0, rows), slice(part // 2, part)),
+        )
+    out_rows = rows * units // width
+    third = half // 3
+    for k, (first, size) in enumerate(((0, third), (third, half - third))):
+        pieces[f"out{k}"] = (
+            out_rows, size, first,
+            (slice(0, out_rows // 2), slice(0, size)), (slice(out_rows // 2, out_rows), slice(0, size)),
+        )
+    pieces["small"] = (32, half, 0, (slice(0, 16), slice(0, half)), (slice(16, 32), slice(0, half)))
+    return pieces
+
+
+def backward_kernel(sizes, *refs):
+    rows_total, length, mem_len, width, units, own_rows = sizes
+    pieces = sum_pieces(width, units, own_rows)
+    (
+        p1, p2, q2h, k2h, v2h, m2h, gm2h, q1h, k1h, v1h, m1h, n1h, n2h, memh, xh, s1h, g2h, g2lowh,
+        wq1h, wk1h, wv1h, wo1h, wq2h, wk2h, wv2h, g_in, g_out, g_small,
+        task, gains, gain_three, down, up,
+    ) = refs[:33]
+    mem_out, input_out = refs[33:35]
+    outs = refs[35:46]
+    gain_out, state_out = refs[46:48]
+    scratch = refs[48:]
+    a = scratch[:5]
+    gq, gk, gv = scratch[5:8]
+    f0, f1, low = scratch[8:11]
+    probs = scratch[11]
+    w = scratch[12:16]
+    grads = scratch[16:20]
+    stage_in, stage_out, stage_small = scratch[20:23]
+    slots = {}
+    at_slot = 23
+    for name in SUM_NAMES:
+        slots[name] = scratch[at_slot : at_slot + 7]
+        at_slot += 7
+    state_sent, state_arriving, gain_sent, gain_arriving, gain_rows_ref = scratch[at_slot : at_slot + 5]
+    send, recv, p_sem, load_sem = scratch[at_slot + 5 :]
+    here = Place()
+    copies = Copies(send, recv)
+    traffic = Traffic()
+    c = here.core
+    loads = {}
+
+    def fetch(name, source, target):
+        loads[name] = pltpu.make_async_copy(source, target, load_sem.at[len(loads)])
+        loads[name].start()
+
+    def need(*names):
+        for name in names:
+            loads[name].wait()
+
+    def half(which, first, size, full):
+        return pl.ds(pl.multiple_of(which * full + first, 128), size)
+
+    fetch("m2", m2h, a[3])
+    fetch("g2low", g2lowh, low)
+    fetch("q2", q2h, a[0])
+    fetch("k2", k2h, a[1])
+    fetch("v2", v2h, a[2])
+    fetch("gm2", gm2h, a[4])
+
+    def probs_copy(source, index):
+        return pltpu.make_async_copy(source.at[index], probs.at[lax.rem(index, 2)], p_sem.at[lax.rem(index, 2)])
+
+    pairs = HEADS // 2
+    count = rows_total * pairs
+    for index in (0, 1):
+        probs_copy(p2, index).start()
+    fetch("wq2", wq2h, w[0])
+    fetch("wo1", wo1h, w[1])
+    fetch("wk2", wk2h, w[2])
+    fetch("wv2", wv2h, w[3])
+    fetch("s1", s1h, f0)
+    fetch("g2", g2h, f1)
+    meet(here)
+
+    def from_hbm(name, array, out, stage):
+        rows, size, first, one, two = pieces[name]
+        full = array.shape[4] // 2
+        return Summed(
+            here, copies, array.at[:, :, :, :, half(1 - c, first, size, full)], lambda: stage[...],
+            (one, two), slots[name], out, first,
+            fetch=(array.at[:, :, :, :, half(c, first, size, full)], stage),
+        )
+
+    for item in (
+        from_hbm("out0", g_out, outs[9], stage_out.at[:, :, :, :, : pieces["out0"][1]]),
+        from_hbm("out1", g_out, outs[9], stage_out),
+        from_hbm("small", g_small, outs[10], stage_small),
+        from_hbm("in0", g_in, outs[8], stage_in),
+        from_hbm("in1", g_in, outs[8], stage_in),
+    ):
+        traffic.add(item)
+        if item.out is outs[10]:
+            small_item = item
+
+    def small_landed():
+        made = down.shape[0]
+        small = outs[10]
+        state = plain_dot(small[0:8, :made].astype(bf16), down[...])
+        state = state + plain_dot(small[8:16, :made].astype(bf16), up[...])
+        traffic.add(Everywhere(here, copies, lambda: state, state_sent, state_arriving, state_out))
+
+    small_item.landed = small_landed
+    users = {}
+
+    def weight_gradient(name, index, source, grad, slot):
+        if slot in users:
+            copies.close(users[slot].core)
+        buffer = grads[slot]
+        rows, size, first, one, two = pieces[name]
+        columns = width // 2
+        for k in range(2):
+            block = inner_cols(source[:, k * columns : (k + 1) * columns], grad[...]).astype(bf16)
+            buffer[2 * k : 2 * k + 2] = block.reshape((2, 2, 2, rows, width))
+        full = width // 2
+        item = Summed(
+            here, copies, buffer.at[:, :, :, :, half(1 - c, 0, size, full)],
+            lambda: buffer[:, :, :, :, half(c, 0, size, full)],
+            (one, two), slots[name], outs[index], 0,
+        )
+        users[slot] = item
+        traffic.add(item)
+
+    def matrix(k):
+        return w[k][...].reshape(width, width)
+
+    def row(r, size=None):
+        size = length if size is None else size
+        return slice(r * size, (r + 1) * size)
+
+    def picked(r, which):
+        return token_gain(task[row(r), :], gains[:, which * width : (which + 1) * width])
+
+    def attention(causal, q, k, v, m, gm, source, keys_all):
+        per_group = 2
+        for group in range(count // per_group):
+            @pl.loop(group * per_group, (group + 1) * per_group)
+            def _(index):
+                slot = lax.rem(index, 2)
+                probs_copy(source, index).wait()
+                r, p = index // pairs, lax.rem(index, pairs)
+                at = pl.ds(pl.multiple_of(p * PAIR, PAIR), PAIR)
+                attend_pair_back(
+                    causal, q, k, v, m, gm, probs.at[slot], gq, gk, gv,
+                    pl.multiple_of(r * length, length), pl.multiple_of(r * keys_all, keys_all), at, length, keys_all,
+                )
+
+                @pl.when(index + 2 < count)
+                def _():
+                    probs_copy(source, index + 2).start()
+
+            traffic.tick()
+
+    traffic.tick()
+    need("m2", "g2low")
+    weight_gradient("o2", 7, a[3], low, 0)
+    traffic.tick()
+    need("q2", "k2", "v2", "gm2")
+    attention(False, a[0], a[1], a[2], a[3], a[4], p2, mem_len)
+    for index in (0, 1):
+        probs_copy(p1, index).start()
+    fetch("n2", n2h, a[0])
+    fetch("mem", memh, a[1])
+    fetch("v1", v1h, a[2])
+    fetch("m1", m1h, a[3])
+    need("wq2", "wo1", "s1", "g2")
+    gain_two = None
+    for r in range(rows_total):
+        stream = f0[row(r), :]
+        stream_grad, gain_tokens = norm_back(stream, picked(r, 1), inner_rows(gq[row(r), :], matrix(0)))
+        grad_one = f1[row(r), :] + stream_grad
+        f1[row(r), :] = grad_one
+        low_now = grad_one.astype(bf16)
+        low[row(r), :] = low_now
+        a[4][row(r), :] = inner_rows(low_now, matrix(1)).astype(bf16)
+        now = gain_rows(task[row(r), :], gain_tokens)
+        gain_two = now if gain_two is None else gain_two + now
+        traffic.tick()
+    fetch("wq1", wq1h, w[0])
+    fetch("wk1", wk1h, w[1])
+    need("n2", "mem")
+    for name, index, source, grad, slot in (
+        ("q2", 4, a[0], gq, 1), ("k2", 5, a[1], gk, 2), ("v2", 6, a[1], gv, 3)
+    ):
+        weight_gradient(name, index, source, grad, slot)
+        traffic.tick()
+    fetch("q1", q1h, a[0])
+    fetch("k1", k1h, a[1])
+    need("wk2", "wv2")
+    for r in range(rows_total):
+        mine = row(r, mem_len)
+        f0[mine, :] = inner_rows(gk[mine, :], matrix(2)) + inner_rows(gv[mine, :], matrix(3))
+        traffic.tick()
+    fetch("mem_out", f0, mem_out)
+    fetch("wv1", wv1h, w[2])
+    need("m1")
+    weight_gradient("o1", 3, a[3], low, 0)
+    traffic.tick()
+    need("q1", "k1", "v1")
+    attention(True, a[0], a[1], a[2], a[3], a[4], p1, length)
+    fetch("n1", n1h, a[0])
+    fetch("x", xh, a[1])
+    need("n1")
+    for name, index, grad, slot in (("q1", 0, gq, 1), ("k1", 1, gk, 2), ("v1", 2, gv, 3)):
+        weight_gradient(name, index, a[0], grad, slot)
+        traffic.tick()
+    need("x", "wq1", "wk1", "wv1")
+    gain_one = None
+    for r in range(rows_total):
+        stream = a[1][row(r), :].astype(f32)
+        cotan = inner_rows(gq[row(r), :], matrix(0)) + inner_rows(gk[row(r), :], matrix(1))
+        cotan = cotan + inner_rows(gv[row(r), :], matrix(2))
+        stream_grad, gain_tokens = norm_back(stream, picked(r, 0), cotan)
+        f1[row(r), :] += stream_grad
+        now = gain_rows(task[row(r), :], gain_tokens)
+        gain_one = now if gain_one is None else gain_one + now
+        traffic.tick()
+    fetch("input_out", f1, input_out)
+    gain_rows_ref[:, :width] = gain_one
+    gain_rows_ref[:, width : 2 * width] = gain_two
+    gain_rows_ref[:, 2 * width :] = gain_three[...]
+    traffic.ready.insert(0, Everywhere(here, copies, lambda: gain_rows_ref[...], gain_sent, gain_arriving, gain_out))
+    traffic.drain()
+    need("mem_out", "input_out")
+    copies.finish()
+
+
+def backward(mem_len, saved, probs, x, mem, weights, g2, g2_low, gmix2, g_in, g_out, g_small, task, gains, gain_three, down, up, own):
+    n1, q1, k1, v1, m1, s1, n2, q2, k2, v2, m2 = saved
+    p1, p2 = (p.reshape((-1, 2) + p.shape[2:]) for p in probs)
+    rows = probs[0].shape[0]
+    tokens, width = x.shape
+    length = tokens // rows
+    units = own[8].shape[1]
+    own_rows = own[0].shape[0]
+    any_space = pl.BlockSpec(memory_space=pl.ANY)
+    vmem = pl.BlockSpec(memory_space=pltpu.VMEM)
+    shape = jax.ShapeDtypeStruct
+    act, full = pltpu.VMEM((tokens, width), bf16), pltpu.VMEM((tokens, width), f32)
+    mem_act = pltpu.VMEM((max(tokens, mem.shape[0]), width), bf16)
+    square = pltpu.VMEM((LINE, 2, 2, 2 * own_rows, width), bf16)
+    pieces = sum_pieces(width, units, own_rows)
+    slots = []
+    for name in SUM_NAMES:
+        r, size, _, one, two = pieces[name]
+        extent = [tuple(s.stop - s.start for s in share) for share in (one, two)]
+        slots += [
+            pltpu.VMEM((LINE, 2, 2, r, size), bf16),
+            pltpu.VMEM((LINE, 2) + extent[0], bf16),
+            pltpu.VMEM((LINE, 2) + extent[1], bf16),
+            pltpu.VMEM((LINE,) + extent[0], bf16),
+            pltpu.VMEM((LINE,) + extent[1], bf16),
+            pltpu.VMEM((LINE - 1, r, size), bf16),
+            pltpu.VMEM((r, size), f32),
+        ]
+
+    def stage(name):
+        r, size = pieces[name][:2]
+        return (LINE, 2, 2, r, size)
+
+    tasks, hidden = gains.shape[0], down.shape[1]
+    copies = 200
+    ins_any = (
+        p1, p2, q2, k2, v2, m2, gmix2, q1, k1, v1, m1, n1, n2, mem, x, s1, g2, g2_low,
+        *(weights[i] for i in range(7)), g_in, g_out, g_small,
+    )
+    return pl.pallas_call(
+        functools.partial(backward_kernel, (rows, length, mem_len, width, units, own_rows)),
+        in_specs=[any_space] * len(ins_any) + [vmem] * 5,
+        out_specs=[any_space] * 2 + [vmem] * 13,
+        out_shape=[shape((mem.shape[0], width), f32), shape((tokens, width), f32)]
+        + [shape(g.shape, f32) for g in own]
+        + [shape((16, width), f32), shape(gains.shape, f32), shape((tasks, hidden), f32)],
+        scratch_shapes=[act] * 5 + [act, mem_act, mem_act] + [full, full, act]
+        + [pltpu.VMEM((2, 2, length, max(length, mem_len)), bf16)]
+        + [square] * 4
+        + [square] * 4
+        + [
+            pltpu.VMEM(stage("in0"), bf16),
+            pltpu.VMEM(stage("out1"), bf16),
+            pltpu.VMEM(stage("small"), bf16),
+        ]
+        + slots
+        + [
+            pltpu.VMEM((4, tasks, hidden), f32),
+            pltpu.VMEM((6, tasks, hidden), f32),
+            pltpu.VMEM((4,) + gains.shape, f32),
+            pltpu.VMEM((6,) + gains.shape, f32),
+            pltpu.VMEM(gains.shape, f32),
+            pltpu.SemaphoreType.DMA((copies,)),
+            pltpu.SemaphoreType.DMA((copies,)),
+            pltpu.SemaphoreType.DMA((2,)),
+            pltpu.SemaphoreType.DMA((32,)),
+        ],
+        compiler_params=pltpu.CompilerParams(
+            collective_id=1, has_side_effects=True, vmem_limit_bytes=63 << 20
+        ),
+        name="backward_as_gradients_leave",
+    )(*ins_any, task, gains, gain_three, down, up)
+
+
+def finish_kernel(count, *refs):
+    shards, small, gain_sum, state, gain_all, low, table, weight, bias_row = (
+        refs[:count], *refs[count : count + 8]
+    )
+    outs = refs[count + 8 : 2 * count + 8]
+    down_out, up_out, gain_out, table_out, weight_out, bias_out, rows = refs[2 * count + 8 :]
+    for shard, out in zip(shards, outs):
+        out[...] = shard[...]
+    made = down_out.shape[0]
+    low_now = low[...]
+    down_out[...] = inner_cols(small[0:8, :made].astype(bf16), low_now)
+    up_out[...] = inner_cols(small[8:16, :made].astype(bf16), low_now)
+    rows[...] = inner_cols(gain_sum[...], low_now.astype(f32), exact_mode)
+    owned = gain_out.shape[0]
+    me = lax.axis_index("dp")
+    gain_out[...] = rows[pl.ds(pl.multiple_of(me * owned, 8), owned), :]
+    makers = gain_all[...].reshape(-1, gain_all.shape[-1])
+    state_grad = state[...] + exact_dot(gain_sum[...], makers)
+    before = exact_dot(table[...], weight[...]) + bias_row[...]
+    pre_grad = gelu_both(before)[1] * state_grad
+    bias_out[...] = jnp.sum(pre_grad, axis=0, keepdims=True)
+    weight_out[...] = inner_cols(table[...], pre_grad, exact_mode)
+    table_out[...] = lax.dot_general(
+        pre_grad, weight[...], (((1,), (1,)), ((), ())), precision=exact_mode, preferred_element_type=f32
+    )
+
+
+def finish(shards, small, gain_sum, state, gain_all, low, table, weight, bias_row, makers):
+    down, up, gain = makers
+    shape = jax.ShapeDtypeStruct
+    vmem = pl.BlockSpec(memory_space=pltpu.VMEM)
+    ins = (*shards, small, gain_sum, state, gain_all, low, table, weight, bias_row)
+    outs = [shape(s.shape, f32) for s in shards]
+    outs += [shape(m.shape, f32) for m in makers] + [shape(a.shape, f32) for a in (table, weight, bias_row)]
+    return pl.pallas_call(
+        functools.partial(finish_kernel, len(shards)),
+        in_specs=[vmem] * len(ins),
+        out_specs=[vmem] * len(outs),
+        out_shape=outs,
+        scratch_shapes=[pltpu.VMEM((gain_sum.shape[1], low.shape[1]), f32)],
+        compiler_params=pltpu.CompilerParams(vmem_limit_bytes=VMEM_BYTES),
+        name="finish",
+    )(*ins)
+
+
 def on_device(
     block_input, memory, cotangent, segments, memory_segments, task_of_segment,
     self_query, self_key, self_value, self_output,
@@ -1182,36 +1588,36 @@
         .reshape(model_width, task_count * ADA)
     )
     up_all = made_up.reshape(task_count * ADA, model_width)
-    output, input_grad, mem_grad, grads, up_all_grad, down_all_grad, gain_grad = feed_and_back(
-        x, mem, cotangent.reshape(token_count, model_width), row_count, token_task,
-        backbone, gain_table, down_all, up_all, saved, probs_one, probs_two,
+    cot = cotangent.reshape(token_count, model_width)
+    output, g2, g2_low, gmix2, hidden_in_grad, hidden_out_grad, up_grad, down_grad, gain_three = feed_forward(
+        saved[5], saved[10], cot, token_task, backbone, gain_table, down_all, up_all
     )
     down_rows = (
-        down_all_grad.reshape(parts, -1, task_count, ADA)
+        down_grad.reshape(parts, -1, task_count, ADA)
         .transpose(0, 2, 1, 3)
         .reshape(parts, task_count, down_own)
     )
-    up_rows = up_all_grad.reshape(task_count, parts, -1).transpose(1, 0, 2)
-    gain_rows_all = gain_grad.reshape(task_count, parts, -1).transpose(1, 0, 2)
+    up_rows = up_grad.reshape(task_count, parts, -1).transpose(1, 0, 2)
     if parts == 32:
-        small = jnp.concatenate((down_rows, gain_rows_all), axis=2)
-        wide = small.shape[2] + (-small.shape[2] % 256)
-        small = jnp.concatenate(
-            (
-                jnp.pad(small, ((0, 0), (0, 0), (0, wide - small.shape[2]))),
-                jnp.pad(up_rows, ((0, 0), (0, 0), (0, wide - up_rows.shape[2]))),
-            ),
-            axis=1,
-        ).astype(bf16)
-        units = [
-            g.reshape((LINE, 2, 2, 2 * w.shape[0], w.shape[1])) for g, w in zip(grads, weights)
-        ]
-        units.append(small.reshape(LINE, 2, 2, 4 * task_count, wide))
-        *shared, small, state_grad = scatter(units, (down_maker, up_maker, gain_maker))
-        own_down = small[:task_count, :down_own].astype(bf16)
-        own_up = small[task_count:, :down_own].astype(bf16)
-        own_gain = small[:task_count, down_own : down_own + gain_own]
+        small = jnp.concatenate((down_rows, up_rows), axis=1).astype(bf16)
+        small = jnp.pad(small, ((0, 0), (0, 0), (0, model_width - down_own)))
+        in_grad = hidden_in_grad.reshape((LINE, 2, 2, -1, hidden_in.shape[1]))
+        out_grad = hidden_out_grad.reshape((LINE, 2, 2, -1, model_width))
+        mem_grad, input_grad, *shared, small, gain_sum, state = backward(
+            mem_len, saved, (probs_one, probs_two), x, mem, outs[:7], g2, g2_low, gmix2, in_grad, out_grad,
+            small.reshape(LINE, 2, 2, 4 * task_count, model_width), token_task, gain_table, gain_three,
+            down_maker, up_maker, weights,
+        )
+        *shared, down_maker_grad, up_maker_grad, gain_maker_grad, table_grad, weight_grad, bias_grad = finish(
+            shared, small, gain_sum, state, outs[11], task_low, task_table, task_weight,
+            task_bias.reshape(1, -1), makers,
+        )
+        bias_grad = bias_grad.reshape(task_bias.shape)
     else:
+        input_grad, mem_grad, grads, gain_one, gain_two = attention_back(
+            x, mem, row_count, token_task, backbone, gain_table, saved, probs_one, probs_two, g2, g2_low, gmix2
+        )
+        grads = (*grads, hidden_in_grad, hidden_out_grad)
         packed = jnp.concatenate([g.reshape(parts, -1, model_width) for g in grads], axis=1)
         packed = lax.psum_scatter(packed, "dp", scatter_dimension=0, tiled=False).astype(f32)
         shared, at = [], 0
@@ -1219,6 +1625,8 @@
             count = w.size // model_width
             shared.append(packed[at : at + count].reshape(w.shape))
             at += count
+        gain_grad = jnp.concatenate((gain_one, gain_two, gain_three), axis=1)
+        gain_rows_all = gain_grad.reshape(task_count, parts, -1).transpose(1, 0, 2)
         small = jnp.concatenate((down_rows, up_rows, gain_rows_all), axis=2)
         small = lax.psum_scatter(small, "dp", scatter_dimension=0, tiled=False)
         own_down = small[:, :down_own].astype(bf16)
@@ -1230,10 +1638,10 @@
             + exact_dot(own_gain, gain_maker.astype(f32)),
             "dp",
         )
-    down_maker_grad = inner_cols(own_down, task_low)
-    up_maker_grad = inner_cols(own_up, task_low)
-    gain_maker_grad = inner_cols(own_gain, task_low.astype(f32), exact_mode)
-    table_grad, weight_grad, bias_grad = task_back(state_grad)
+        down_maker_grad = inner_cols(own_down, task_low)
+        up_maker_grad = inner_cols(own_up, task_low)
+        gain_maker_grad = inner_cols(own_gain, task_low.astype(f32), exact_mode)
+        table_grad, weight_grad, bias_grad = task_back(state_grad)
     return (
         output.reshape(row_count, seq_len, model_width),
         input_grad.reshape(row_count, seq_len, model_width),

time: 455 us -> 414 us (0.910)
  Pallas kernels: 416 us -> 386 us
  matrix products: 6.65 us -> 0 us
  local copies, waits for them, and re-layouts: 22.2 us -> 17.4 us
    pallas_call x10 -> x3, Pallas kernels: 155 us -> 69.8 us  [call(): pl.pallas_call(kernel, grid=grid, in_specs=[pl.BlockSpec(b, m) for _, b,...]
    pallas_call x1 -> x2, Pallas kernels: 124 us -> 180 us  [the longest x1 175 us: backward(): pl.pallas_call(functools.partial(backward_kernel, (rows, length, mem_len,...]
    dot_general x6 -> x0, matrix products: 6.65 us -> none  [the longest x3 3.56 us: inner_cols(): lax.dot_general(left_side, right_side, (((0,), (0,)), ((), ())), precisio...]
    unnamed x40 -> x6, local copies, waits for them, and re-layouts: 10.3 us -> 5.58 us
where the time goes in v5:
time: 414 us; the launch traced here: 408 us
  Pallas kernels  386 us (93%)
  local copies, waits for them, and re-layouts  17.4 us (4%)
    pallas_call x1, Pallas kernels, backward(): pl.pallas_call(functools.partial(backward_kernel, (rows, length, mem_len,...  175 us
    pallas_call x1, Pallas kernels, forward(): pl.pallas_call(forward_kernel, in_specs=[vmem] * 21, out_specs=[any_space...  137 us
    pallas_call x3, Pallas kernels, call(): pl.pallas_call(kernel, grid=grid, in_specs=[pl.BlockSpec(b, m) for _, b,...  69.8 us

profile of v5, /device:TPU:0, one launch (start us, length us, event | category | flops | bytes accessed | tf_op | source)
XLA Modules:
  0.0 408.3 jit_solution(2151594102026461100)
XLA Ops:
  0.7 136.5 %forward_as_weights_arrive.1 = (bf16[4,2,2,48,768]{4,3,2,1,0:T(8,128)(2,1)}, bf16[4,2,2,48,768]{4,3,2,1,0:T(8,128)(2,1)}, bf16[4,2,2,48,768]{4,3,2,1,0:T(8,128)(...) custom-call(bf16[1024,768]{1,0:T(8,128)(2,1)} %bitcast.35, ...), custom_call_target="tpu_custom_call" | custom-call | tf_op jit(solution)/shard_map/forward_as_weights_arrive/pallas_call | solution.py:941
  137.2 1.3 slice.13.gain
  138.6 1.4 convert.18
  140.0 0.1 fusion.3
  140.0 0.1 copy_bitcast_fusion
  140.1 1.2 convert_element_type.22.up_all
  141.3 1.3 convert_element_type.20
  142.6 0.6 copy.45
  143.2 0.9 copy.47.down_all
  144.1 47.2 %feed_forward_and_back.1 = (bf16[1024,768]{1,0:T(8,128)(2,1)}, bf16[1024,768]{1,0:T(8,128)(2,1)}, bf16[1024,3072]{1,0:T(8,128)(2,1)}, bf16[1024,3072]{1,0:T(8,12...) custom-call(f32[1024,768]{1,0:T(8,128)} %get-tuple-element.89.s1.ref, ...), custom_call_target="tpu_custom_call" | custom-call | flops 21743271936 | bytes 42323968 | tf_op jit(solution)/shard_map/feed_forward_and_back/pallas_call | solution.py:93
  191.3 0.0 copy-start.1
  191.3 1.2 convert.17
  192.5 0.5 reshape.129
  193.0 0.1 copy.56
  193.1 0.0 copy-done.1
  193.2 0.2 copy.48
  193.4 2.5 reshape.127
  195.9 2.0 copy.49
  198.0 1.0 reshape.128
  199.0 1.0 fusion.2
  200.0 9.7 %hidden_in_grad.1 = bf16[768,3072]{1,0:T(8,128)(2,1)} custom-call(bf16[1024,768]{1,0:T(8,128)(2,1)} %get-tuple-element.119.refs_0_, bf16[1024,3072]{1,0:T(8,128)(2,1)} %get-tuple-element.120.refs_1_), custom_call_target="tpu_custom_call" | custom-call | flops 4831838208 | bytes 12582912 | tf_op jit(solution)/shard_map/hidden_in_grad/pallas_call | solution.py:93
  209.7 12.9 %hidden_out_grad.1 = bf16[3072,768]{1,0:T(8,128)(2,1)} custom-call(bf16[1024,3072]{1,0:T(8,128)(2,1)} %get-tuple-element.121.refs_0_, bf16[1024,768]{1,0:T(8,128)(2,1)} %get-tuple-element.122.refs_1_), custom_call_target="tpu_custom_call" | custom-call | flops 4831838208 | bytes 12582912 | tf_op jit(solution)/shard_map/hidden_out_grad/pallas_call | solution.py:93
  222.6 175.2 %backward_as_gradients_leave.1 = (f32[1024,768]{1,0:T(8,128)}, f32[1024,768]{1,0:T(8,128)}, f32[24,768]{1,0:T(8,128)}, f32[24,768]{1,0:T(8,128)}, f32[24,768]{1,...) custom-call(bf16[12,2,512,512]{3,2,1,0:T(8,128)(2,1)} %bitcast.31, ...), custom_call_target="tpu_custom_call" | custom-call | tf_op jit(solution)/shard_map/backward_as_gradients_leave/pallas_call | solution.py:1449
  397.8 4.7 %finish.1 = (f32[24,768]{1,0:T(8,128)}, f32[24,768]{1,0:T(8,128)}, f32[24,768]{1,0:T(8,128)}, f32[24,768]{1,0:T(8,128)}, f32[24,768]{1,0:T(8,128)}, /*index=5*/f...) custom-call(f32[24,768]{1,0:T(8,128)} %get-tuple-element.128.refs_0_, ...), custom_call_target="tpu_custom_call" | custom-call | tf_op jit(solution)/shard_map/finish/pallas_call | solution.py:1518
  402.5 0.0 copy-start
  402.5 3.9 copy.59
  406.4 0.0 copy-done
  406.4 1.7 copy.60
  (1 shorter events, 0.0 us)
Async XLA Ops:
  191.3 1.8 copy-start.1
  402.5 3.9 copy-start

commit v6 on v5

--- a/solution.py
+++ b/solution.py
@@ -602,6 +602,11 @@
             copy.wait_send()
 
 
+ORDER = reversed
+FIRST_PACE = 1
+PACE = 2
+
+
 class Unit:
     def __init__(self, here, copies, source, whole_array, index, first, second):
         self.here, self.copies = here, copies
@@ -614,7 +619,7 @@
 
     def depart(self):
         here, copies = self.here, self.copies
-        source = self.source()
+        source = self.source(None)
         target = self.window(here.z, here.y, here.x)
         self.going["z"] = [copies.remote(source, target, here.along_z(k)) for k in (1, 2, 3)]
         self.own = copies.local(source, target)
@@ -709,63 +714,82 @@
     opened = set()
 
     def piece(i, rows, first, width):
-        def source():
+        at = half(i, c, first, width)
+        count = rows.stop - rows.start
+        if (width // 2) % 128 == 0:
+            windows = (
+                (rows, half(i, c, first, width // 2)),
+                (rows, half(i, c, first + width // 2, width // 2)),
+            )
+            local = (
+                (rows, pl.ds(first, width // 2)),
+                (rows, pl.ds(first + width // 2, width // 2)),
+            )
+        else:
+            cut = rows.start + (count // 2 if count % 32 == 0 else (count // 32 + i % 2) * 16)
+            split = (slice(rows.start, cut), slice(cut, rows.stop))
+            windows = tuple((part, at) for part in split)
+            local = tuple((part, pl.ds(first, width)) for part in split)
+
+        def source(share):
             if i not in opened:
                 opened.add(i)
                 pair[i].wait_recv()
                 blocks[i][...] = halves[i][...].astype(bf16)
-            return blocks[i].at[rows, pl.ds(first, width)]
-
-        at = half(i, c, first, width)
-        count = rows.stop - rows.start
-        if (width // 2) % 128 == 0:
-            one = (rows, half(i, c, first, width // 2))
-            two = (rows, half(i, c, first + width // 2, width // 2))
-        else:
-            cut = rows.start + (count // 2 if count % 32 == 0 else (count // 32 + i % 2) * 16)
-            one = (slice(rows.start, cut), at)
-            two = (slice(cut, rows.stop), at)
-        return Unit(here, copies, source, outs[i], (rows, at), one, two)
+            return blocks[i].at[(rows, pl.ds(first, width)) if share is None else local[share]]
+
+        return Unit(here, copies, source, outs[i], (rows, at), *windows)
 
     def square(i):
         return piece(i, slice(0, outs[i].shape[3]), 0, own[i].shape[1] // 2)
 
     gain_own = gain.shape[0]
     gain_cut = gain_own // 16 * 8
-    made_cut = made.shape[1] // 2
+    made_cut = made.shape[1] // 256 * 128
     gain_unit = Unit(
-        here, copies, lambda: gain_rows_all, gains_out, (c,),
+        here, copies, lambda _: gain_rows_all, gains_out, (c,),
         (c, pl.ds(0, gain_cut)), (c, pl.ds(gain_cut, gain_own - gain_cut)),
     )
     made_unit = Unit(
-        here, copies, lambda: made, made_out, (c,),
-        (c, slice(None), pl.ds(0, made_cut)), (c, slice(None), pl.ds(made_cut, made_cut)),
+        here, copies, lambda _: made, made_out, (c,),
+        (c, slice(None), pl.ds(0, made_cut)), (c, slice(None), pl.ds(made_cut, made.shape[1] - made_cut)),
     )
     in_half = w_in.shape[1] // 4
     out_rows = outs[9].shape[3]
     units = [gain_unit] + [square(i) for i in (0, 1, 2, 5, 6, 3, 4, 7)]
-    units += [piece(8, slice(0, outs[8].shape[3]), k * in_half, in_half) for k in (0, 1)]
+    units += [
+        piece(8, slice(0, outs[8].shape[3]), k * in_half, in_half) for k in (0, 1)
+    ]
     units += [made_unit]
     units += [
-        piece(9, slice(k * out_rows // 2, (k + 1) * out_rows // 2), 0, w_out.shape[1] // 2)
+        piece(
+            9, slice(k * out_rows // 2, (k + 1) * out_rows // 2), 0, w_out.shape[1] // 2
+        )
         for k in (0, 1)
     ]
     loads = {}
     landing = {1: (0,), 2: (1,), 3: (2,), 4: (5,), 5: (6,), 6: (3,), 7: (4,), 8: (7,)}
 
+    def stage_at(u, turn):
+        pace = FIRST_PACE if u < 4 else PACE
+        return (turn - u) // pace if turn >= u and (turn - u) % pace == 0 else -1
+
     def tick(turn):
-        for late in range(5):
-            u = turn - late
-            if 0 <= u < len(units):
-                units[u].stages()[late]()
-                if late == 4 and u in landing:
-                    (i,) = landing[u]
-                    loads[i] = pltpu.make_async_copy(outs[i], local_w[i], load_sem.at[i])
-                    loads[i].start()
-                if late == 4 and u == 0:
-                    loads["gain"] = pltpu.make_async_copy(gains_out, gain_full, load_sem.at[8])
-                    loads["gain"].start()
-
+        for u in range(min(turn, len(units) - 1), -1, -1):
+            if stage_at(u, turn) == 0:
+                units[u].depart()
+        for u in ORDER(range(len(units))):
+            late = stage_at(u, turn)
+            if not 0 < late < 5:
+                continue
+            units[u].stages()[late]()
+            if late == 4 and u in landing:
+                (i,) = landing[u]
+                loads[i] = pltpu.make_async_copy(outs[i], local_w[i], load_sem.at[i])
+                loads[i].start()
+            if late == 4 and u == 0:
+                loads["gain"] = pltpu.make_async_copy(gains_out, gain_full, load_sem.at[8])
+                loads["gain"].start()
 
     def matrix(i):
         return local_w[i][...].reshape(-1, own[i].shape[1])
@@ -773,14 +797,13 @@
     state = gelu_in_kernel(exact_dot(table[...], weight[...]) + bias_row[...])
     low = state.astype(bf16)
     low_out[...] = low
+    values = jnp.concatenate((inner_rows(low, down[...]), inner_rows(low, up[...])), axis=0)
     made[...] = jnp.zeros_like(made)
-    made[:, : down.shape[0]] = inner_rows(low, down[...])
-    made_at = made.shape[1] // 2
-    made[:, made_at : made_at + up.shape[0]] = inner_rows(low, up[...])
-
-    for now in range(8):
-        tick(now)
-    ticks = iter(range(8, len(units) + 4))
+    made[:, : down.shape[0]] = values.astype(bf16)
+
+    for turn in range(3 + 4 * FIRST_PACE + 1):
+        tick(turn)
+    ticks = iter(range(3 + 4 * FIRST_PACE + 1, len(units) + 4 * PACE))
 
     def between():
         turn = next(ticks, None)
@@ -937,14 +960,14 @@
     kept = [t_low, t_low, t_low, t_low, t_low, t_full, t_low, t_low, m_low, m_low, t_low]
     shape = jax.ShapeDtypeStruct
     probs = (rows, HEADS, length, mem_len)
-    copies = 11 * 16 + 16
+    copies = 11 * 16 + 32
     outs = pl.pallas_call(
         forward_kernel,
         in_specs=[vmem] * 21,
         out_specs=[any_space] * 12 + [vmem] * 3 + [any_space] * 13,
         out_shape=[shape(s, bf16) for s in chip]
         + [
-            shape(spaces + (2, n_tasks, 2 * made_half), f32),
+            shape(spaces + (2, 2 * n_tasks, made_half), bf16),
             shape(spaces + (2,) + gain.shape, f32),
             shape((n_tasks, weight.shape[1]), bf16),
             shape((n_tasks, 3 * width), f32),
@@ -958,7 +981,7 @@
         + [pltpu.VMEM(s, bf16) for s in chip[:8]]
         + [pltpu.VMEM(s, d) for s, d in kept]
         + [
-            pltpu.VMEM((n_tasks, 2 * made_half), f32),
+            pltpu.VMEM((2 * n_tasks, made_half), bf16),
             pltpu.VMEM(gain.shape, f32),
             pltpu.VMEM((length, max(length, mem_len)), f32),
             pltpu.VMEM((2, 2, length, max(length, mem_len)), bf16),
@@ -977,6 +1000,10 @@
     return outs
 
 
+BACK_ORDER = reversed
+BACK_PACE = 3
+
+
 class Stepwise:
     def __init__(self, stages):
         self.stages = list(stages)
@@ -986,19 +1013,23 @@
 
 
 class Traffic:
-    def __init__(self):
-        self.ready, self.flying = [], []
+    def __init__(self, pace):
+        self.ready, self.flying, self.pace, self.now = [], [], pace, 0
 
     def add(self, item):
         self.ready.append(item)
 
     def tick(self):
-        for item in list(self.flying):
+        self.now += 1
+        for item in BACK_ORDER(list(self.flying)):
+            if (self.now - item.began) % self.pace:
+                continue
             item.advance()
             if not item.stages:
                 self.flying.remove(item)
         if self.ready:
             item = self.ready.pop(0)
+            item.began = self.now
             item.advance()
             self.flying.append(item)
 
@@ -1015,12 +1046,16 @@
         self.here, self.copies = here, copies
         self.theirs, self.mine, self.fetch = theirs, mine, fetch
         self.shares, self.slots, self.out, self.out_first = shares, slots, out, out_first
-        self.landed = None
+        self.landed = self.follower = None
+        self.follows = False
 
     def begin(self):
         self.core = self.copies.remote(self.theirs, self.slots[0], self.here.sibling())
-        if self.fetch is not None:
-            self.local = self.copies.local(*self.fetch)
+        if self.fetch is not None and not self.follows:
+            self.start_fetch()
+
+    def start_fetch(self):
+        self.local = self.copies.local(*self.fetch)
 
     def over_first(self):
         here, held = self.here, self.slots[0]
@@ -1028,6 +1063,8 @@
             self.local.wait()
         self.core.wait_recv()
         held[...] += self.mine()
+        if self.follower is not None:
+            self.follower.start_fetch()
         one, two = self.shares
         self.first = (
             self.copies.remote(held.at[(slice(None), 1 - here.y, slice(None)) + one], self.slots[1], here.over_y()),
@@ -1062,16 +1099,20 @@
             for k in (1, 2, 3)
         ]
 
-    def window(self, core, width, full):
-        return pl.ds(pl.multiple_of(core * full + self.out_first, 128), width)
-
-    def to_owner(self):
-        here, held, final = self.here, self.slots[0], self.slots[6]
-        total = held[here.z, here.y, here.x].astype(f32)
+    def gathered(self):
+        here = self.here
+        total = self.slots[0][here.z, here.y, here.x].astype(f32)
         for k, copy in enumerate(self.third):
             copy.wait_recv()
             total = total + self.slots[5][k].astype(f32)
-        final[...] = total
+        return total
+
+    def window(self, core, width, full):
+        return pl.ds(pl.multiple_of(core * full + self.out_first, 128), width)
+
+    def to_owner(self):
+        here, final = self.here, self.slots[6]
+        final[...] = self.gathered()
         rows, full = self.out.shape[0], self.out.shape[1] // 2
         c = here.core
         at = self.window(c, final.shape[1], full)
@@ -1218,7 +1259,7 @@
     send, recv, p_sem, load_sem = scratch[at_slot + 5 :]
     here = Place()
     copies = Copies(send, recv)
-    traffic = Traffic()
+    traffic = Traffic(BACK_PACE)
     c = here.core
     loads = {}
 
@@ -1264,16 +1305,17 @@
             fetch=(array.at[:, :, :, :, half(c, first, size, full)], stage),
         )
 
-    for item in (
+    out_one, out_two, small_item, in_one, in_two = flown = (
         from_hbm("out0", g_out, outs[9], stage_out.at[:, :, :, :, : pieces["out0"][1]]),
         from_hbm("out1", g_out, outs[9], stage_out),
         from_hbm("small", g_small, outs[10], stage_small),
         from_hbm("in0", g_in, outs[8], stage_in),
         from_hbm("in1", g_in, outs[8], stage_in),
-    ):
+    )
+    for item in flown:
         traffic.add(item)
-        if item.out is outs[10]:
-            small_item = item
+    for item, follower in ((out_one, out_two), (in_one, in_two)):
+        item.follower, follower.follows = follower, True
 
     def small_landed():
         made = down.shape[0]
@@ -1485,11 +1527,30 @@
     shards, small, gain_sum, state, gain_all, low, table, weight, bias_row = (
         refs[:count], *refs[count : count + 8]
     )
-    outs = refs[count + 8 : 2 * count + 8]
-    down_out, up_out, gain_out, table_out, weight_out, bias_out, rows = refs[2 * count + 8 :]
+    large = refs[count + 8 : count + 10]
+    outs = refs[count + 10 : 2 * count + 10]
+    down_out, up_out, gain_out, table_out, weight_out, bias_out = refs[2 * count + 10 : 2 * count + 16]
+    large_outs, (rows, held_a, held_b, sems) = (
+        refs[2 * count + 16 : 2 * count + 18], refs[2 * count + 18 :]
+    )
+    held = (held_a, held_b)
+    moves = [
+        pltpu.make_async_copy(source, buffer, sems.at[k])
+        for k, (source, buffer) in enumerate(zip(large, held))
+    ]
+    for move in moves:
+        move.start()
     for shard, out in zip(shards, outs):
         out[...] = shard[...]
     made = down_out.shape[0]
+    for move in moves:
+        move.wait()
+    moves = [
+        pltpu.make_async_copy(buffer, target, sems.at[2 + k])
+        for k, (buffer, target) in enumerate(zip(held, large_outs))
+    ]
+    for move in moves:
+        move.start()
     low_now = low[...]
     down_out[...] = inner_cols(small[0:8, :made].astype(bf16), low_now)
     up_out[...] = inner_cols(small[8:16, :made].astype(bf16), low_now)
@@ -1506,24 +1567,32 @@
     table_out[...] = lax.dot_general(
         pre_grad, weight[...], (((1,), (1,)), ((), ())), precision=exact_mode, preferred_element_type=f32
     )
-
-
-def finish(shards, small, gain_sum, state, gain_all, low, table, weight, bias_row, makers):
+    for move in moves:
+        move.wait()
+
+
+def finish(mem_grad, input_grad, shards, small, gain_sum, state, gain_all, low, table, weight, bias_row, makers):
     down, up, gain = makers
     shape = jax.ShapeDtypeStruct
     vmem = pl.BlockSpec(memory_space=pltpu.VMEM)
     ins = (*shards, small, gain_sum, state, gain_all, low, table, weight, bias_row)
     outs = [shape(s.shape, f32) for s in shards]
     outs += [shape(m.shape, f32) for m in makers] + [shape(a.shape, f32) for a in (table, weight, bias_row)]
+    large = (mem_grad, input_grad)
+    any_space = pl.BlockSpec(memory_space=pl.ANY)
     return pl.pallas_call(
         functools.partial(finish_kernel, len(shards)),
-        in_specs=[vmem] * len(ins),
-        out_specs=[vmem] * len(outs),
-        out_shape=outs,
-        scratch_shapes=[pltpu.VMEM((gain_sum.shape[1], low.shape[1]), f32)],
+        in_specs=[vmem] * len(ins) + [any_space] * 2,
+        out_specs=[vmem] * len(outs) + [any_space] * 2,
+        out_shape=outs + [shape(a.shape, f32) for a in large],
+        scratch_shapes=[
+            pltpu.VMEM((gain_sum.shape[1], low.shape[1]), f32),
+            *(pltpu.VMEM(a.shape, f32) for a in large),
+            pltpu.SemaphoreType.DMA((4,)),
+        ],
         compiler_params=pltpu.CompilerParams(vmem_limit_bytes=VMEM_BYTES),
         name="finish",
-    )(*ins)
+    )(*ins, *large)
 
 
 def on_device(
@@ -1558,10 +1627,11 @@
             task_table, task_weight, task_bias.reshape(1, -1), makers,
         )
         backbone = [w.reshape(-1, w.shape[-1]) for w in outs[:10]]
-        made = outs[10].reshape(parts, task_count, -1)
+        made = outs[10].reshape(parts, 2 * task_count, -1)
         task_low, gain_table, token_task = outs[12:15]
         saved, probs_one, probs_two = outs[15:26], outs[26], outs[27]
-        made_up = joined(made[:, :, made.shape[2] // 2 :][:, :, :down_own]).astype(bf16)
+        made_up = joined(made[:, task_count:, :down_own])
+        made = made[:, :task_count]
     else:
         packed = jnp.concatenate([w.reshape(-1, model_width) for w in weights], axis=0)
         packed = lax.all_gather(packed, "dp", axis=0, tiled=False)
@@ -1608,8 +1678,11 @@
             small.reshape(LINE, 2, 2, 4 * task_count, model_width), token_task, gain_table, gain_three,
             down_maker, up_maker, weights,
         )
-        *shared, down_maker_grad, up_maker_grad, gain_maker_grad, table_grad, weight_grad, bias_grad = finish(
-            shared, small, gain_sum, state, outs[11], task_low, task_table, task_weight,
+        (
+            *shared, down_maker_grad, up_maker_grad, gain_maker_grad,
+            table_grad, weight_grad, bias_grad, mem_grad, input_grad,
+        ) = finish(
+            mem_grad, input_grad, shared, small, gain_sum, state, outs[11], task_low, task_table, task_weight,
             task_bias.reshape(1, -1), makers,
         )
         bias_grad = bias_grad.reshape(task_bias.shape)

time: 414 us -> 355 us (0.86)
  Pallas kernels: 386 us -> 333 us
  local copies, waits for them, and re-layouts: 17.4 us -> 12.9 us
    pallas_call x1, Pallas kernels: 175 us -> 133 us  [backward(): pl.pallas_call(functools.partial(backward_kernel, (rows, length, mem_len,...]
    pallas_call x1, Pallas kernels: 137 us -> 122 us  [forward(): pl.pallas_call(forward_kernel, in_specs=[vmem] * 21, out_specs=[any_space...]
    unnamed x6 -> x2, local copies, waits for them, and re-layouts: 5.58 us -> 0.01 us
where the time goes in v6:
time: 355 us; the launch traced here: 349 us
  Pallas kernels  333 us (94%)
  local copies, waits for them, and re-layouts  12.9 us (4%)
    pallas_call x1, Pallas kernels, backward(): pl.pallas_call(functools.partial(backward_kernel, (rows, length, mem_len,...  133 us
    pallas_call x1, Pallas kernels, forward(): pl.pallas_call(forward_kernel, in_specs=[vmem] * 21, out_specs=[any_space...  122 us
    pallas_call x3, Pallas kernels, call(): pl.pallas_call(kernel, grid=grid, in_specs=[pl.BlockSpec(b, m) for _, b,...  69.8 us
    pallas_call x1, Pallas kernels, finish(): pl.pallas_call(functools.partial(finish_kernel, len(shards)), in_specs=[v...  8.56 us

profile of v6, /device:TPU:0, one launch (start us, length us, event | category | flops | bytes accessed | tf_op | source)
XLA Modules:
  0.0 349.4 jit_solution(8584756388182144199)
XLA Ops:
  0.7 122.2 %forward_as_weights_arrive.1 = (bf16[4,2,2,48,768]{4,3,2,1,0:T(8,128)(2,1)}, bf16[4,2,2,48,768]{4,3,2,1,0:T(8,128)(2,1)}, bf16[4,2,2,48,768]{4,3,2,1,0:T(8,128)(...) custom-call(bf16[1024,768]{1,0:T(8,128)(2,1)} %bitcast.35, ...), custom_call_target="tpu_custom_call" | custom-call | tf_op jit(solution)/shard_map/forward_as_weights_arrive/pallas_call | solution.py:964
  122.8 1.3 slice.11.gain
  124.2 1.1 fusion.3
  125.3 0.1 copy_bitcast_fusion
  125.4 1.2 reshape_reshape.7.up_all
  126.6 1.3 reshape_reshape.6
  127.9 0.6 copy.45
  128.5 0.9 copy.47.down_all
  129.4 47.2 %feed_forward_and_back.1 = (bf16[1024,768]{1,0:T(8,128)(2,1)}, bf16[1024,768]{1,0:T(8,128)(2,1)}, bf16[1024,3072]{1,0:T(8,128)(2,1)}, bf16[1024,3072]{1,0:T(8,12...) custom-call(f32[1024,768]{1,0:T(8,128)} %get-tuple-element.91.s1.ref, ...), custom_call_target="tpu_custom_call" | custom-call | flops 21743271936 | bytes 42323968 | tf_op jit(solution)/shard_map/feed_forward_and_back/pallas_call | solution.py:93
  176.6 0.0 copy-start
  176.6 1.2 convert.12
  177.8 0.5 reshape.121
  178.3 0.1 copy.56
  178.4 0.0 copy-done
  178.5 0.2 copy.48
  178.7 2.5 reshape.119
  181.2 2.0 copy.49
  183.2 1.0 reshape.120
  184.3 1.0 fusion.2
  185.3 9.7 %hidden_in_grad.1 = bf16[768,3072]{1,0:T(8,128)(2,1)} custom-call(bf16[1024,768]{1,0:T(8,128)(2,1)} %get-tuple-element.121.refs_0_, bf16[1024,3072]{1,0:T(8,128)(2,1)} %get-tuple-element.122.refs_1_), custom_call_target="tpu_custom_call" | custom-call | flops 4831838208 | bytes 12582912 | tf_op jit(solution)/shard_map/hidden_in_grad/pallas_call | solution.py:93
  195.0 12.9 %hidden_out_grad.1 = bf16[3072,768]{1,0:T(8,128)(2,1)} custom-call(bf16[1024,3072]{1,0:T(8,128)(2,1)} %get-tuple-element.123.refs_0_, bf16[1024,768]{1,0:T(8,128)(2,1)} %get-tuple-element.124.refs_1_), custom_call_target="tpu_custom_call" | custom-call | flops 4831838208 | bytes 12582912 | tf_op jit(solution)/shard_map/hidden_out_grad/pallas_call | solution.py:93
  207.9 132.7 %backward_as_gradients_leave.1 = (f32[1024,768]{1,0:T(8,128)}, f32[1024,768]{1,0:T(8,128)}, f32[24,768]{1,0:T(8,128)}, f32[24,768]{1,0:T(8,128)}, f32[24,768]{1,...) custom-call(bf16[12,2,512,512]{3,2,1,0:T(8,128)(2,1)} %bitcast.31, ...), custom_call_target="tpu_custom_call" | custom-call | tf_op jit(solution)/shard_map/backward_as_gradients_leave/pallas_call | solution.py:1491
  340.6 8.6 %finish.1 = (f32[24,768]{1,0:T(8,128)}, f32[24,768]{1,0:T(8,128)}, f32[24,768]{1,0:T(8,128)}, f32[24,768]{1,0:T(8,128)}, f32[24,768]{1,0:T(8,128)}, /*index=5*/f...) custom-call(f32[24,768]{1,0:T(8,128)} %get-tuple-element.128.refs_0_, ...), custom_call_target="tpu_custom_call" | custom-call | tf_op jit(solution)/shard_map/finish/pallas_call | solution.py:1583
  (1 shorter events, 0.0 us)
Async XLA Ops:
  176.6 1.8 copy-start

commit v7 on v6

--- a/solution.py
+++ b/solution.py
@@ -265,6 +265,8 @@
 
 
 CHUNK = 768
+FEED_CHUNK = 768
+OUTER_BLOCK = 768
 
 
 def feed_kernel(
@@ -277,18 +279,20 @@
     stream = s1[...] + plain_dot(mixed[...], wo[...])
     picked = token_gain(task[...], gain[...])
     n3[...] = (stream * inverse_rms(stream) * picked).astype(bf16)
-    total[...] = jnp.zeros_like(total)
-
-    @pl.loop(0, units // CHUNK)
-    def _(j):
-        cols = pl.ds(pl.multiple_of(j * CHUNK, CHUNK), CHUNK)
-        value, rate = gelu_both(plain_dot(n3[...], w_in[:, cols]))
+    parts = [slice(k, k + FEED_CHUNK) for k in range(0, units, FEED_CHUNK)]
+    normed = n3[...]
+    hidden = plain_dot(normed, w_in[:, parts[0]])
+    feed = None
+    for k, cols in enumerate(parts):
+        now = hidden
+        if k + 1 < len(parts):
+            hidden = plain_dot(normed, w_in[:, parts[k + 1]])
+        value, rate = gelu_both(now)
         value = value.astype(bf16)
         act[:, cols] = value
         slope[:, cols] = rate.astype(bf16)
-        total[...] += plain_dot(value, w_out[cols, :])
-
-    feed = total[...]
+        term = plain_dot(value, w_out[cols, :])
+        feed = term if feed is None else feed + term
     feed_low = feed.astype(bf16)
     tokens, wide = stream.shape[0], down_all.shape[1]
     owner = lax.broadcasted_iota(jnp.int32, (tokens, wide), 1) - task[...] * ADA
@@ -381,7 +385,7 @@
 
 def outers(sources, grads, which, name):
     tokens, width = sources[0].shape
-    block = 256
+    block = OUTER_BLOCK if width > 768 else 256
     return call(
         functools.partial(outer_kernel, which, len(sources)),
         (width // block,),
@@ -444,7 +448,6 @@
 def feed_forward(s1, m2, cot, task, weights, gain_table, down_all, up_all):
     tokens, width = s1.shape
     wo2, w_in, w_out = weights[7:]
-    gain_three = gain_table[:, 2 * width :]
     block = BLOCK
     grid = (tokens // block,)
     act_shape = (tokens, width)
@@ -456,8 +459,8 @@
         feed_kernel,
         grid,
         [
-            by_row(s1, block), by_row(m2, block), whole(wo2), by_row(task, block), whole(gain_three),
-            whole(w_in), whole(w_out), whole(down_all), whole(up_all), by_row(cot, block),
+            by_row(s1, block), by_row(m2, block), whole(wo2), by_row(task, block),
+            (gain_table, (gain_table.shape[0], width), lambda *_: (0, 2)), whole(w_in), whole(w_out), whole(down_all), whole(up_all), by_row(cot, block),
         ],
         [
             low_out(act_shape), low_out(act_shape), out_row((tokens, units), bf16, block), out_row((tokens, units), bf16, block),
@@ -468,9 +471,8 @@
         flops=2 * square + 8 * tokens * width * units,
         name="feed_forward_and_back",
     )
-    (hidden_in_grad,) = outers((n3,), (gu,), (0,), "hidden_in_grad")
     (hidden_out_grad,) = outers((act,), (gfeed,), (0,), "hidden_out_grad")
-    return output, g2, g2_low, gmix2, hidden_in_grad, hidden_out_grad, up_grad, down_grad, gain3
+    return output, g2, g2_low, gmix2, n3, gu, hidden_out_grad, up_grad, down_grad, gain3
 
 
 def attention_back(x, mem, rows, task, weights, gain_table, saved, p1, p2, g2, g2_low, gmix2):
@@ -602,7 +604,6 @@
             copy.wait_send()
 
 
-ORDER = reversed
 FIRST_PACE = 1
 PACE = 2
 
@@ -778,7 +779,7 @@
         for u in range(min(turn, len(units) - 1), -1, -1):
             if stage_at(u, turn) == 0:
                 units[u].depart()
-        for u in ORDER(range(len(units))):
+        for u in reversed(range(len(units))):
             late = stage_at(u, turn)
             if not 0 < late < 5:
                 continue
@@ -1000,37 +1001,36 @@
     return outs
 
 
-BACK_ORDER = reversed
-BACK_PACE = 3
+BACK_PACES = (2, 6, 6, 6, 3)
+QUICK_PACES = (1, 1, 1, 1)
+EARLY_TICKS = 3
 
 
 class Stepwise:
-    def __init__(self, stages):
-        self.stages = list(stages)
-
-    def advance(self):
+    def __init__(self, stages, paces):
+        self.stages, self.paces = list(stages), list(paces)
+
+    def advance(self, now):
         self.stages.pop(0)()
+        self.due = now + (self.paces.pop(0) if self.stages else 0)
 
 
 class Traffic:
-    def __init__(self, pace):
-        self.ready, self.flying, self.pace, self.now = [], [], pace, 0
+    def __init__(self):
+        self.ready, self.flying, self.now = [], [], 0
 
     def add(self, item):
         self.ready.append(item)
 
     def tick(self):
         self.now += 1
-        for item in BACK_ORDER(list(self.flying)):
-            if (self.now - item.began) % self.pace:
-                continue
-            item.advance()
-            if not item.stages:
-                self.flying.remove(item)
+        for item in reversed(list(self.flying)):
+            if self.now >= item.due:
+                item.advance(self.now)
+        self.flying = [item for item in self.flying if item.stages]
         if self.ready:
             item = self.ready.pop(0)
-            item.began = self.now
-            item.advance()
+            item.advance(self.now)
             self.flying.append(item)
 
     def drain(self):
@@ -1041,13 +1041,14 @@
 class Summed(Stepwise):
     def __init__(self, here, copies, theirs, mine, shares, slots, out, out_first, fetch=None):
         super().__init__(
-            [self.begin, self.over_first, self.over_second, self.over_line, self.to_owner, self.end]
+            [self.begin, self.over_first, self.over_second, self.over_line, self.to_owner, self.end],
+            BACK_PACES,
         )
         self.here, self.copies = here, copies
         self.theirs, self.mine, self.fetch = theirs, mine, fetch
         self.shares, self.slots, self.out, self.out_first = shares, slots, out, out_first
         self.landed = self.follower = None
-        self.follows = False
+        self.follows = self.added = False
 
     def begin(self):
         self.core = self.copies.remote(self.theirs, self.slots[0], self.here.sibling())
@@ -1063,6 +1064,7 @@
             self.local.wait()
         self.core.wait_recv()
         held[...] += self.mine()
+        self.added = True
         if self.follower is not None:
             self.follower.start_fetch()
         one, two = self.shares
@@ -1128,7 +1130,7 @@
 
 class Everywhere(Stepwise):
     def __init__(self, here, copies, value, sent, arriving, out):
-        super().__init__([self.begin, self.step_x, self.step_y, self.step_z, self.end])
+        super().__init__([self.begin, self.step_x, self.step_y, self.step_z, self.end], QUICK_PACES)
         self.here, self.copies, self.value = here, copies, value
         self.sent, self.arriving, self.out = sent, arriving, out
 
@@ -1236,30 +1238,32 @@
     pieces = sum_pieces(width, units, own_rows)
     (
         p1, p2, q2h, k2h, v2h, m2h, gm2h, q1h, k1h, v1h, m1h, n1h, n2h, memh, xh, s1h, g2h, g2lowh,
-        wq1h, wk1h, wv1h, wo1h, wq2h, wk2h, wv2h, g_in, g_out, g_small,
+        wq1h, wk1h, wv1h, wo1h, wq2h, wk2h, wv2h, n3h, guh, g_out, g_small,
         task, gains, gain_three, down, up,
-    ) = refs[:33]
-    mem_out, input_out = refs[33:35]
-    outs = refs[35:46]
-    gain_out, state_out = refs[46:48]
-    scratch = refs[48:]
+    ) = refs[:34]
+    mem_out, input_out = refs[34:36]
+    outs = refs[36:47]
+    gain_out, state_out = refs[47:49]
+    scratch = refs[49:]
     a = scratch[:5]
     gq, gk, gv = scratch[5:8]
     f0, f1, low = scratch[8:11]
     probs = scratch[11]
     w = scratch[12:16]
     grads = scratch[16:20]
-    stage_in, stage_out, stage_small = scratch[20:23]
+    stage_out, stage_small = scratch[20:22]
     slots = {}
-    at_slot = 23
+    at_slot = 22
     for name in SUM_NAMES:
         slots[name] = scratch[at_slot : at_slot + 7]
         at_slot += 7
-    state_sent, state_arriving, gain_sent, gain_arriving, gain_rows_ref = scratch[at_slot : at_slot + 5]
-    send, recv, p_sem, load_sem = scratch[at_slot + 5 :]
+    state_sent, state_arriving, gain_sent, gain_arriving, late_sent, late_arriving, gain_rows_ref = scratch[
+        at_slot : at_slot + 7
+    ]
+    send, recv, p_sem, load_sem = scratch[at_slot + 7 :]
     here = Place()
     copies = Copies(send, recv)
-    traffic = Traffic(BACK_PACE)
+    traffic = Traffic()
     c = here.core
     loads = {}
 
@@ -1274,6 +1278,18 @@
     def half(which, first, size, full):
         return pl.ds(pl.multiple_of(which * full + first, 128), size)
 
+    full_in = units // 2
+    panels = [(which, k) for k in (0, 1) for which in (1, 0)]
+
+    def fetch_panel(turn):
+        which, k = panels[turn]
+        core = 1 - c if which else c
+        cols = pl.ds(pl.multiple_of(core * full_in + k * width, 128), width)
+        fetch(("panel", turn), guh.at[:, cols], (gq, gk)[turn % 2])
+
+    fetch("n3", n3h, gv)
+    fetch_panel(0)
+    fetch_panel(1)
     fetch("m2", m2h, a[3])
     fetch("g2low", g2lowh, low)
     fetch("q2", q2h, a[0])
@@ -1305,17 +1321,14 @@
             fetch=(array.at[:, :, :, :, half(c, first, size, full)], stage),
         )
 
-    out_one, out_two, small_item, in_one, in_two = flown = (
+    out_one, out_two, small_item = flown = (
         from_hbm("out0", g_out, outs[9], stage_out.at[:, :, :, :, : pieces["out0"][1]]),
         from_hbm("out1", g_out, outs[9], stage_out),
         from_hbm("small", g_small, outs[10], stage_small),
-        from_hbm("in0", g_in, outs[8], stage_in),
-        from_hbm("in1", g_in, outs[8], stage_in),
     )
     for item in flown:
         traffic.add(item)
-    for item, follower in ((out_one, out_two), (in_one, in_two)):
-        item.follower, follower.follows = follower, True
+    out_one.follower, out_two.follows = out_two, True
 
     def small_landed():
         made = down.shape[0]
@@ -1327,23 +1340,32 @@
     small_item.landed = small_landed
     users = {}
 
-    def weight_gradient(name, index, source, grad, slot):
-        if slot in users:
-            copies.close(users[slot].core)
-        buffer = grads[slot]
-        rows, size, first, one, two = pieces[name]
+    def free(slot):
+        item = users.pop(slot, None)
+        if item is not None:
+            while not item.added:
+                traffic.tick()
+            if any(item.core is copy for copy in copies.open):
+                copies.close(item.core)
+
+    def product(source, grad, slot):
+        free(slot)
         columns = width // 2
         for k in range(2):
             block = inner_cols(source[:, k * columns : (k + 1) * columns], grad[...]).astype(bf16)
-            buffer[2 * k : 2 * k + 2] = block.reshape((2, 2, 2, rows, width))
+            grads[slot][2 * k : 2 * k + 2] = block.reshape((2, 2, 2, 2 * own_rows, width))
+        return grads[slot]
+
+    def weight_gradient(name, index, source, grad, slot):
+        buffer = product(source, grad, slot)
+        rows, size, first, one, two = pieces[name]
         full = width // 2
-        item = Summed(
+        users[slot] = Summed(
             here, copies, buffer.at[:, :, :, :, half(1 - c, 0, size, full)],
             lambda: buffer[:, :, :, :, half(c, 0, size, full)],
             (one, two), slots[name], outs[index], 0,
         )
-        users[slot] = item
-        traffic.add(item)
+        traffic.add(users[slot])
 
     def matrix(k):
         return w[k][...].reshape(width, width)
@@ -1375,7 +1397,24 @@
 
             traffic.tick()
 
-    traffic.tick()
+    for _ in range(EARLY_TICKS):
+        traffic.tick()
+    need("n3")
+    for turn, (which, k) in enumerate(panels):
+        need(("panel", turn))
+        buffer = product(gv, (gq, gk)[turn % 2], turn)
+        if turn + 2 < len(panels):
+            fetch_panel(turn + 2)
+        if which == 0:
+            _, _, first, one, two = pieces[f"in{k}"]
+            mine = buffer
+            item = Summed(
+                here, copies, theirs, lambda mine=mine: mine[...], (one, two), slots[f"in{k}"], outs[8], first
+            )
+            users[turn - 1] = users[turn] = item
+            traffic.add(item)
+        theirs = buffer
+        traffic.tick()
     need("m2", "g2low")
     weight_gradient("o2", 7, a[3], low, 0)
     traffic.tick()
@@ -1400,6 +1439,11 @@
         now = gain_rows(task[row(r), :], gain_tokens)
         gain_two = now if gain_two is None else gain_two + now
         traffic.tick()
+    gain_rows_ref[:, width : 2 * width] = gain_two
+    gain_rows_ref[:, 2 * width :] = gain_three[...]
+    traffic.add(
+        Everywhere(here, copies, lambda: gain_rows_ref[:, width:], late_sent, late_arriving, gain_out.at[:, width:])
+    )
     fetch("wq1", wq1h, w[0])
     fetch("wk1", wk1h, w[1])
     need("n2", "mem")
@@ -1441,15 +1485,15 @@
         traffic.tick()
     fetch("input_out", f1, input_out)
     gain_rows_ref[:, :width] = gain_one
-    gain_rows_ref[:, width : 2 * width] = gain_two
-    gain_rows_ref[:, 2 * width :] = gain_three[...]
-    traffic.ready.insert(0, Everywhere(here, copies, lambda: gain_rows_ref[...], gain_sent, gain_arriving, gain_out))
+    traffic.ready.insert(
+        0, Everywhere(here, copies, lambda: gain_rows_ref[:, :width], gain_sent, gain_arriving, gain_out.at[:, :width])
+    )
     traffic.drain()
     need("mem_out", "input_out")
     copies.finish()
 
 
-def backward(mem_len, saved, probs, x, mem, weights, g2, g2_low, gmix2, g_in, g_out, g_small, task, gains, gain_three, down, up, own):
+def backward(mem_len, saved, probs, x, mem, weights, g2, g2_low, gmix2, n3, gu, g_out, g_small, task, gains, gain_three, down, up, own):
     n1, q1, k1, v1, m1, s1, n2, q2, k2, v2, m2 = saved
     p1, p2 = (p.reshape((-1, 2) + p.shape[2:]) for p in probs)
     rows = probs[0].shape[0]
@@ -1486,7 +1530,7 @@
     copies = 200
     ins_any = (
         p1, p2, q2, k2, v2, m2, gmix2, q1, k1, v1, m1, n1, n2, mem, x, s1, g2, g2_low,
-        *(weights[i] for i in range(7)), g_in, g_out, g_small,
+        *(weights[i] for i in range(7)), n3, gu, g_out, g_small,
     )
     return pl.pallas_call(
         functools.partial(backward_kernel, (rows, length, mem_len, width, units, own_rows)),
@@ -1500,7 +1544,6 @@
         + [square] * 4
         + [square] * 4
         + [
-            pltpu.VMEM(stage("in0"), bf16),
             pltpu.VMEM(stage("out1"), bf16),
             pltpu.VMEM(stage("small"), bf16),
         ]
@@ -1508,13 +1551,15 @@
         + [
             pltpu.VMEM((4, tasks, hidden), f32),
             pltpu.VMEM((6, tasks, hidden), f32),
-            pltpu.VMEM((4,) + gains.shape, f32),
-            pltpu.VMEM((6,) + gains.shape, f32),
+            pltpu.VMEM((4, tasks, width), f32),
+            pltpu.VMEM((6, tasks, width), f32),
+            pltpu.VMEM((4, tasks, 2 * width), f32),
+            pltpu.VMEM((6, tasks, 2 * width), f32),
             pltpu.VMEM(gains.shape, f32),
             pltpu.SemaphoreType.DMA((copies,)),
             pltpu.SemaphoreType.DMA((copies,)),
             pltpu.SemaphoreType.DMA((2,)),
-            pltpu.SemaphoreType.DMA((32,)),
+            pltpu.SemaphoreType.DMA((40,)),
         ],
         compiler_params=pltpu.CompilerParams(
             collective_id=1, has_side_effects=True, vmem_limit_bytes=63 << 20
@@ -1659,7 +1704,7 @@
     )
     up_all = made_up.reshape(task_count * ADA, model_width)
     cot = cotangent.reshape(token_count, model_width)
-    output, g2, g2_low, gmix2, hidden_in_grad, hidden_out_grad, up_grad, down_grad, gain_three = feed_forward(
+    output, g2, g2_low, gmix2, n3, gu, hidden_out_grad, up_grad, down_grad, gain_three = feed_forward(
         saved[5], saved[10], cot, token_task, backbone, gain_table, down_all, up_all
     )
     down_rows = (
@@ -1671,10 +1716,9 @@
     if parts == 32:
         small = jnp.concatenate((down_rows, up_rows), axis=1).astype(bf16)
         small = jnp.pad(small, ((0, 0), (0, 0), (0, model_width - down_own)))
-        in_grad = hidden_in_grad.reshape((LINE, 2, 2, -1, hidden_in.shape[1]))
         out_grad = hidden_out_grad.reshape((LINE, 2, 2, -1, model_width))
         mem_grad, input_grad, *shared, small, gain_sum, state = backward(
-            mem_len, saved, (probs_one, probs_two), x, mem, outs[:7], g2, g2_low, gmix2, in_grad, out_grad,
+            mem_len, saved, (probs_one, probs_two), x, mem, outs[:7], g2, g2_low, gmix2, n3, gu, out_grad,
             small.reshape(LINE, 2, 2, 4 * task_count, model_width), token_task, gain_table, gain_three,
             down_maker, up_maker, weights,
         )
@@ -1690,7 +1734,7 @@
         input_grad, mem_grad, grads, gain_one, gain_two = attention_back(
             x, mem, row_count, token_task, backbone, gain_table, saved, probs_one, probs_two, g2, g2_low, gmix2
         )
-        grads = (*grads, hidden_in_grad, hidden_out_grad)
+        grads = (*grads, *outers((n3,), (gu,), (0,), "hidden_in_grad"), hidden_out_grad)
         packed = jnp.concatenate([g.reshape(parts, -1, model_width) for g in grads], axis=1)
         packed = lax.psum_scatter(packed, "dp", scatter_dimension=0, tiled=False).astype(f32)
         shared, at = [], 0

time: 355 us -> 339 us (0.955)
  Pallas kernels: 333 us -> 319 us
    pallas_call x3 -> x2, Pallas kernels: 69.8 us -> 52.5 us  [call(): pl.pallas_call(kernel, grid=grid, in_specs=[pl.BlockSpec(b, m) for _, b,...]
where the time goes in v7:
time: 339 us; the launch traced here: 334 us
  Pallas kernels  319 us (94%)
  local copies, waits for them, and re-layouts  11.4 us (3%)
    pallas_call x1, Pallas kernels, backward(): pl.pallas_call(functools.partial(backward_kernel, (rows, length, mem_len,...  136 us
    pallas_call x1, Pallas kernels, forward(): pl.pallas_call(forward_kernel, in_specs=[vmem] * 21, out_specs=[any_space...  122 us
    pallas_call x2, Pallas kernels, call(): pl.pallas_call(kernel, grid=grid, in_specs=[pl.BlockSpec(b, m) for _, b,...  52.5 us
    pallas_call x1, Pallas kernels, finish(): pl.pallas_call(functools.partial(finish_kernel, len(shards)), in_specs=[v...  8.56 us

profile of v7, /device:TPU:0, one launch (start us, length us, event | category | flops | bytes accessed | tf_op | source)
XLA Modules:
  0.0 333.5 jit_solution(12989680946579385334)
XLA Ops:
  0.7 122.2 %forward_as_weights_arrive.1 = (bf16[4,2,2,48,768]{4,3,2,1,0:T(8,128)(2,1)}, bf16[4,2,2,48,768]{4,3,2,1,0:T(8,128)(2,1)}, bf16[4,2,2,48,768]{4,3,2,1,0:T(8,128)(...) custom-call(bf16[1024,768]{1,0:T(8,128)(2,1)} %bitcast.34, ...), custom_call_target="tpu_custom_call" | custom-call | tf_op jit(solution)/shard_map/forward_as_weights_arrive/pallas_call | solution.py:965
  122.8 1.1 fusion.3
  124.0 0.1 copy_bitcast_fusion
  124.0 1.2 reshape_reshape.7.up_all
  125.2 1.3 reshape_reshape.6
  126.5 0.6 copy.45
  127.2 0.9 copy.47.down_all
  128.1 43.3 %feed_forward_and_back.1 = (bf16[1024,768]{1,0:T(8,128)(2,1)}, bf16[1024,768]{1,0:T(8,128)(2,1)}, bf16[1024,3072]{1,0:T(8,128)(2,1)}, bf16[1024,3072]{1,0:T(8,12...) custom-call(f32[1024,768]{1,0:T(8,128)} %get-tuple-element.91.s1.ref, ...), custom_call_target="tpu_custom_call" | custom-call | flops 21743271936 | bytes 42373120 | tf_op jit(solution)/shard_map/feed_forward_and_back/pallas_call | solution.py:93
  171.3 0.0 copy-start
  171.3 1.2 convert.12
  172.5 0.5 reshape.117
  173.0 0.1 copy.56
  173.1 0.0 copy-done
  173.2 0.2 copy.48
  173.4 2.5 reshape.115
  175.9 1.9 copy.49
  177.8 1.0 reshape.116
  178.8 1.0 fusion.2
  179.8 9.2 %hidden_out_grad.1 = bf16[3072,768]{1,0:T(8,128)(2,1)} custom-call(bf16[1024,3072]{1,0:T(8,128)(2,1)} %get-tuple-element.123.refs_0_, bf16[1024,768]{1,0:T(8,128)(2,1)} %get-tuple-element.124.refs_1_), custom_call_target="tpu_custom_call" | custom-call | flops 4831838208 | bytes 12582912 | tf_op jit(solution)/shard_map/hidden_out_grad/pallas_call | solution.py:93
  189.0 135.7 %backward_as_gradients_leave.1 = (f32[1024,768]{1,0:T(8,128)}, f32[1024,768]{1,0:T(8,128)}, f32[24,768]{1,0:T(8,128)}, f32[24,768]{1,0:T(8,128)}, f32[24,768]{1,...) custom-call(bf16[12,2,512,512]{3,2,1,0:T(8,128)(2,1)} %bitcast.30, ...), custom_call_target="tpu_custom_call" | custom-call | tf_op jit(solution)/shard_map/backward_as_gradients_leave/pallas_call | solution.py:1535
  324.8 8.6 %finish.1 = (f32[24,768]{1,0:T(8,128)}, f32[24,768]{1,0:T(8,128)}, f32[24,768]{1,0:T(8,128)}, f32[24,768]{1,0:T(8,128)}, f32[24,768]{1,0:T(8,128)}, /*index=5*/f...) custom-call(f32[24,768]{1,0:T(8,128)} %get-tuple-element.128.refs_0_, ...), custom_call_target="tpu_custom_call" | custom-call | tf_op jit(solution)/shard_map/finish/pallas_call | solution.py:1628
  (1 shorter events, 0.0 us)
Async XLA Ops:
  171.3 1.8 copy-start

commit v8 on v7

--- a/solution.py
+++ b/solution.py
@@ -272,7 +272,7 @@
 def feed_kernel(
     s1, mixed, wo, task, gain, w_in, w_out, down_all, up_all, cot,
     output, n3, act, gu, gfeed, g2, g2_low, gmix, up_grad, down_grad, gain_grad,
-    slope, total,
+    slope,
 ):
     first = pl.program_id(0) == 0
     units = w_in.shape[1]
@@ -306,17 +306,18 @@
     gfeed[...] = grad_feed
     up_now = inner_cols(narrow, cotan)
     down_now = inner_cols(feed_low, gb)
-    total[...] = jnp.zeros_like(total)
-
-    @pl.loop(0, units // CHUNK)
-    def _(j):
-        cols = pl.ds(pl.multiple_of(j * CHUNK, CHUNK), CHUNK)
-        grad = slope[:, cols].astype(f32) * inner_rows(gfeed[...], w_out[cols, :])
-        grad = grad.astype(bf16)
+    grad_hidden = inner_rows(grad_feed, w_out[parts[0], :])
+    total = None
+    for k, cols in enumerate(parts):
+        now = grad_hidden
+        if k + 1 < len(parts):
+            grad_hidden = inner_rows(grad_feed, w_out[parts[k + 1], :])
+        grad = (slope[:, cols].astype(f32) * now).astype(bf16)
         gu[:, cols] = grad
-        total[...] += inner_rows(grad, w_in[:, cols])
-
-    stream_grad, gain_tokens = norm_back(stream, picked, total[...])
+        term = inner_rows(grad, w_in[:, cols])
+        total = term if total is None else total + term
+
+    stream_grad, gain_tokens = norm_back(stream, picked, total)
     grad_two = cotan.astype(f32) + stream_grad
     g2[...] = grad_two
     low = grad_two.astype(bf16)
@@ -467,7 +468,7 @@
             low_out(act_shape), full_out(act_shape), low_out(act_shape), low_out(act_shape),
             out_whole((wide, width), f32), out_whole((width, wide), f32), out_whole((tasks, width), f32),
         ],
-        scratch=[pltpu.VMEM((block, units), bf16), pltpu.VMEM((block, width), f32)],
+        scratch=[pltpu.VMEM((block, units), bf16)],
         flops=2 * square + 8 * tokens * width * units,
         name="feed_forward_and_back",
     )

time: 339 us -> 338 us (level)
  no operation moved by 1% of the time
where the time goes in v8:
time: 338 us; the launch traced here: 332 us
  Pallas kernels  318 us (94%)
  local copies, waits for them, and re-layouts  11.4 us (3%)
    pallas_call x1, Pallas kernels, backward(): pl.pallas_call(functools.partial(backward_kernel, (rows, length, mem_len,...  136 us
    pallas_call x1, Pallas kernels, forward(): pl.pallas_call(forward_kernel, in_specs=[vmem] * 21, out_specs=[any_space...  122 us
    pallas_call x2, Pallas kernels, call(): pl.pallas_call(kernel, grid=grid, in_specs=[pl.BlockSpec(b, m) for _, b,...  51.2 us
    pallas_call x1, Pallas kernels, finish(): pl.pallas_call(functools.partial(finish_kernel, len(shards)), in_specs=[v...  8.56 us

profile of v8, /device:TPU:0, one launch (start us, length us, event | category | flops | bytes accessed | tf_op | source)
XLA Modules:
  0.0 332.4 jit_solution(15558118961808702470)
XLA Ops:
  0.7 122.2 %forward_as_weights_arrive.1 = (bf16[4,2,2,48,768]{4,3,2,1,0:T(8,128)(2,1)}, bf16[4,2,2,48,768]{4,3,2,1,0:T(8,128)(2,1)}, bf16[4,2,2,48,768]{4,3,2,1,0:T(8,128)(...) custom-call(bf16[1024,768]{1,0:T(8,128)(2,1)} %bitcast.34, ...), custom_call_target="tpu_custom_call" | custom-call | tf_op jit(solution)/shard_map/forward_as_weights_arrive/pallas_call | solution.py:966
  122.8 1.1 fusion.3
  124.0 0.1 copy_bitcast_fusion
  124.0 1.2 reshape_reshape.7.up_all
  125.2 1.3 reshape_reshape.6
  126.5 0.6 copy.45
  127.2 0.9 copy.47.down_all
  128.1 42.0 %feed_forward_and_back.1 = (bf16[1024,768]{1,0:T(8,128)(2,1)}, bf16[1024,768]{1,0:T(8,128)(2,1)}, bf16[1024,3072]{1,0:T(8,128)(2,1)}, bf16[1024,3072]{1,0:T(8,12...) custom-call(f32[1024,768]{1,0:T(8,128)} %get-tuple-element.91.s1.ref, ...), custom_call_target="tpu_custom_call" | custom-call | flops 21743271936 | bytes 42373120 | tf_op jit(solution)/shard_map/feed_forward_and_back/pallas_call | solution.py:93
  170.1 0.0 copy-start
  170.1 1.2 convert.12
  171.2 0.5 reshape.117
  171.8 0.1 copy.56
  171.9 0.0 copy-done
  171.9 0.2 copy.48
  172.1 2.5 reshape.115
  174.6 1.9 copy.49
  176.5 1.0 reshape.116
  177.5 1.0 fusion.2
  178.5 9.2 %hidden_out_grad.1 = bf16[3072,768]{1,0:T(8,128)(2,1)} custom-call(bf16[1024,3072]{1,0:T(8,128)(2,1)} %get-tuple-element.123.refs_0_, bf16[1024,768]{1,0:T(8,128)(2,1)} %get-tuple-element.124.refs_1_), custom_call_target="tpu_custom_call" | custom-call | flops 4831838208 | bytes 12582912 | tf_op jit(solution)/shard_map/hidden_out_grad/pallas_call | solution.py:93
  187.8 135.8 %backward_as_gradients_leave.1 = (f32[1024,768]{1,0:T(8,128)}, f32[1024,768]{1,0:T(8,128)}, f32[24,768]{1,0:T(8,128)}, f32[24,768]{1,0:T(8,128)}, f32[24,768]{1,...) custom-call(bf16[12,2,512,512]{3,2,1,0:T(8,128)(2,1)} %bitcast.30, ...), custom_call_target="tpu_custom_call" | custom-call | tf_op jit(solution)/shard_map/backward_as_gradients_leave/pallas_call | solution.py:1536
  323.6 8.6 %finish.1 = (f32[24,768]{1,0:T(8,128)}, f32[24,768]{1,0:T(8,128)}, f32[24,768]{1,0:T(8,128)}, f32[24,768]{1,0:T(8,128)}, f32[24,768]{1,0:T(8,128)}, /*index=5*/f...) custom-call(f32[24,768]{1,0:T(8,128)} %get-tuple-element.128.refs_0_, ...), custom_call_target="tpu_custom_call" | custom-call | tf_op jit(solution)/shard_map/finish/pallas_call | solution.py:1629
  (1 shorter events, 0.0 us)
Async XLA Ops:
  170.1 1.8 copy-start
